TPU v7x, 32 devices: a whole 2x2x4 slice. The times are simulated.
32 devices in a mesh: sent: 32 (over z, y, x, core).
Axes of the slice: x: 2, y: 2, z: 4, core: 2. Of those that a mesh axis runs over, the one named last changes fastest.
Arguments:
- embeddings: bfloat16 [8192, 768], P('sent'), may hold values from -6 to 6
- cotangent: bfloat16 [2, 8192, 768], P(None, 'sent'), may hold values from -0.011962891 to 0.011962891
- drop_masks: int32 [2, 3, 8192, 768], P(None, None, 'sent'), may hold values 0 or 1
- lengths: int32 [256], P('sent'), may hold values from 0 to 128, as said below
- buckets: int32 [32], replicated, may hold values from 0 to 2, as said below
- attn_params: float32 [2463744], P('sent'), may hold values from -3 to 3
- attn_moment: float32 [2463744], P('sent'), may hold values from -1 to 1
- attn_second: float32 [2463744], P('sent'), may hold values from 0 to 1, as said below
- attn_ema: float32 [2463744], P('sent'), may hold values from -3 to 3
- head_params: float32 [5314560], P('sent'), may hold values from -3 to 3
- head_moment: float32 [5314560], P('sent'), may hold values from -1 to 1
- head_second: float32 [5314560], P('sent'), may hold values from 0 to 1, as said below
- head_ema: float32 [5314560], P('sent'), may hold values from -3 to 3
Outputs:
- hidden: bfloat16 [2, 8192, 768], P(None, 'sent')
- input_grad: float32 [8192, 768], P('sent')
- loss: float32 [], replicated
- grad_norm: float32 [], replicated
- attn_first: float32 [2463744], P('sent')
- attn_second_new: float32 [2463744], P('sent')
- attn_updated: float32 [2463744], P('sent')
- attn_average: float32 [2463744], P('sent')
- head_first: float32 [5314560], P('sent')
- head_second_new: float32 [5314560], P('sent')
- head_updated: float32 [5314560], P('sent')
- head_average: float32 [5314560], P('sent')
Inputs may be any that keep to these rules, and one draw needn't show every extreme that they name: `buckets`: sentences of device b have 32 * 2^code rows; some device has code 2. `lengths`: slot s of a device holds a sentence of 1 to its bucket length rows when s < 256 // (bucket length), else 0; the first slot of every device is full. `attn_second`: positive. `head_second`: positive.
All inputs are finite; a program needn't handle non-finite values. No bound on the sum of `drop_masks` on one device may be relied on, other than what follows from the above.
Results may differ from a plain program's by a relative error of at most 0.017.
The roundings to bfloat16 on the way count: a program that leaves them out, or rounds other values in their place, can miss the bound.
Values may be sent and summed in bfloat16 or wider, within the bound.
No kernel may reach another device: no remote copies, remote signals or barrier semaphores. Data moves between devices by JAX's collectives and lax.ppermute only.
A program may use at most 192 MiB of HBM per device.

v0:
```python
import functools

import jax
import jax.numpy as jnp
from jax import lax
from jax.experimental import pallas as pl
from jax.experimental.pallas import tpu as pltpu
from jax.sharding import PartitionSpec as P

D = 768
H = 12
HD = 64
LMIN = 32
POS = 128
STEP = 5


logit_divisor = 0.05
keep_prob = 0.9
norm_eps = 1e-06
clip_bound = 0.001
beta_first = 0.5
beta_second = 0.5
learn_rate = 0.05
decay_rate = 0.01
adam_eps = 1e-08
ema_rate = 0.8
masked_scores = -1e30
highest = lax.Precision.HIGHEST


def layer_norm(tensor, gain_vec, shift_vec):
    center = tensor - jnp.mean(tensor, axis=-1, keepdims=True)
    spread = jnp.mean(center * center, axis=-1, keepdims=True)
    return center * lax.rsqrt(spread + norm_eps) * gain_vec + shift_vec


def gelu_exact(tensor):
    return 0.5 * tensor * (1.0 + jax.scipy.special.erf(tensor * 0.7071067811865476))


def unit_scale(tensor):
    return tensor * lax.rsqrt(jnp.sum(tensor * tensor, axis=-1, keepdims=True) + norm_eps)


def bucket_length(bucket_code):
    return (LMIN * jnp.where(bucket_code == 0, 1, jnp.where(bucket_code == 1, 2, 4))).astype(
        jnp.int32
    )


def plain_dot(left_op, right_op):
    return jnp.dot(left_op, right_op, preferred_element_type=jnp.float32)


def rows_dot(left_op, right_op):
    return lax.dot_general(
        left_op, right_op, (((0,), (0,)), ((), ())), preferred_element_type=jnp.float32
    )


def target_dot_terms(left_op, right_op):
    return lax.dot_general(
        left_op, right_op, (((1,), (1,)), ((), ())), preferred_element_type=jnp.float32
    )


def adam_step(grad_flat, params, moment, second, average):
    first_new = beta_first * moment + (1.0 - beta_first) * grad_flat
    second_new = beta_second * second + (1.0 - beta_second) * grad_flat * grad_flat
    fix_first = 1.0 - beta_first**STEP
    fix_second = 1.0 - beta_second**STEP
    adam_dir = first_new / fix_first / (jnp.sqrt(second_new / fix_second) + adam_eps)
    updated = params - learn_rate * (adam_dir + decay_rate * params)
    average_new = ema_rate * average + (1.0 - ema_rate) * updated
    return (first_new, second_new, updated, average_new)


LANES = 128
VMEM_CAP = 60 * 2**20


def room(mib):
    return pltpu.CompilerParams(vmem_limit_bytes=mib * 2**20)


def far(*arrays):
    return [pltpu.with_memory_space_constraint(array, pltpu.HBM) for array in arrays]


def bring(pairs, sems, first=0):
    copies = []
    for source, target in pairs:
        copies.append(pltpu.make_async_copy(source, target, sems.at[first + len(copies)]))
        copies[-1].start()
    return copies


def await_all(copies):
    for copy in copies:
        copy.wait()


def result(shape, dtype, stays=False):
    return pltpu.VMEM(shape, dtype) if stays else jax.ShapeDtypeStruct(shape, dtype)
CORE, XBIT, YBIT, ZBITS = 1, 2, 4, (8, 16, 24)


def swap(value, bit):
    count = lax.axis_size("sent")
    return lax.ppermute(value, "sent", [(i, i ^ bit) for i in range(count)])


def is_grid(count, *shards):
    return count == 32 and all(2 * shard % LANES == 0 for shard in shards)


def block_rows(shard):
    return -(-(-(-shard // LANES) + 8) // 16) * 16


def first_row(device, shard):
    return (device * shard) // LANES


def pack_shard(values, device):
    shard = values.shape[0]
    rows = block_rows(shard)
    size = rows * LANES
    odd = (device * shard) % LANES != 0
    lead = jnp.where(
        odd,
        jnp.pad(values, (LANES // 2, size - shard - LANES // 2)),
        jnp.pad(values, (0, size - shard)),
    ).reshape(rows, LANES)
    offset = first_row(device, shard) % 8
    padded = jnp.pad(lead, ((8, 0), (0, 0)))
    return lax.dynamic_slice(padded, (8 - offset, 0), (rows, LANES)).astype(jnp.bfloat16)


def unpack_shard(block, device, shard):
    rows = -(-shard // LANES)
    offset = first_row(device, shard) % 8
    odd = (device * shard) % LANES != 0
    flat = lax.dynamic_slice(block, (offset, 0), (rows, LANES)).reshape(-1)
    longer = jnp.pad(flat, (0, LANES))
    return jnp.where(odd, longer[LANES // 2 : LANES // 2 + shard], flat[:shard])


WHOLE = ((0, 0, 4), (1, 0, 4), (2, 0, 4), (3, 0, 2), (3, 2, 2))
HALVES = tuple((across, first, 2) for across in range(4) for first in (0, 2))


def piece_slots(me, layout):
    slots = []
    for core in (0, 1):
        for across, first, n in layout:
            slots.append([me ^ (core + 2 * across + 8 * (first + k)) for k in range(n)])
    return slots


def after(value, *others):
    return lax.optimization_barrier((value, others))[0]


def with_sibling(own):
    return tuple(own) + tuple(swap(piece, CORE) for piece in own)


def gather_attn(values, device):
    block = pack_shard(values, device)
    zs = [swap(block, bit) for bit in ZBITS]
    line = jnp.stack([block] + zs)
    x, y = swap(line, XBIT), swap(line, YBIT)
    diagonal = (swap(y[:2], XBIT), swap(x[2:], YBIT))
    return with_sibling((line, x, y) + diagonal), zs[0], diagonal


def gather_head_line(values, device, first):
    block = after(pack_shard(values, device), first)
    return [block] + [swap(block, bit) for bit in ZBITS]


def gather_head(line, x, y):
    return with_sibling((line, x, y, swap(y[:2], XBIT), swap(x[2:], YBIT)))


def low_sum(*terms):
    total = terms[0].astype(jnp.float32)
    for term in terms[1:]:
        total = total + term.astype(jnp.float32)
    return total.astype(jnp.bfloat16)


def scatter_core(pieces):
    half = len(pieces) // 2
    got = [swap(piece, CORE) for piece in reversed(pieces[half:])][::-1]
    return [low_sum(piece, other) for piece, other in zip(pieces[:half], got)]


def scatter_attn(sums):
    line, x, y, d_low, d_high = sums
    d_low, d_high = swap(d_low, XBIT), swap(d_high, YBIT)
    x = swap(jnp.concatenate([x[:2], low_sum(x[2:], d_high)]), XBIT)
    y = swap(jnp.concatenate([low_sum(y[:2], d_low), y[2:]]), YBIT)
    line = low_sum(line, x, y)
    return scatter_along(line[0], [line[k] for k in (1, 2, 3)])


def scatter_along(own, others):
    total = own.astype(jnp.float32)
    for value, bit in zip(others, ZBITS):
        total = total + swap(value, bit).astype(jnp.float32)
    return total


def plain_rows(left, right, dims):
    return lax.dot_general(left, right, (dims, ((), ())), preferred_element_type=jnp.float32)


NN, NT, TN = ((1,), (0,)), ((1,), (1,)), ((0,), (0,))


def one_hot(shape, left, right):
    rows = lax.broadcasted_iota(jnp.int32, shape, 0)
    cols = lax.broadcasted_iota(jnp.int32, shape, 1)
    return jnp.where(left(rows, cols) == right(rows, cols), 1.0, 0.0)


def vectors_of(flat_rows):
    spread = one_hot((D, 48), lambda r, c: r >> 4, lambda r, c: c).astype(jnp.bfloat16)
    rows = plain_rows(spread, flat_rows.astype(jnp.bfloat16), NN)
    rows = rows * one_hot((D, LANES), lambda r, c: r & 15, lambda r, c: c >> 3)
    fold = one_hot((8, LANES), lambda r, c: r, lambda r, c: c & 7).astype(jnp.bfloat16)
    return plain_rows(fold, rows.astype(jnp.bfloat16), NT)


def flat_of(vectors):
    fold = one_hot((8, LANES), lambda r, c: r, lambda r, c: c & 7).astype(jnp.bfloat16)
    rows = plain_rows(vectors.astype(jnp.bfloat16), fold, TN)
    rows = rows * one_hot((D, LANES), lambda r, c: r & 15, lambda r, c: c >> 3)
    spread = one_hot((D, 48), lambda r, c: r >> 4, lambda r, c: c).astype(jnp.bfloat16)
    return plain_rows(spread, rows.astype(jnp.bfloat16), TN)


def keep_of(mask):
    return mask.astype(jnp.float32) * (1.0 / keep_prob)


def place_blocks(shard, layout, pieces, me, stage, flat, sems):
    count, rows = stage.shape[0], stage.shape[1]
    for piece, slots in zip(pieces, piece_slots(me, layout)):
        for k, slot in enumerate(slots):
            pltpu.make_async_copy(piece.at[k], stage.at[slot], sems.at[slot]).start()
    flat[pl.ds(0, 8), :] = jnp.zeros((8, LANES), jnp.float32)

    def place(device, carry):
        pltpu.make_async_copy(pieces[0].at[0], stage.at[device], sems.at[device]).wait()
        at = pl.multiple_of(device * shard // LANES // 8 * 8, 8)
        before = flat[pl.ds(at, 8), :]
        flat[pl.ds(at, rows), :] = stage[device].astype(jnp.float32)
        flat[pl.ds(at, 8), :] += before
        return carry

    lax.fori_loop(0, count, place, 0)


def gather_matrix(flat, w_ref, w_out=None, out_sems=None):
    cols = w_ref.shape[1] // LANES

    def gather_rows(group, carry):
        at = pl.multiple_of(group * 16, 16)
        for col in range(cols):
            rows16 = flat[pl.ds(group * 16 * cols + col, 16, stride=cols), :]
            w_ref[pl.ds(at, 16), pl.ds(col * LANES, LANES)] = rows16.astype(jnp.bfloat16)
        return carry

    parts = 4
    span = D // parts
    copies = []
    for part in range(parts):
        lax.fori_loop(part * span // 16, (part + 1) * span // 16, gather_rows, 0)
        here = pl.ds(part * span, span)
        if w_out is not None:
            copies.append(pltpu.make_async_copy(w_ref.at[here], w_out.at[here], out_sems.at[part]))
            copies[-1].start()
    return copies


VEC = 8 + POS


def table_of(flat, base, body, tail):
    lane = lax.broadcasted_iota(jnp.int32, (D // 16, LANES), 1)
    for q in range(16):
        here = flat[pl.ds(base + q, D // 16, stride=17), :]
        later = flat[pl.ds(base + q + 1, D // 16, stride=17), :]
        both = jnp.where(lane >= 8 * q, here, later)
        shift = (LANES - 8 * q) % LANES
        body[pl.ds(q, D // 16, stride=16), :] = pltpu.roll(both, shift, 1) if shift else both
        tail[pl.ds(q, D // 16, stride=16), :] = pltpu.roll(later, shift, 1) if shift else later
    return body[...].T, tail[...].T[:8]


def flat_table(flat, base, first, last, body, tail):
    body[...] = first.T
    tail[...] = jnp.concatenate([last, jnp.zeros((LANES - 8, D), jnp.float32)]).T
    lane = lax.broadcasted_iota(jnp.int32, (D // 16, LANES), 1)
    carried = None
    for q in range(17):
        row = carried
        if q < 16:
            main = body[pl.ds(q, D // 16, stride=16), :]
            end = tail[pl.ds(q, D // 16, stride=16), :]
            if q:
                main, end = pltpu.roll(main, 8 * q, 1), pltpu.roll(end, 8 * q, 1)
            row = main if carried is None else jnp.where(lane >= 8 * q, main, carried)
            carried = jnp.where(lane < 8 * q, main, end)
        flat[pl.ds(base + q, D // 16, stride=17), :] = row


def repeat_places(table, length):
    twice = jnp.concatenate([table[:64]] * 2)
    four = jnp.concatenate([table[:32]] * 4)
    return jnp.where(length == 128, table, jnp.where(length == 64, twice, four))


def fold_places(rows, length):
    half = rows[:64] + rows[64:]
    quarter = half[:32] + half[32:]
    none = jnp.zeros_like(rows)
    twice = jnp.concatenate([half, none[:64]])
    four = jnp.concatenate([quarter, none[:96]])
    return jnp.where(length == 128, rows, jnp.where(length == 64, twice, four))


def stack_heads(pair):
    lane = lax.broadcasted_iota(jnp.int32, pair.shape, 1)
    none = jnp.zeros_like(pair)
    return jnp.concatenate([jnp.where(lane < HD, pair, none), jnp.where(lane < HD, none, pair)])


def unstack_heads(rows):
    half = rows.shape[0] // 2
    lane = lax.broadcasted_iota(jnp.int32, (half, rows.shape[1]), 1)
    return jnp.where(lane < HD, rows[:half], rows[half:])


ROWS = 64


def attn_kernel(shard, me_ref, length_ref, lens_ref, *refs):
    pieces, (emb_ref, mask_hbm) = refs[:10], refs[10:12]
    (w_out, vec_ref, rows_ref, in_low_ref, qkv_ref, prob_ref, mixed_ref, res_ref, norm_ref, low_ref) = refs[12:22]
    (stage, flat, w_ref, body, tail, mask, attn_in, bias_ref, sems, out_sems, mask_sems) = refs[22:]
    me = me_ref[0]
    tokens = emb_ref.shape[0]
    masks = []
    for view in range(2):
        for which in range(2):
            at = 2 * view + which
            masks.append(pltpu.make_async_copy(mask_hbm.at[view, which], mask.at[at], mask_sems.at[at]))
            masks[-1].start()
    place_blocks(shard, WHOLE, pieces, me, stage, flat, sems)
    copies = gather_matrix(flat, w_ref, w_out, out_sems)
    first, last = table_of(flat, D * w_ref.shape[1] // LANES, body, tail)
    vecs = first[:8]
    vec_ref[...] = vecs
    length = length_ref[0]
    places = repeat_places(jnp.concatenate([first[8:], last]), length)
    for copy in masks:
        copy.wait()
    for block in range(tokens // LANES):
        key = lax.broadcasted_iota(jnp.int32, (LANES, LANES), 1) + block * LANES
        query = lax.broadcasted_iota(jnp.int32, (LANES, LANES), 0) + block * LANES
        shift = jnp.where(length == 128, 7, jnp.where(length == 64, 6, 5))
        sent = lax.shift_right_logical(key, jnp.full_like(key, 1) * shift)
        sent_q = lax.shift_right_logical(query, jnp.full_like(key, 1) * shift)
        real = jnp.zeros_like(key)
        for slot in range(lens_ref.shape[0]):
            real = jnp.where(sent == slot, lens_ref[slot], real)
        ok = (sent == sent_q) & ((key & (length - 1)) < real)
        bias_ref[block] = jnp.where(ok, 0.0, masked_scores)
        here = pl.ds(block * LANES, LANES)
        emb = emb_ref[here, :].astype(jnp.float32) + places + vecs[7:8]
        rows_ref[here, :] = emb
        normed = layer_norm(emb, vecs[5:6], vecs[6:7])
        for view in range(2):
            at = pl.ds(view * tokens + block * LANES, LANES)
            given = normed * keep_of(mask[2 * view, here, :])
            attn_in[at, :] = given
            in_low_ref[at, :] = given.astype(jnp.bfloat16)
    for part in range(3):
        cols = pl.ds(part * D, D)
        made = plain_rows(in_low_ref[...], w_ref[:, cols], NN)
        if part != 1:
            made = made + vecs[part // 2 : part // 2 + 1]
        qkv_ref[:, cols] = made.astype(jnp.bfloat16)

    def attend(block, carry):
        here = pl.ds(pl.multiple_of(block * LANES, LANES), LANES)
        bias = bias_ref[block & 1]
        bias = jnp.concatenate([bias, bias])
        for pair in range(H // 2):
            q = stack_heads(qkv_ref[here, pl.ds(pair * LANES, LANES)])
            k = qkv_ref[here, pl.ds(D + pair * LANES, LANES)]
            v = qkv_ref[here, pl.ds(2 * D + pair * LANES, LANES)]
            scores = plain_rows(q, k, NT) * HD ** (-0.5) + bias
            expo = jnp.exp(scores - jnp.max(scores, axis=-1, keepdims=True))
            probs = expo / jnp.sum(expo, axis=-1, keepdims=True)
            prob_ref[block, pair] = probs
            mixed = unstack_heads(plain_rows(probs.astype(jnp.bfloat16), v, NN))
            mixed_ref[here, pl.ds(pair * LANES, LANES)] = mixed.astype(jnp.bfloat16)
        return carry

    lax.fori_loop(0, 2 * tokens // LANES, attend, 0)
    res_ref[...] = plain_rows(mixed_ref[...], w_ref[:, 3 * D :], NN)
    for view in range(2):
        def finish(chunk, carry, view=view):
            own = pl.ds(pl.multiple_of(chunk * ROWS, ROWS), ROWS)
            at = pl.ds(pl.multiple_of(view * tokens + chunk * ROWS, ROWS), ROWS)
            res = attn_in[at, :] + keep_of(mask[2 * view + 1, own, :]) * (res_ref[at, :] + vecs[2:3])
            res_ref[at, :] = res
            norm = layer_norm(res, vecs[3:4], vecs[4:5])
            norm_ref[at, :] = norm
            low_ref[at, :] = norm.astype(jnp.bfloat16)
            return carry

        lax.fori_loop(0, tokens // ROWS, finish, 0, unroll=True)
    for copy in copies:
        copy.wait()


def attn_forward(pieces, me, shard, length, lengths, embeddings, masks):
    rows = pieces[0].shape[1]
    whole = shard * 32 // LANES
    tokens = embeddings.shape[0]
    both = 2 * tokens
    any_space, vmem = pl.BlockSpec(memory_space=pltpu.HBM), pl.BlockSpec(memory_space=pltpu.VMEM)
    smem = pl.BlockSpec(memory_space=pltpu.SMEM)
    f32, low = jnp.float32, jnp.bfloat16
    shapes = [
        ((D, 4 * D), low),
        ((8, D), f32),
        ((tokens, D), f32),
        ((both, D), low),
        ((both, 3 * D), low),
        ((both // LANES, H // 2, 2 * LANES, LANES), f32),
        ((both, D), low),
        ((both, D), f32),
        ((both, D), f32),
        ((both, D), low),
    ]
    return pl.pallas_call(
        functools.partial(attn_kernel, shard),
        out_shape=tuple(jax.ShapeDtypeStruct(*s) for s in shapes),
        in_specs=[smem] * 3 + [any_space] * len(pieces) + [vmem, any_space],
        out_specs=(any_space,) + (vmem,) * 9,
        scratch_shapes=[
            pltpu.VMEM((32, rows, LANES), low),
            pltpu.VMEM((whole + rows, LANES), f32),
            pltpu.VMEM((D, 4 * D), low),
            pltpu.VMEM((D, LANES), f32),
            pltpu.VMEM((D, LANES), f32),
            pltpu.VMEM((4, tokens, D), jnp.int32),
            pltpu.VMEM((both, D), f32),
            pltpu.VMEM((tokens // LANES, LANES, LANES), f32),
            pltpu.SemaphoreType.DMA((32,)),
            pltpu.SemaphoreType.DMA((4,)),
            pltpu.SemaphoreType.DMA((4,)),
        ],
        compiler_params=pltpu.CompilerParams(vmem_limit_bytes=VMEM_CAP),
    )(jnp.reshape(me, (1,)), jnp.reshape(length, (1,)), lengths, *far(*pieces), embeddings, *far(masks))


def sum_rows(rows):
    return jnp.sum(rows, axis=0, keepdims=True)


def norm_back_kernel(pick_ref, d_first, d_cls_in, res_in, vec_in, mask_hbm, mixed_in, w_in,
                     d_res_ref, g_out_ref, d_mixed, part_ref,
                     mask, given, branch, d_cls, res_ref, vec_ref, mixed_ref, w_ref, sems):
    tokens = mask.shape[1]
    both = 2 * tokens
    copies = bring(
        [(d_first, given), (d_cls_in, d_cls), (res_in, res_ref), (vec_in, vec_ref)]
        + [(mask_hbm.at[view, 1], mask.at[view]) for view in range(2)]
        + [(w_in.at[:, pl.ds(3 * D, D)], w_ref), (mixed_in, mixed_ref)],
        sems,
    )
    await_all(copies[:6])
    n = d_cls.shape[0] // 2
    for slot in range(n):
        real = jnp.where(slot < pick_ref[n], 1.0, 0.0)
        for view in range(2):
            at = pl.ds(view * tokens + pick_ref[slot], 1)
            given[at, :] += real * d_cls[view * n + slot : view * n + slot + 1, :]
    gain = vec_ref[3:4, :]
    sums = tuple(jnp.zeros((1, D), jnp.float32) for _ in range(3))
    for view in range(2):
        def one_chunk(chunk, sums, view=view):
            own = pl.ds(pl.multiple_of(chunk * ROWS, ROWS), ROWS)
            at = pl.ds(pl.multiple_of(view * tokens + chunk * ROWS, ROWS), ROWS)
            grad = given[at, :]
            center, inv = norm_parts(res_ref[at, :])
            d_res, unit = norm_back(grad, center, inv, gain)
            d_branch = d_res * keep_of(mask[view, own, :])
            d_res_ref[at, :] = d_res
            branch[at, :] = d_branch.astype(jnp.bfloat16)
            return (
                sums[0] + sum_rows(d_branch),
                sums[1] + sum_rows(grad * unit),
                sums[2] + sum_rows(grad),
            )

        sums = lax.fori_loop(0, tokens // ROWS, one_chunk, sums, unroll=True)
    await_all(copies[6:])
    d_mixed[...] = plain_rows(branch[...], w_ref[...], NT).astype(jnp.bfloat16)
    g_out_ref[...] = plain_rows(mixed_ref[...], branch[...], TN).astype(jnp.bfloat16)
    for k in range(3):
        part_ref[k : k + 1, :] = sums[k]
    part_ref[3:8, :] = jnp.zeros((5, D), jnp.float32)


def norm_backward(picks, d_first, d_cls, res, vecs, masks, mixed, w_attn):
    both = res.shape[0]
    any_space, vmem = pl.BlockSpec(memory_space=pltpu.HBM), pl.BlockSpec(memory_space=pltpu.VMEM)
    f32, low = jnp.float32, jnp.bfloat16
    return pl.pallas_call(
        norm_back_kernel,
        out_shape=(
            result((both, D), f32),
            result((D, D), low),
            result((both, D), low, True),
            result((8, D), f32),
        ),
        in_specs=[pl.BlockSpec(memory_space=pltpu.SMEM)] + [any_space] * 7,
        out_specs=(vmem,) * 4,
        scratch_shapes=[
            pltpu.VMEM((2, both // 2, D), jnp.int32),
            pltpu.VMEM((both, D), f32),
            pltpu.VMEM((both, D), low),
            pltpu.VMEM(d_cls.shape, f32),
            pltpu.VMEM((both, D), f32),
            pltpu.VMEM((8, D), f32),
            pltpu.VMEM((both, D), low),
            pltpu.VMEM((D, D), low),
            pltpu.SemaphoreType.DMA((8,)),
        ],
        compiler_params=room(16),
    )(picks, *far(d_first, d_cls, res, vecs, masks, mixed, w_attn))


def attn_back_kernel(d_mixed, qkv_ref, prob_ref, d_qkv_ref, part_ref):
    part_ref[...] = jnp.zeros_like(part_ref)

    def one_block(block, carry):
        here = pl.ds(pl.multiple_of(block * LANES, LANES), LANES)
        for pair in range(H // 2):
            cols = pl.ds(pair * LANES, LANES)
            q = stack_heads(qkv_ref[here, cols])
            k = qkv_ref[here, pl.ds(D + pair * LANES, LANES)]
            v = qkv_ref[here, pl.ds(2 * D + pair * LANES, LANES)]
            d_out = stack_heads(d_mixed[here, cols])
            probs = prob_ref[block, pair]
            d_v = plain_rows(probs.astype(jnp.bfloat16), d_out, TN)
            d_probs = plain_rows(d_out, v, NT)
            delta = jnp.sum(probs * d_probs, axis=-1, keepdims=True)
            score = (probs * (d_probs - delta) * HD ** (-0.5)).astype(jnp.bfloat16)
            d_q = unstack_heads(plain_rows(score, k, NN))
            d_k = plain_rows(score, q, TN)
            d_qkv_ref[here, cols] = d_q.astype(jnp.bfloat16)
            d_qkv_ref[here, pl.ds(D + pair * LANES, LANES)] = d_k.astype(jnp.bfloat16)
            d_qkv_ref[here, pl.ds(2 * D + pair * LANES, LANES)] = d_v.astype(jnp.bfloat16)
            part_ref[0:1, cols] += sum_rows(d_q)
            part_ref[1:2, cols] += sum_rows(d_v)
        return carry

    lax.fori_loop(0, qkv_ref.shape[0] // LANES, one_block, 0)


def attn_backward(d_mixed, qkv, probs):
    vmem = pl.BlockSpec(memory_space=pltpu.VMEM)
    return pl.pallas_call(
        attn_back_kernel,
        out_shape=(result(qkv.shape, jnp.bfloat16, True), result((8, D), jnp.float32)),
        in_specs=[vmem] * 3,
        out_specs=(vmem,) * 2,
        compiler_params=room(16),
    )(d_mixed, qkv, probs)


def attn_grad_kernel(shard, me_ref, length_ref, d_qkv, *refs):
    sources, input_ref, pieces, scratch = refs[:9], refs[9], refs[10:20], refs[20:]
    stage, flat, body, tail, d_in, sems, in_sems, mask = scratch[:8]
    in_low, w_ref, d_res, rows_ref, vec_ref, g_out, part_ref, norm_part_ref = scratch[8:]
    in_hbm, w_hbm, d_res_hbm, rows_hbm, vec_hbm, mask_hbm, g_hbm, part_hbm, norm_part_hbm = sources
    cols = 4 * D // LANES
    tokens = rows_ref.shape[0]
    copies = bring(
        [(in_hbm, in_low), (g_hbm, g_out), (w_hbm.at[:, pl.ds(0, 3 * D)], w_ref), (d_res_hbm, d_res)]
        + [(mask_hbm.at[view, 0], mask.at[view]) for view in range(2)]
        + [(rows_hbm, rows_ref), (vec_hbm, vec_ref), (part_hbm, part_ref), (norm_part_hbm, norm_part_ref)],
        in_sems,
    )
    await_all(copies[:2])
    span, width = 256, 3 * LANES

    def one_block(block, carry):
        left = in_low[:, pl.ds(pl.multiple_of(block * span, span), span)]
        for k in range(3 * D // width):
            grads = plain_rows(left, d_qkv[:, pl.ds(k * width, width)], TN)
            for col in range(width // LANES):
                for group in range(span // 16):
                    at = (block * span + group * 16) * cols + k * width // LANES + col
                    tile = grads[group * 16 : (group + 1) * 16, col * LANES : (col + 1) * LANES]
                    flat[pl.ds(at, 16, stride=cols), :] = tile
        return carry

    lax.fori_loop(0, D // span, one_block, 0)

    def one_group(group, carry):
        at = pl.multiple_of(group * 16, 16)
        for col in range(D // LANES):
            tile = g_out[pl.ds(at, 16), pl.ds(col * LANES, LANES)].astype(jnp.float32)
            flat[pl.ds(group * 16 * cols + 3 * D // LANES + col, 16, stride=cols), :] = tile
        return carry

    lax.fori_loop(0, D // 16, one_group, 0)
    copies[2].wait()
    d_in[...] = plain_rows(d_qkv[...], w_ref[...], NT)
    await_all(copies[3:])
    gain = vec_ref[5:6, :]

    def one_chunk(chunk, sums):
        own = pl.ds(pl.multiple_of(chunk * ROWS, ROWS), ROWS)
        other = pl.ds(pl.multiple_of(tokens + chunk * ROWS, ROWS), ROWS)
        grad = (d_in[own, :] + d_res[own, :]) * keep_of(mask[0, own, :])
        grad = grad + (d_in[other, :] + d_res[other, :]) * keep_of(mask[1, own, :])
        center, inv = norm_parts(rows_ref[own, :])
        back, unit = norm_back(grad, center, inv, gain)
        input_ref[own, :] = back
        return (sums[0] + sum_rows(grad * unit), sums[1] + sum_rows(grad), sums[2] + sum_rows(back))

    none = tuple(jnp.zeros((1, D), jnp.float32) for _ in range(3))
    sums = lax.fori_loop(0, tokens // ROWS, one_chunk, none, unroll=True)
    table = jnp.zeros((LANES, D), jnp.float32)
    for block in range(tokens // LANES):
        table = table + input_ref[block * LANES : (block + 1) * LANES, :]
    table = fold_places(table, length_ref[0])
    first = jnp.concatenate([part_ref[0:2, :], norm_part_ref[0:3, :], *sums, table[: LANES - 8]])
    base = D * cols
    flat_table(flat, base, first, table[LANES - 8 :], body, tail)
    rows = stage.shape[1]
    flat[pl.ds(base + D * VEC // LANES, rows), :] = jnp.zeros((rows, LANES), jnp.float32)
    store_pieces(shard, WHOLE, me_ref[0], pieces, stage, flat, sems)


def attn_grads(me, shard, length, d_qkv, in_low, w_attn, d_res, rows_in, vecs, masks, g_out, parts, norm_parts_in):
    rows = block_rows(shard)
    whole = shard * 32 // LANES
    tokens = rows_in.shape[0]
    counts = [len(slots) for slots in piece_slots(0, WHOLE)]
    any_space, vmem = pl.BlockSpec(memory_space=pltpu.HBM), pl.BlockSpec(memory_space=pltpu.VMEM)
    smem = pl.BlockSpec(memory_space=pltpu.SMEM)
    f32, low = jnp.float32, jnp.bfloat16
    return pl.pallas_call(
        functools.partial(attn_grad_kernel, shard),
        out_shape=(jax.ShapeDtypeStruct((tokens, D), f32),)
        + tuple(jax.ShapeDtypeStruct((n, rows, LANES), low) for n in counts),
        in_specs=[smem, smem, vmem] + [any_space] * 9,
        out_specs=(vmem,) + (any_space,) * len(counts),
        scratch_shapes=[
            pltpu.VMEM((32, rows, LANES), low),
            pltpu.VMEM((whole + rows, LANES), f32),
            pltpu.VMEM((D, LANES), f32),
            pltpu.VMEM((D, LANES), f32),
            pltpu.VMEM((2 * tokens, D), f32),
            pltpu.SemaphoreType.DMA((32,)),
            pltpu.SemaphoreType.DMA((10,)),
            pltpu.VMEM((2, tokens, D), jnp.int32),
            pltpu.VMEM((2 * tokens, D), low),
            pltpu.VMEM((D, 3 * D), low),
            pltpu.VMEM((2 * tokens, D), f32),
            pltpu.VMEM((tokens, D), f32),
            pltpu.VMEM((8, D), f32),
            pltpu.VMEM((D, D), low),
            pltpu.VMEM((8, D), f32),
            pltpu.VMEM((8, D), f32),
        ],
        compiler_params=room(40),
    )(
        jnp.reshape(me, (1,)),
        jnp.reshape(length, (1,)),
        d_qkv,
        *far(in_low, w_attn, d_res, rows_in, vecs, masks, g_out, parts, norm_parts_in),
    )


def head_kernel(shard, me_ref, pick_ref, *refs):
    pieces, (first_hbm, mask_hbm) = refs[:10], refs[10:12]
    w_ref, vec_ref, unit_ref, cls_ref = refs[12:16]
    stage, flat, first_all, picked, mask, sems, in_sems = refs[16:]
    cols = w_ref.shape[1] // LANES
    tokens = mask.shape[1]
    loads = [pltpu.make_async_copy(first_hbm, first_all, in_sems.at[2])]
    for view in range(2):
        loads.append(pltpu.make_async_copy(mask_hbm.at[view, 2], mask.at[view], in_sems.at[view]))
    for load in loads:
        load.start()
    place_blocks(shard, WHOLE, pieces, me_ref[0], stage, flat, sems)
    gather_matrix(flat, w_ref)
    for load in loads:
        load.wait()
    n = unit_ref.shape[0] // 2
    for view in range(2):
        for slot in range(n):
            at, to = pick_ref[slot], view * n + slot
            picked[to : to + 1, :] = first_all[pl.ds(view * tokens + at, 1), :]
            cls_ref[to : to + 1, 2 * D : 3 * D] = keep_of(mask[view, pl.ds(at, 1), :])
    vecs = vectors_of(flat[pl.ds(D * cols, 48), :])
    vec_ref[...] = vecs
    first = picked[...]
    up_bias = jnp.concatenate([vecs[c : c + 1] for c in range(4)], axis=1)
    up_pre = plain_rows(first.astype(jnp.bfloat16), w_ref[:, : 4 * D], NN) + up_bias
    active = gelu_exact(up_pre).astype(jnp.bfloat16)
    down = plain_rows(active, w_ref[:, 4 * D : 8 * D], NT) + vecs[4:5]
    res = first + cls_ref[:, 2 * D : 3 * D] * down
    cls_low = layer_norm(res, vecs[5:6], vecs[6:7]).astype(jnp.bfloat16)
    pooled = jnp.tanh(plain_rows(cls_low, w_ref[:, 8 * D :], NN) + vecs[7:8])
    unit_ref[...] = unit_scale(pooled).astype(jnp.bfloat16)
    cls_ref[:, :D] = pooled
    cls_ref[:, D : 2 * D] = res
    cls_ref[:, 3 * D :] = up_pre


def make_head(pieces, me, shard, picks, first_norm, masks):
    rows = pieces[0].shape[1]
    whole = shard * 32 // LANES
    n = 2 * (picks.shape[0] - 1)
    any_space, vmem = pl.BlockSpec(memory_space=pltpu.HBM), pl.BlockSpec(memory_space=pltpu.VMEM)
    smem = pl.BlockSpec(memory_space=pltpu.SMEM)
    f32, low = jnp.float32, jnp.bfloat16
    return pl.pallas_call(
        functools.partial(head_kernel, shard),
        out_shape=(
            result((D, 9 * D), low, True),
            result((8, D), f32, True),
            result((n, D), low),
            result((n, 7 * D), f32),
        ),
        in_specs=[smem] * 2 + [any_space] * (len(pieces) + 2),
        out_specs=(vmem,) * 4,
        scratch_shapes=[
            pltpu.VMEM((32, rows, LANES), low),
            pltpu.VMEM((whole + rows, LANES), f32),
            pltpu.VMEM(first_norm.shape, f32),
            pltpu.VMEM((n, D), f32),
            pltpu.VMEM((2,) + masks.shape[2:], jnp.int32),
            pltpu.SemaphoreType.DMA((32,)),
            pltpu.SemaphoreType.DMA((3,)),
        ],
        compiler_params=room(42),
    )(jnp.reshape(me, (1,)), picks, *far(*pieces, first_norm, masks))


def norm_back(grad, center, inv, gain):
    unit = center * inv
    scaled = grad * gain
    mean = jnp.mean(scaled, axis=-1, keepdims=True)
    along = jnp.mean(scaled * unit, axis=-1, keepdims=True)
    return inv * (scaled - mean - unit * along), unit


def norm_parts(rows):
    center = rows - jnp.mean(rows, axis=-1, keepdims=True)
    return center, lax.rsqrt(jnp.mean(center * center, axis=-1, keepdims=True) + norm_eps)


def gelu_slope(values):
    cdf = 0.5 * (1.0 + lax.erf(values * 0.7071067811865476))
    return cdf + values * (0.3989422804014327 * jnp.exp(-0.5 * values * values))


CHUNK = 1024


def forward_kernel(first_low, first_ref, w_ref, vec_ref, mask_hbm, cot_ref,
                   act_ref, slope_ref, hidden_ref, d_res_ref, down_ref, part_ref,
                   mask, acc, made, sems):
    tokens = mask.shape[1]
    both = 2 * tokens
    copies = []
    for view in range(2):
        copies.append(pltpu.make_async_copy(mask_hbm.at[view, 2], mask.at[view], sems.at[view]))
    for copy in copies:
        copy.start()
    vecs = vec_ref[...]
    for k in range(4 * D // CHUNK):
        cols = pl.ds(k * CHUNK, CHUNK)
        bias = jnp.concatenate([vecs[c : c + 1] for c in range(4)], axis=1)[:, k * CHUNK : (k + 1) * CHUNK]
        made[...] = plain_rows(first_low[...], w_ref[:, cols], NN)

        def one_group(group, carry, bias=bias, cols=cols):
            at = pl.ds(pl.multiple_of(group * ROWS, ROWS), ROWS)
            up = made[at, :] + bias
            cdf = 0.5 * (1.0 + lax.erf(up * 0.7071067811865476))
            act_ref[at, cols] = (up * cdf).astype(jnp.bfloat16)
            slope = cdf + up * (0.3989422804014327 * jnp.exp(-0.5 * up * up))
            slope_ref[at, cols] = slope.astype(jnp.bfloat16)
            return carry

        lax.fori_loop(0, both // ROWS, one_group, 0, unroll=4)
    for copy in copies:
        copy.wait()
    acc[...] = plain_rows(act_ref[...], w_ref[:, 4 * D : 8 * D], NT)
    sums = tuple(jnp.zeros((1, D), jnp.float32) for _ in range(3))
    for view in range(2):
        def one_chunk(chunk, sums, view=view):
            own = pl.ds(pl.multiple_of(chunk * ROWS, ROWS), ROWS)
            at = pl.ds(pl.multiple_of(view * tokens + chunk * ROWS, ROWS), ROWS)
            keep = keep_of(mask[view, own, :])
            center, inv = norm_parts(first_ref[at, :] + keep * (acc[at, :] + vecs[4:5]))
            grad = cot_ref[view, own, :].astype(jnp.float32)
            hidden_ref[view, own, :] = (center * inv * vecs[5:6] + vecs[6:7]).astype(jnp.bfloat16)
            d_res, unit = norm_back(grad, center, inv, vecs[5:6])
            d_down = d_res * keep
            d_res_ref[at, :] = d_res
            down_ref[at, :] = d_down.astype(jnp.bfloat16)
            return (sums[0] + sum_rows(d_down), sums[1] + sum_rows(grad * unit), sums[2] + sum_rows(grad))

        sums = lax.fori_loop(0, tokens // ROWS, one_chunk, sums, unroll=True)
    part_ref[...] = jnp.zeros_like(part_ref)
    for k in range(3):
        part_ref[4 + k : 5 + k, :] = sums[k]


def head_forward(first_low, first_norm, w_head, vecs, masks, cotangent):
    both = first_low.shape[0]
    tokens = both // 2
    any_space, vmem = pl.BlockSpec(memory_space=pltpu.HBM), pl.BlockSpec(memory_space=pltpu.VMEM)
    f32, low = jnp.float32, jnp.bfloat16
    return pl.pallas_call(
        forward_kernel,
        out_shape=(
            result((both, 4 * D), low, True),
            result((both, 4 * D), low, True),
            result((2, tokens, D), low),
            result((both, D), f32, True),
            result((both, D), low, True),
            result((8, D), f32, True),
        ),
        in_specs=[vmem, vmem, vmem, vmem, any_space, vmem],
        out_specs=(vmem,) * 6,
        scratch_shapes=[
            pltpu.VMEM((2, tokens, D), jnp.int32),
            pltpu.VMEM((both, D), f32),
            pltpu.VMEM((both, CHUNK), f32),
            pltpu.SemaphoreType.DMA((2,)),
        ],
        compiler_params=room(14),
    )(first_low, first_norm, w_head, vecs, masks, cotangent)


def backward_kernel(down_ref, slope_ref, d_res_ref, part_in, w_ref, up_ref, first_ref, part_ref, made):
    part_ref[...] = part_in[...]
    both = down_ref.shape[0]
    sums = []
    for k in range(4 * D // CHUNK):
        cols = pl.ds(k * CHUNK, CHUNK)
        made[...] = plain_rows(down_ref[...], w_ref[:, pl.ds(4 * D + k * CHUNK, CHUNK)], NN)

        def one_group(group, total, cols=cols):
            at = pl.ds(pl.multiple_of(group * ROWS, ROWS), ROWS)
            d_up = made[at, :] * slope_ref[at, cols].astype(jnp.float32)
            up_ref[at, cols] = d_up.astype(jnp.bfloat16)
            return total + sum_rows(d_up)

        sums.append(lax.fori_loop(0, both // ROWS, one_group, jnp.zeros((1, CHUNK), jnp.float32), unroll=4))
    sums = jnp.concatenate(sums, axis=1)
    for c in range(4):
        part_ref[c : c + 1, :] = sums[:, c * D : (c + 1) * D]
    first_ref[...] = d_res_ref[...] + plain_rows(up_ref[...], w_ref[:, : 4 * D], NT)


def head_backward(down_low, slope, d_res, parts, w_head):
    both = down_low.shape[0]
    vmem = pl.BlockSpec(memory_space=pltpu.VMEM)
    f32, low = jnp.float32, jnp.bfloat16
    return pl.pallas_call(
        backward_kernel,
        out_shape=(
            result((both, 4 * D), low, True),
            result((both, D), f32),
            result((8, D), f32, True),
        ),
        in_specs=[vmem] * 5,
        out_specs=(vmem,) * 3,
        scratch_shapes=[
            pltpu.VMEM((both, CHUNK), f32),
        ],
        compiler_params=room(10),
    )(down_low, slope, d_res, parts, w_head)


def pick_columns(core, blocks):
    shape = (blocks * 32, D)
    index = lax.broadcasted_iota(jnp.int32, shape, 0)
    wanted = (index >> 5) * 48 + 24 * core + (index & 31)
    return (wanted == lax.broadcasted_iota(jnp.int32, shape, 1)).astype(jnp.bfloat16)


def pooled_kernel(me_ref, own_ref, sib_ref, w_hbm, cls_own, cls_sib, vrow_in, vcol_in, vec_in,
                  loss_ref, first_ref, out_ref, low_ref, part_ref,
                  units, sims, back, cls, vrow_ref, vcol_ref, vec_ref, w_ref, sems, w_sems):
    me = me_ref[0]
    core = me & 1
    n = units.shape[1]
    pairs = []
    for side, ref in ((0, own_ref), (1, sib_ref)):
        for across in range(4):
            for k in range(4):
                pairs.append((ref.at[across, k], units.at[me ^ (side + 2 * across + 8 * k)]))
    place = pl.multiple_of(core * n, n)
    pairs += [(cls_own, cls.at[pl.ds(place, n)]), (cls_sib, cls.at[pl.ds(n - place, n)])]
    pairs += [(vrow_in, vrow_ref), (vcol_in, vcol_ref), (vec_in, vec_ref)]
    copies = bring(pairs, sems)
    w_copies = bring(
        [
            (w_hbm.at[:, pl.ds(start, size)], w_ref.at[:, pl.ds(start, size)])
            for start, size in ((8 * D, D), (4 * D, 4 * D), (0, 4 * D))
        ],
        w_sems,
    )
    await_all(copies)
    half = n // 2
    total = units.shape[0] * n
    everyone = units[...].reshape(total, D)
    table = plain_rows(everyone, everyone, NT) * (1.0 / logit_divisor)
    row = lax.broadcasted_iota(jnp.int32, (total, total), 0)
    col = lax.broadcasted_iota(jnp.int32, (total, total), 1)
    valid_row = vrow_ref[...] > 0
    table = jnp.where(((col & (n - 1)) >= half) & (vcol_ref[...] > 0), table, masked_scores)
    top = jnp.max(table, axis=-1, keepdims=True)
    row_lse = top + jnp.log(jnp.sum(jnp.exp(table - top), axis=-1, keepdims=True))
    diagonal = col == row + half
    positive = jnp.sum(jnp.where(diagonal, table, 0.0), axis=-1, keepdims=True)
    row_one = lax.broadcasted_iota(jnp.int32, (total, 1), 0)
    anchors = ((row_one & (n - 1)) < half) & valid_row
    loss_ref[0, 0] = jnp.sum(jnp.where(anchors, row_lse - positive, 0.0))
    slope = (jnp.exp(table - row_lse) - jnp.where(diagonal, 1.0, 0.0)) * (1.0 / logit_divisor)
    sims[...] = jnp.where(anchors, slope, 0.0).astype(jnp.bfloat16)
    back[...] = plain_rows(sims[...], everyone, TN)
    chip = pl.ds(pl.multiple_of((me >> 1) * 2 * n, 2 * n), 2 * n)
    d_unit = plain_rows(sims[chip, :], everyone, NN) + back[chip, :]
    pooled = cls[:, :D]
    inv = lax.rsqrt(jnp.sum(pooled * pooled, axis=-1, keepdims=True) + norm_eps)
    along = jnp.sum(pooled * d_unit, axis=-1, keepdims=True)
    d_pooled = inv * d_unit - pooled * (inv * inv * inv * along)
    d_pre = d_pooled * (1.0 - pooled * pooled)
    pool_low = d_pre.astype(jnp.bfloat16)
    await_all(w_copies)
    d_cls = plain_rows(pool_low, w_ref[:, 8 * D :], NT)
    center, scale = norm_parts(cls[:, D : 2 * D])
    cls_low = (center * scale * vec_ref[5:6, :] + vec_ref[6:7, :]).astype(jnp.bfloat16)
    d_res, unit = norm_back(d_cls, center, scale, vec_ref[5:6, :])
    d_down = d_res * cls[:, 2 * D : 3 * D]
    down_low = d_down.astype(jnp.bfloat16)
    d_up = plain_rows(down_low, w_ref[:, 4 * D : 8 * D], NN) * gelu_slope(cls[:, 3 * D :])
    up_low = d_up.astype(jnp.bfloat16)
    cls[:, :D] = d_res + plain_rows(up_low, w_ref[:, : 4 * D], NT)
    first_ref[...] = cls[pl.ds(place, n), :D]
    out_ref[:, :D] = d_down
    out_ref[:, D:] = d_up
    low_ref[:, :D] = cls_low
    low_ref[:, D:] = pool_low
    up_sum = jnp.sum(d_up, axis=0, keepdims=True)
    rows = [up_sum[:, c * D : (c + 1) * D] for c in range(4)]
    rows += [jnp.sum(each, axis=0, keepdims=True) for each in (d_down, d_cls * unit, d_cls, d_pre)]
    for k, value in enumerate(rows):
        part_ref[k : k + 1, :] = value


def pooled_backward(me, units, w_head, cls, valid, vecs):
    n = cls[0].shape[0]
    total = valid.shape[0]
    hbm, vmem = pl.BlockSpec(memory_space=pltpu.HBM), pl.BlockSpec(memory_space=pltpu.VMEM)
    smem = pl.BlockSpec(memory_space=pltpu.SMEM)
    f32, low = jnp.float32, jnp.bfloat16
    return pl.pallas_call(
        pooled_kernel,
        out_shape=(
            result((1, 1), f32),
            result((n, D), f32),
            result((2 * n, 5 * D), f32, True),
            result((2 * n, 2 * D), low, True),
            result((8, D), f32, True),
        ),
        in_specs=[smem] + [hbm] * 8,
        out_specs=(smem,) + (vmem,) * 4,
        scratch_shapes=[
            pltpu.VMEM((32, n, D), low),
            pltpu.VMEM((total, total), low),
            pltpu.VMEM((total, D), f32),
            pltpu.VMEM((2 * n, 7 * D), f32),
            pltpu.VMEM((total, 1), f32),
            pltpu.VMEM((1, total), f32),
            pltpu.VMEM((8, D), f32),
            pltpu.VMEM((D, 9 * D), low),
            pltpu.SemaphoreType.DMA((37,)),
            pltpu.SemaphoreType.DMA((3,)),
        ],
        compiler_params=room(25),
    )(jnp.reshape(me, (1,)), *units, *far(w_head), *cls, valid[:, None], valid[None, :], vecs)


def head_grad_kernel(shard, me_ref, pick_ref, *refs):
    mains, (cls, cls_low, cls_part, part_in, part_sib_in) = refs[:8], refs[8:13]
    pieces, scratch = refs[13:21], refs[21:]
    first, up, down, act, part, part_sib, stage, flat, sems, in_sems = scratch
    me = me_ref[0]
    core = me & 1
    many = mains[0].shape[0]
    n = cls.shape[0] // 2
    half = n // 2
    place = pl.multiple_of(core * n, n)
    pairs = []
    for k, whole in enumerate((first, up, down, act)):
        for side in range(2):
            pairs.append((mains[2 * k + side], whole.at[pl.ds(side * many, many)]))
    loads = bring(pairs + [(part_in, part), (part_sib_in, part_sib)], in_sems)
    for load in loads[:6]:
        load.wait()
    top_row = lax.broadcasted_iota(jnp.int32, (16, 1), 0) == 0
    for side in range(2):
        first_at = place if side == 0 else n - place
        for view in range(2):
            for slot in range(half):
                at = pl.multiple_of(side * many + view * (many // 2) + pick_ref[side, slot], 16)
                source = pl.ds(first_at + view * half + slot, 1)
                for whole, cols in ((up, pl.ds(D, 4 * D)), (down, pl.ds(0, D))):
                    more = jnp.where(top_row, cls[source, cols], 0.0)
                    whole[pl.ds(at, 16), :] = (whole[pl.ds(at, 16), :] + more).astype(jnp.bfloat16)
    blocks, rows = stage.shape[0], stage.shape[1]
    cols = 9 * D // LANES
    pick = pick_columns(core, blocks)

    def spread(grads, first_col):
        for block in range(blocks):
            for group in range(4):
                for k in range(grads.shape[1] // LANES):
                    at = group * 8 * cols + first_col + k
                    size = 8 if group < 3 else 2
                    tile = grads[block * 32 + group * 8 : block * 32 + group * 8 + size]
                    flat[block, pl.ds(at, size, stride=cols), :] = tile[:, k * LANES : (k + 1) * LANES]

    def fill(left, right, first_col):
        chunk = 4 * LANES
        for k in range(right.shape[1] // chunk):
            spread(plain_rows(left, right[:, pl.ds(k * chunk, chunk)], NN), first_col + k * chunk // LANES)

    fill(plain_rows(pick, first[...], NT).astype(jnp.bfloat16), up, 0)
    few = plain_rows(pick, cls_low[:, :D], NT).astype(jnp.bfloat16)
    spread(plain_rows(few, cls_low[:, D:], NN), 8 * D // LANES)
    for load in loads[6:]:
        load.wait()
    fill(plain_rows(pick, down[...], NT).astype(jnp.bfloat16), act, 4 * D // LANES)

    @pl.when(core == 1)
    def _():
        flat[blocks - 1, pl.ds(24 * cols, 48), :] = flat_of(part[...] + part_sib[...] + cls_part[...])

    outs = []
    for piece, slots in list(zip(pieces, piece_slots(me, HALVES)))[::-1]:
        for k, slot in enumerate(slots):
            chip_at = slot >> 1
            at = pl.multiple_of(slot * shard // LANES // 8 * 8 - slot * 24 * cols, 8)
            stage[chip_at] = flat[chip_at, pl.ds(at, rows), :].astype(jnp.bfloat16)
            copy = pltpu.make_async_copy(stage.at[chip_at], piece.at[k], sems.at[len(outs)])
            copy.start()
            outs.append(copy)
    for copy in outs:
        copy.wait()


def head_grads(me, shard, picks, mains, cls, cls_low, cls_part, parts):
    many = mains[0].shape[0]
    rows = block_rows(shard)
    hbm, vmem = pl.BlockSpec(memory_space=pltpu.HBM), pl.BlockSpec(memory_space=pltpu.VMEM)
    smem = pl.BlockSpec(memory_space=pltpu.SMEM)
    f32, low = jnp.float32, jnp.bfloat16
    return pl.pallas_call(
        functools.partial(head_grad_kernel, shard),
        out_shape=tuple(result((2, rows, LANES), low) for _ in HALVES),
        in_specs=[smem] * 2 + [hbm] * 8 + [vmem] * 3 + [hbm] * 2,
        out_specs=(hbm,) * len(HALVES),
        scratch_shapes=[
            pltpu.VMEM((2 * many, D), low),
            pltpu.VMEM((2 * many, 4 * D), low),
            pltpu.VMEM((2 * many, D), low),
            pltpu.VMEM((2 * many, 4 * D), low),
            pltpu.VMEM((8, D), f32),
            pltpu.VMEM((8, D), f32),
            pltpu.VMEM((16, rows, LANES), low),
            pltpu.VMEM((16, 26 * 9 * D // LANES + 4, LANES), f32),
            pltpu.SemaphoreType.DMA((16,)),
            pltpu.SemaphoreType.DMA((10,)),
        ],
        compiler_params=room(44),
    )(jnp.reshape(me, (1,)), picks, *mains, cls, cls_low, cls_part, *parts)


def store_pieces(shard, layout, me, pieces, stage, flat, sems):
    rows = stage.shape[1]
    copies = []
    for piece, slots in list(zip(pieces, piece_slots(me, layout)))[::-1]:
        for k, slot in enumerate(slots):
            at = pl.multiple_of(slot * shard // LANES // 8 * 8, 8)
            stage[slot] = flat[pl.ds(at, rows), :].astype(jnp.bfloat16)
            copy = pltpu.make_async_copy(stage.at[slot], piece.at[k], sems.at[len(copies)])
            copy.start()
            copies.append(copy)
    for copy in copies:
        copy.wait()


def sum_small(value):
    for bit in (CORE, XBIT, YBIT, 8, 16):
        value = value + swap(value, bit)
    return value


def on_grid(
    embeddings,
    cotangent,
    drop_masks,
    lengths,
    buckets,
    attn_params,
    attn_moment,
    attn_second,
    attn_ema,
    head_params,
    head_moment,
    head_second,
    head_ema,
):
    tok_rows = embeddings.shape[0]
    slot_count = lengths.shape[0]
    all_rows = 2 * tok_rows
    device = lax.axis_index("sent")
    shards = (attn_params.shape[0], head_params.shape[0])
    attn_pieces, attn_first, attn_last = gather_attn(attn_params, device)
    head_zs = gather_head_line(head_params, device, attn_first)
    bucket_all = bucket_length(buckets)
    slot_ids = jnp.arange(slot_count, dtype=jnp.int32)
    valid_everything = (
        (slot_ids[None, :] < (tok_rows // bucket_all)[:, None]).astype(jnp.float32).reshape(-1)
    )
    bucket_len = bucket_all[device]

    def picks_of(length):
        count = tok_rows // length
        return jnp.concatenate([jnp.minimum(slot_ids, count - 1) * length, count[None]])

    picks = picks_of(bucket_len)
    both_picks = jnp.stack([picks, picks_of(bucket_all[device ^ CORE])])
    head_line = after(jnp.stack(head_zs), *attn_last)
    head_x, head_y = swap(head_line, XBIT), swap(head_line, YBIT)
    (
        attn_mats,
        attn_vecs,
        emb_rows,
        attn_in_low,
        qkv_low,
        probs,
        mixed_low,
        first_res,
        first_norm,
        first_low,
    ) = attn_forward(attn_pieces, device, shards[0], bucket_len, lengths, embeddings, drop_masks)
    head_x, head_y, first_norm = lax.optimization_barrier((head_x, head_y, first_norm))
    head_pieces = gather_head(head_line, head_x, head_y)
    first_sib = swap(first_low, CORE)
    head_mats, head_vecs, unit_low, cls = make_head(
        head_pieces, device, shards[1], picks, first_norm, drop_masks
    )
    unit_zs = [unit_low] + [swap(unit_low, bit) for bit in ZBITS]
    cls_sib = swap(cls, CORE)
    active_low, slope, hidden_out, d_second_res, down_low, parts = head_forward(
        first_low, first_norm, head_mats, head_vecs, drop_masks, cotangent
    )
    active_low, down_low, unit_zs, cls_sib = lax.optimization_barrier(
        (active_low, down_low, unit_zs, cls_sib)
    )
    unit_line = jnp.stack(unit_zs)
    unit_lines = [unit_line] + [swap(unit_line, bit) for bit in (XBIT, YBIT, XBIT | YBIT)]
    active_sib, down_sib = swap(active_low, CORE), swap(down_low, CORE)
    up_low, d_first, parts = head_backward(down_low, slope, d_second_res, parts, head_mats)
    up_low, unit_lines, active_sib, down_sib = lax.optimization_barrier(
        (up_low, unit_lines, active_sib, down_sib)
    )
    units = jnp.stack(unit_lines)
    units_sib = swap(units, CORE)
    up_sib, parts_sib = swap(after(up_low, units_sib), CORE), swap(parts, CORE)
    valid_views = jnp.broadcast_to(
        valid_everything.reshape(-1, 1, slot_count), (bucket_all.shape[0], 2, slot_count)
    ).reshape(-1)
    loss_sum, d_first_cls, cls_grads, cls_low, cls_part = pooled_backward(
        device, (units, units_sib), head_mats, (cls, cls_sib), valid_views, head_vecs
    )
    head_pieces = head_grads(
        device,
        shards[1],
        both_picks,
        (first_low, first_sib, up_low, up_sib, down_low, down_sib, active_low, active_sib),
        cls_grads,
        cls_low,
        cls_part,
        (parts, parts_sib),
    )
    loss_sum = loss_sum[0, 0]
    d_first, head_pieces = lax.optimization_barrier((d_first, head_pieces))
    line_low, line_high, x_low, x_high, y_low, y_high, d_low, d_high = head_pieces
    d_low, d_high = swap(d_low, XBIT), swap(d_high, YBIT)
    d_first_res, g_out, d_mixed, norm_parts_in = norm_backward(
        picks, d_first, d_first_cls, first_res, attn_vecs, drop_masks, mixed_low, attn_mats
    )
    d_qkv, attn_parts = attn_backward(d_mixed, qkv_low, probs)
    d_qkv, d_low, d_high = lax.optimization_barrier((d_qkv, d_low, d_high))
    x_high, y_high = swap(low_sum(x_high, d_high), XBIT), swap(y_high, YBIT)
    input_grad, *attn_pieces = attn_grads(
        device,
        shards[0],
        bucket_len,
        d_qkv,
        attn_in_low,
        attn_mats,
        d_first_res,
        emb_rows,
        attn_vecs,
        drop_masks,
        g_out,
        attn_parts,
        norm_parts_in,
    )
    attn_pieces, d_low, x_low, x_high, y_high = lax.optimization_barrier(
        (attn_pieces, d_low, x_low, x_high, y_high)
    )
    line_high = low_sum(line_high, x_high, y_high)
    x_low, y_low = swap(x_low, XBIT), swap(low_sum(y_low, d_low), YBIT)
    attn_sums = scatter_core(attn_pieces)
    attn_sums, x_low, y_low = lax.optimization_barrier((attn_sums, x_low, y_low))
    line_low = low_sum(line_low, x_low, y_low)
    head_sum = scatter_along(line_low[0], [line_low[1], line_high[0], line_high[1]])
    head_share = unpack_shard(head_sum, device, shards[1])
    attn_share = unpack_shard(scatter_attn(attn_sums), device, shards[0])
    squares = jnp.sum(attn_share * attn_share) + jnp.sum(head_share * head_share)
    total_squares = sum_small(squares)
    loss = loss_sum / jnp.sum(valid_everything)
    grad_norm = jnp.sqrt(total_squares)
    clip_scale = jnp.minimum(1.0, clip_bound / grad_norm)
    attn_new = adam_step(attn_share * clip_scale, attn_params, attn_moment, attn_second, attn_ema)
    head_new = adam_step(head_share * clip_scale, head_params, head_moment, head_second, head_ema)
    return (
        hidden_out,
        input_grad,
        loss,
        grad_norm,
        attn_new[0],
        attn_new[1],
        attn_new[2],
        attn_new[3],
        head_new[0],
        head_new[1],
        head_new[2],
        head_new[3],
    )


def on_any_mesh(
    embeddings,
    cotangent,
    drop_masks,
    lengths,
    buckets,
    attn_params,
    attn_moment,
    attn_second,
    attn_ema,
    head_params,
    head_moment,
    head_second,
    head_ema,
):
    tok_rows = embeddings.shape[0]
    slot_count = lengths.shape[0]
    all_rows = 2 * tok_rows
    device = lax.axis_index("sent")
    attn_full, head_full = (
        lax.all_gather(attn_params.astype(jnp.bfloat16), "sent", axis=0, tiled=True),
        lax.all_gather(head_params.astype(jnp.bfloat16), "sent", axis=0, tiled=True),
    )
    attn_mats = attn_full[: 4 * D * D].reshape(D, 4 * D)
    attn_vecs_low = attn_full[4 * D * D :].reshape(D, 8 + POS)
    attn_vecs = attn_vecs_low.astype(jnp.float32)
    head_mats = head_full[: 9 * D * D].reshape(D, 9 * D)
    head_vecs = head_full[9 * D * D :].reshape(D, 8).astype(jnp.float32)
    w_qkv = attn_mats[:, : 3 * D]
    w_out = attn_mats[:, 3 * D :]
    w_up = head_mats[:, : 4 * D]
    w_down = head_mats[:, 4 * D : 8 * D]
    w_pool = head_mats[:, 8 * D :]
    bucket_all = bucket_length(buckets)
    slot_ids = jnp.arange(slot_count, dtype=jnp.int32)
    valid_everything = (
        (slot_ids[None, :] < (tok_rows // bucket_all)[:, None]).astype(jnp.float32).reshape(-1)
    )
    bucket_len = bucket_all[device]
    sent_count = tok_rows // bucket_len
    valid_own = (slot_ids < sent_count).astype(jnp.float32)
    row_ids = jnp.arange(tok_rows, dtype=jnp.int32)
    sentence = row_ids // bucket_len
    row_place = row_ids % bucket_len
    slot_len = jnp.sum(
        jnp.where(sentence[:, None] == slot_ids[None, :], lengths[None, :], 0), axis=1
    )
    key_ok = row_place < slot_len
    block = POS
    sent_blocks = sentence.reshape(-1, block)
    ok_blocks = key_ok.reshape(-1, block)
    allowed = (sent_blocks[:, :, None] == sent_blocks[:, None, :]) & ok_blocks[:, None, :]
    allowed = jnp.concatenate([allowed, allowed], axis=0)[:, None]
    place_hot = (row_place[:, None] == jnp.arange(POS, dtype=jnp.int32)[None, :]).astype(
        jnp.bfloat16
    )
    pos_rows = plain_dot(place_hot, attn_vecs_low[:, 8:].T)
    emb_rows = embeddings.astype(jnp.float32) + pos_rows + attn_vecs[:, 7]
    normed, emb_back = jax.vjp(layer_norm, emb_rows, attn_vecs[:, 5], attn_vecs[:, 6])
    keep_masks = drop_masks.astype(jnp.float32) / keep_prob
    keep_attn = keep_masks[:, 1].reshape(all_rows, D)
    keep_ffn = keep_masks[:, 2].reshape(all_rows, D)
    attn_in = (normed[None] * keep_masks[:, 0]).reshape(all_rows, D)
    attn_in_low = attn_in.astype(jnp.bfloat16)
    qkv_bias = jnp.concatenate([attn_vecs[:, 0], jnp.zeros((D,), jnp.float32), attn_vecs[:, 1]])
    qkv_low = (plain_dot(attn_in_low, w_qkv) + qkv_bias).astype(jnp.bfloat16)
    head_split = qkv_low.reshape(-1, block, 3, H, HD)
    queries = head_split[:, :, 0]
    keys_low = head_split[:, :, 1]
    values_low = head_split[:, :, 2]
    score_scale = HD ** (-0.5)
    raw_scores = jnp.einsum(
        "bqhd,bkhd->bhqk", queries, keys_low, preferred_element_type=jnp.float32
    )
    scores = jnp.where(allowed, raw_scores * score_scale, masked_scores)
    row_top = jnp.max(scores, axis=-1, keepdims=True)
    expo_vals = jnp.exp(scores - row_top)
    row_total = jnp.sum(expo_vals, axis=-1, keepdims=True)
    attn_probs = expo_vals / row_total
    score_lse = row_top + jnp.log(row_total)
    mixed_out = jnp.einsum(
        "bhqk,bkhd->bqhd",
        attn_probs.astype(jnp.bfloat16),
        values_low,
        preferred_element_type=jnp.float32,
    )
    mixed_low = mixed_out.reshape(all_rows, D).astype(jnp.bfloat16)
    branch = plain_dot(mixed_low, w_out) + attn_vecs[:, 2]
    first_res = attn_in + keep_attn * branch
    first_norm, first_back = jax.vjp(layer_norm, first_res, attn_vecs[:, 3], attn_vecs[:, 4])
    first_low = first_norm.astype(jnp.bfloat16)
    up_bias = head_vecs[:, :4].T.reshape(4 * D)
    up_pre = plain_dot(first_low, w_up) + up_bias
    active, gelu_back = jax.vjp(gelu_exact, up_pre)
    active_low = active.astype(jnp.bfloat16)
    down_out = target_dot_terms(active_low, w_down) + head_vecs[:, 4]
    second_res = first_norm + keep_ffn * down_out
    second_norm, second_back = jax.vjp(layer_norm, second_res, head_vecs[:, 5], head_vecs[:, 6])
    hidden_out = second_norm.astype(jnp.bfloat16).reshape(2, tok_rows, D)
    cls_pick = jnp.minimum(slot_ids, sent_count - 1) * bucket_len
    cls_rows = jnp.take(second_norm.reshape(2, tok_rows, D), cls_pick, axis=1).reshape(
        2 * slot_count, D
    )
    cls_low = cls_rows.astype(jnp.bfloat16)
    pooled = jnp.tanh(plain_dot(cls_low, w_pool) + head_vecs[:, 7])
    unit_rows, unit_back = jax.vjp(unit_scale, pooled)
    unit_low = unit_rows.astype(jnp.bfloat16)
    query_embeddings = unit_low[:slot_count]
    positive_view_set = unit_low[slot_count:]
    target_sentence_set, everyone = (
        lax.all_gather(positive_view_set, "sent", axis=0, tiled=True),
        lax.all_gather(query_embeddings, "sent", axis=0, tiled=True),
    )
    own_cols = device * slot_count + slot_ids
    col_ids = jnp.arange(target_sentence_set.shape[0], dtype=jnp.int32)
    pos_hot = col_ids[None, :] == own_cols[:, None]
    cosine_logit_table = jnp.where(
        valid_everything[None, :] > 0,
        target_dot_terms(query_embeddings, target_sentence_set) / logit_divisor,
        masked_scores,
    )
    sim_top = jnp.max(cosine_logit_table, axis=-1, keepdims=True)
    row_lse = sim_top[:, 0] + jnp.log(jnp.sum(jnp.exp(cosine_logit_table - sim_top), axis=-1))
    positive = jnp.sum(jnp.where(pos_hot, cosine_logit_table, 0.0), axis=-1)
    local_loss = jnp.sum(valid_own * (row_lse - positive))
    loss_sum = lax.psum(local_loss, "sent")
    cosine_logit_cotangent = valid_own[:, None] * (
        jnp.exp(cosine_logit_table - row_lse[:, None]) - pos_hot.astype(jnp.float32)
    )
    cosine_logit_summed = (cosine_logit_cotangent / logit_divisor).astype(jnp.bfloat16)
    d_anchor = plain_dot(cosine_logit_summed, target_sentence_set)
    all_lse = lax.all_gather(row_lse, "sent", axis=0, tiled=True)
    back_sim = target_dot_terms(everyone, positive_view_set) / logit_divisor
    back_hot = (col_ids[:, None] == own_cols[None, :]).astype(jnp.float32)
    back_grad = valid_everything[:, None] * (
        jnp.exp(back_sim - all_lse[:, None]) * valid_own[None, :] - back_hot
    )
    d_partner = rows_dot((back_grad / logit_divisor).astype(jnp.bfloat16), everyone)
    d_unit = jnp.concatenate([d_anchor, d_partner], axis=0)
    d_pooled = unit_back(d_unit)[0]
    d_pool_pre = d_pooled * (1.0 - pooled * pooled)
    pool_low = d_pool_pre.astype(jnp.bfloat16)
    g_pool = rows_dot(cls_low, pool_low)
    g_pool_bias = jnp.sum(d_pool_pre, axis=0)
    d_cls = target_dot_terms(pool_low, w_pool).reshape(2, slot_count, D)
    pick_hot = ((row_ids[None, :] == cls_pick[:, None]) & (slot_ids[:, None] < sent_count)).astype(
        jnp.float32
    )
    d_second = cotangent.astype(jnp.float32) + jnp.einsum(
        "st,vsd->vtd", pick_hot, d_cls, precision=highest
    )
    d_second_res, g_gain_two, g_shift_two = second_back(d_second.reshape(all_rows, D))
    d_down = d_second_res * keep_ffn
    g_down_bias = jnp.sum(d_down, axis=0)
    down_low = d_down.astype(jnp.bfloat16)
    g_down = rows_dot(down_low, active_low)
    d_active = plain_dot(down_low, w_down)
    d_up = gelu_back(d_active)[0]
    g_up_bias = jnp.sum(d_up, axis=0)
    up_low = d_up.astype(jnp.bfloat16)
    g_up = rows_dot(first_low, up_low)
    d_first = d_second_res + target_dot_terms(up_low, w_up)
    head_vec_grad = jnp.concatenate(
        [
            g_up_bias.reshape(4, D).T,
            jnp.stack([g_down_bias, g_gain_two, g_shift_two, g_pool_bias], axis=1),
        ],
        axis=1,
    )
    head_grad = jnp.concatenate(
        [jnp.concatenate([g_up, g_down, g_pool], axis=1).reshape(-1), head_vec_grad.reshape(-1)]
    )
    d_first_res, g_gain_one, g_shift_one = first_back(d_first)
    d_branch = d_first_res * keep_attn
    g_out_bias = jnp.sum(d_branch, axis=0)
    branch_low = d_branch.astype(jnp.bfloat16)
    g_out = rows_dot(mixed_low, branch_low)
    d_mixed = target_dot_terms(branch_low, w_out).astype(jnp.bfloat16).reshape(-1, block, H, HD)
    again = jnp.where(
        allowed,
        jnp.einsum("bqhd,bkhd->bhqk", queries, keys_low, preferred_element_type=jnp.float32)
        * score_scale,
        masked_scores,
    )
    probs_again = jnp.exp(again - score_lse)
    d_values = jnp.einsum(
        "bhqk,bqhd->bkhd",
        probs_again.astype(jnp.bfloat16),
        d_mixed,
        preferred_element_type=jnp.float32,
    )
    d_probs = jnp.einsum("bqhd,bkhd->bhqk", d_mixed, values_low, preferred_element_type=jnp.float32)
    row_delta = jnp.sum(probs_again * d_probs, axis=-1, keepdims=True)
    score_low = (probs_again * (d_probs - row_delta) * score_scale).astype(jnp.bfloat16)
    d_queries = jnp.einsum(
        "bhqk,bkhd->bqhd", score_low, keys_low, preferred_element_type=jnp.float32
    )
    d_keys = jnp.einsum("bhqk,bqhd->bkhd", score_low, queries, preferred_element_type=jnp.float32)
    d_qkv = jnp.stack([d_queries, d_keys, d_values], axis=2).reshape(all_rows, 3 * D)
    g_q_bias = jnp.sum(d_queries.reshape(all_rows, D), axis=0)
    g_v_bias = jnp.sum(d_values.reshape(all_rows, D), axis=0)
    qkv_grad_low = d_qkv.astype(jnp.bfloat16)
    g_qkv = rows_dot(attn_in_low, qkv_grad_low)
    d_attn_in = d_first_res + target_dot_terms(qkv_grad_low, w_qkv)
    d_normed = jnp.sum(d_attn_in.reshape(2, tok_rows, D) * keep_masks[:, 0], axis=0)
    input_grad, g_gain_emb, g_shift_emb = emb_back(d_normed)
    g_type = jnp.sum(input_grad, axis=0)
    g_table = lax.dot_general(
        place_hot.astype(jnp.float32),
        input_grad,
        (((0,), (0,)), ((), ())),
        precision=highest,
        preferred_element_type=jnp.float32,
    )
    attn_vec_grad = jnp.concatenate(
        [
            jnp.stack(
                [
                    g_q_bias,
                    g_v_bias,
                    g_out_bias,
                    g_gain_one,
                    g_shift_one,
                    g_gain_emb,
                    g_shift_emb,
                    g_type,
                ],
                axis=1,
            ),
            g_table.T,
        ],
        axis=1,
    )
    attn_grad = jnp.concatenate(
        [jnp.concatenate([g_qkv, g_out], axis=1).reshape(-1), attn_vec_grad.reshape(-1)]
    )
    attn_share, head_share = (
        lax.psum_scatter(attn_grad, "sent", scatter_dimension=0, tiled=True),
        lax.psum_scatter(head_grad, "sent", scatter_dimension=0, tiled=True),
    )
    squares = jnp.sum(attn_share * attn_share) + jnp.sum(head_share * head_share)
    total_squares = lax.psum(squares, "sent")
    loss = loss_sum / jnp.sum(valid_everything)
    grad_norm = jnp.sqrt(total_squares)
    clip_scale = jnp.minimum(1.0, clip_bound / grad_norm)
    attn_new = adam_step(attn_share * clip_scale, attn_params, attn_moment, attn_second, attn_ema)
    head_new = adam_step(head_share * clip_scale, head_params, head_moment, head_second, head_ema)
    return (
        hidden_out,
        input_grad,
        loss,
        grad_norm,
        attn_new[0],
        attn_new[1],
        attn_new[2],
        attn_new[3],
        head_new[0],
        head_new[1],
        head_new[2],
        head_new[3],
    )


def on_device(*arrays):
    shards = (arrays[5].shape[0], arrays[9].shape[0])
    local = on_grid if is_grid(lax.axis_size("sent"), *shards) else on_any_mesh
    return local(*arrays)


def solution(mesh):
    in_specs = (
        P("sent", None),
        P(None, "sent", None),
        P(None, None, "sent", None),
        P("sent"),
        P(),
        P("sent"),
        P("sent"),
        P("sent"),
        P("sent"),
        P("sent"),
        P("sent"),
        P("sent"),
        P("sent"),
    )
    out_specs = (
        P(None, "sent", None),
        P("sent", None),
        P(),
        P(),
        P("sent"),
        P("sent"),
        P("sent"),
        P("sent"),
        P("sent"),
        P("sent"),
        P("sent"),
        P("sent"),
    )
    return jax.shard_map(
        on_device, mesh=mesh, in_specs=in_specs, out_specs=out_specs, check_vma=False
    )
```

profile of v0, /device:TPU:0, one launch (start us, length us, event | category | flops | bytes accessed | tf_op | source)
XLA Modules:
  0.0 322.4 jit_solution(6506354956674419703)
XLA Ops:
  0.7 1.2 select_bitcast_fusion.1
  2.0 3.1 collective-permute-start
  5.1 2.6 collective-permute-start.1
  7.7 3.8 %collective-permute-done = bf16[624,128]{1,0:T(8,128)(2,1)S(1)} collective-permute-done((bf16[624,128]{1,0:T(8,128)(2,1)S(1)}, bf16[624,128]{1,0:T(8,128)(2,1)S(1)}, u32[]{:S(2)}, u32[]{:S(2)}) %collective-permute-start) | collective-permute-done | bytes 159776 | tf_op jit(solution)/shard_map/ppermute | solution.py:111
  11.6 8.3 %collective-permute-done.1 = bf16[624,128]{1,0:T(8,128)(2,1)S(1)} collective-permute-done((bf16[624,128]{1,0:T(8,128)(2,1)S(1)}, bf16[624,128]{1,0:T(8,128)(2,1)S(1)}, u32[]{:S(2)}, u32[]{:S(2)}) %collective-permute-start.1) | collective-permute-done | bytes 159776 | tf_op jit(solution)/shard_map/ppermute | solution.py:111
  20.0 1.6 collective-permute-start.4
  21.6 1.5 collective-permute-start.3
  23.4 2.3 collective-permute-start.14
  25.7 1.9 collective-permute-start.12
  27.8 5.9 %collective-permute-done.4.refs_2_ = bf16[4,624,128]{2,1,0:T(8,128)(2,1)S(1)} collective-permute-done((bf16[4,624,128]{2,1,0:T(8,128)(2,1)S(1)}, bf16[4,624,128]{2,1,0:T(8,128)(2,1)S(1)}, u32[]{:S(2)}, u32[]{:S(2)}) %collective-permute-start.4) | collective-permute-done | bytes 639008 | tf_op jit(solution)/shard_map/ppermute | solution.py:111
  33.7 1.6 collective-permute-start.5
  35.3 1.7 collective-permute-done.3.refs_1_
  37.4 3.6 %collective-permute-done.12 = bf16[1312,128]{1,0:T(8,128)(2,1)S(1)} collective-permute-done((bf16[1312,128]{1,0:T(8,128)(2,1)S(1)}, bf16[1312,128]{1,0:T(8,128)(2,1)S(1)}, u32[]{:S(2)}, u32[]{:S(2)}) %collective-permute-start.12) | collective-permute-done | bytes 335904 | tf_op jit(solution)/shard_map/ppermute | solution.py:111
  41.0 12.5 %collective-permute-done.13 = bf16[1312,128]{1,0:T(8,128)(2,1)S(1)} collective-permute-done((bf16[1312,128]{1,0:T(8,128)(2,1)S(1)}, bf16[1312,128]{1,0:T(8,128)(2,1)S(1)}, u32[]{:S(2)}, u32[]{:S(2)}) %collective-permute-start.13) | collective-permute-done | bytes 335904 | tf_op jit(solution)/shard_map/ppermute | solution.py:111
  53.4 1.2 pad_maximum_fusion.refs_0_
  56.4 1.5 collective-permute-done.7.refs_5_
  58.0 1.7 collective-permute-done.8.refs_6_
  62.3 20.3 %shard_map.220 = (bf16[768,3072]{1,0:T(8,128)(2,1)}, f32[8,768]{1,0:T(8,128)}, f32[256,768]{1,0:T(8,128)}, bf16[512,768]{1,0:T(8,128)(2,1)}, bf16[512,2304]{1,0:...) custom-call(s32[1]{0:T(128)} %bitcast.me_ref, ...), custom_call_target="tpu_custom_call" | custom-call | tf_op jit(solution)/shard_map/pallas_call | solution.py:454
  82.6 3.2 %collective-permute-done.15.refs_1_ = bf16[4,1312,128]{2,1,0:T(8,128)(2,1)} collective-permute-done((bf16[4,1312,128]{2,1,0:T(8,128)(2,1)}, bf16[4,1312,128]{2,1,0:T(8,128)(2,1)}, u32[]{:S(2)}, u32[]{:S(2)}) %collective-permute-start.15) | collective-permute-done | bytes 1343520 | tf_op jit(solution)/shard_map/ppermute | solution.py:111
  86.1 1.1 slice.65
  87.3 1.1 slice.64
  88.4 1.6 collective-permute-start.17
  90.7 15.3 %collective-permute-done.17.refs_3_ = bf16[2,1312,128]{2,1,0:T(8,128)(2,1)S(1)} collective-permute-done((bf16[2,1312,128]{2,1,0:T(8,128)(2,1)S(1)}, bf16[2,1312,128]{2,1,0:T(8,128)(2,1)S(1)}, u32[]{:S(2)}, u32[]{:S(2)}) %collective-permute-start.17) | collective-permute-done | bytes 671776 | tf_op jit(solution)/shard_map/ppermute | solution.py:111
  106.0 1.5 collective-permute-done.18.refs_4_
  110.3 11.6 %shard_map.221 = (bf16[768,6912]{1,0:T(8,128)(2,1)S(1)}, f32[8,768]{1,0:T(8,128)S(1)}, bf16[16,768]{1,0:T(8,128)(2,1)S(1)}, f32[16,5376]{1,0:T(8,128)S(1)}) custom-call(s32[1]{0:T(128)} %bitcast.me_ref, s32[9]{0:T(128)S(1)} %pad_add_fusion.1.pick_ref, bf16[4,1312,128]{2,1,0:T(8,128)(2,1)} %pad_maximum_fusion.refs_0_, ...), custom_call_target="tpu_custom_call" | custom-call | tf_op jit(solution)/shard_map/pallas_call | solution.py:744
  122.5 4.4 %collective-permute-start.25 = (bf16[16,768]{1,0:T(8,128)(2,1)S(1)}, bf16[16,768]{1,0:T(8,128)(2,1)S(1)}, u32[]{:S(2)}, u32[]{:S(2)}) collective-permute-start(bf16[16,768]{1,0:T(8,128)(2,1)S(1)} %get-tuple-element.138), channel_id=1, source_target_pairs={{0,16},{1,17},{2,18},{3,19},{4,20},{5,21},{6,22},{7,23},{8,24},{9,... | collective-permute-start | bytes 73736 | tf_op jit(solution)/shard_map/ppermute | solution.py:111
  127.0 12.8 %shard_map.222 = (bf16[512,3072]{1,0:T(8,128)(2,1)S(1)}, bf16[512,3072]{1,0:T(8,128)(2,1)S(1)}, bf16[2,256,768]{2,1,0:T(8,128)(2,1)}, f32[512,768]{1,0:T(8,128)S...) custom-call(bf16[512,768]{1,0:T(8,128)(2,1)S(1)} %copy-done.2, f32[512,768]{1,0:T(8,128)S(1)} %copy-done.1, ...), custom_call_target="tpu_custom_call" | custom-call | tf_op jit(solution)/shard_map/pallas_call | solution.py:843
  141.9 2.1 collective-permute-start.31
  144.0 9.6 %shard_map.223 = (bf16[512,3072]{1,0:T(8,128)(2,1)}, f32[512,768]{1,0:T(8,128)S(1)}, f32[8,768]{1,0:T(8,128)S(1)}) custom-call(bf16[512,768]{1,0:T(8,128)(2,1)S(1)} %get-tuple-element.132.down_ref.refs_4_, bf16[512,3072]{1,0:T(8,128)(2,1)S(1)} %get-tuple-element.133.slope_ref, f32[512,768]{1,0:T(8,128)S(1)} %get-tuple-element.134.d_res_ref, ...), custom_call_target="tpu_custom_call" | custom-call | tf_op jit(solution)/shard_map/pallas_call | solution.py:890
  153.6 1.2 copy-done.6
  155.0 1.7 collective-permute-done.34.sib_ref
  160.5 1.0 copy-done.17
  161.5 1.0 copy-done.19
  162.5 9.1 %shard_map.224 = (f32[1,1]{1,0:T(1,128)}, f32[16,768]{1,0:T(8,128)S(1)}, f32[32,3840]{1,0:T(8,128)S(1)}, bf16[32,1536]{1,0:T(8,128)(2,1)S(1)}, f32[8,768]{1,0:T(8,128)S(1)}) custom-call(s32[1]{0:T(128)} %bitcast.me_ref, bf16[4,4,16,768]{3,2,1,0:T(8,128)(2,1)S(1)} %pad_maximum_fusion.4.own_ref, bf16[4,4,16,768]{3,2,1,0:T(8,128)(2,1)S(1)} %collective-permute-done.34.sib_ref, ...), custom_call_target="tpu_custom_call" | custom-call | tf_op jit(solution)/shard_map/pallas_call | solution.py:990
  172.2 16.6 %shard_map.225 = (bf16[2,1312,128]{2,1,0:T(8,128)(2,1)S(1)}, bf16[2,1312,128]{2,1,0:T(8,128)(2,1)S(1)}, bf16[2,1312,128]{2,1,0:T(8,128)(2,1)S(1)}, bf16[2,1312,1...) custom-call(s32[1]{0:T(128)} %bitcast.me_ref, ...), custom_call_target="tpu_custom_call" | custom-call | tf_op jit(solution)/shard_map/pallas_call | solution.py:1092
  191.1 1.3 collective-permute-start.40
  192.4 6.1 %shard_map.226 = (f32[512,768]{1,0:T(8,128)S(1)}, bf16[768,768]{1,0:T(8,128)(2,1)S(1)}, bf16[512,768]{1,0:T(8,128)(2,1)S(1)}, f32[8,768]{1,0:T(8,128)S(1)}) custom-call(s32[9]{0:T(128)S(1)} %pad_add_fusion.1.pick_ref, f32[512,768]{1,0:T(8,128)} %copy-done.6, f32[16,768]{1,0:T(8,128)} %copy-done.20, f32[512,768]{1,0:T(8,128)} %get-tuple-element.166.res_in, ...), custom_call_target="tpu_custom_call" | custom-call | tf_op jit(solution)/shard_map/pallas_call | solution.py:529
  198.5 8.0 %shard_map.227 = (bf16[512,2304]{1,0:T(8,128)(2,1)S(1)}, f32[8,768]{1,0:T(8,128)S(1)}) custom-call(bf16[512,768]{1,0:T(8,128)(2,1)S(1)} %get-tuple-element.170.d_mixed, bf16[512,2304]{1,0:T(8,128)(2,1)S(1)} %copy-done.5, f32[4,6,256,128]{3,2,1,0:T(8,128)S(1)} %copy-done.4), custom_call_target="tpu_custom_call" | custom-call | tf_op jit(solution)/shard_map/pallas_call | solution.py:584
  208.2 1.0 add_convert_fusion.3
  209.2 1.4 collective-permute-start.39
  212.6 18.8 %shard_map.228 = (f32[256,768]{1,0:T(8,128)}, bf16[4,624,128]{2,1,0:T(8,128)(2,1)S(1)}, bf16[4,624,128]{2,1,0:T(8,128)(2,1)S(1)}, bf16[4,624,128]{2,1,0:T(8,128)...) custom-call(s32[1]{0:T(128)} %bitcast.me_ref, ...), custom_call_target="tpu_custom_call" | custom-call | tf_op jit(solution)/shard_map/pallas_call | solution.py:667
  233.5 1.4 add_convert_fusion
  236.8 1.5 collective-permute-start.56
  238.4 2.5 collective-permute-start.57
  241.3 6.4 %collective-permute-done.47 = bf16[2,1312,128]{2,1,0:T(8,128)(2,1)S(1)} collective-permute-done((bf16[2,1312,128]{2,1,0:T(8,128)(2,1)S(1)}, bf16[2,1312,128]{2,1,0:T(8,128)(2,1)S(1)}, u32[]{:S(2)}, u32[]{:S(2)}) %collective-permute-start.47) | collective-permute-done | bytes 671776 | tf_op jit(solution)/shard_map/ppermute | solution.py:111
  247.7 5.3 %collective-permute-done.46 = bf16[2,1312,128]{2,1,0:T(8,128)(2,1)S(1)} collective-permute-done((bf16[2,1312,128]{2,1,0:T(8,128)(2,1)S(1)}, bf16[2,1312,128]{2,1,0:T(8,128)(2,1)S(1)}, u32[]{:S(2)}, u32[]{:S(2)}) %collective-permute-start.46) | collective-permute-done | bytes 671776 | tf_op jit(solution)/shard_map/ppermute | solution.py:111
  253.0 1.3 collective-permute-start.48
  256.0 5.6 %collective-permute-done.48 = bf16[2,624,128]{2,1,0:T(8,128)(2,1)S(1)} collective-permute-done((bf16[2,624,128]{2,1,0:T(8,128)(2,1)S(1)}, bf16[2,624,128]{2,1,0:T(8,128)(2,1)S(1)}, u32[]{:S(2)}, u32[]{:S(2)}) %collective-permute-start.48) | collective-permute-done | bytes 319520 | tf_op jit(solution)/shard_map/ppermute | solution.py:111
  262.5 1.5 collective-permute-done.50
  264.4 4.4 %collective-permute-done.55 = bf16[1312,128]{1,0:T(8,128)(2,1)S(1)} collective-permute-done((bf16[1312,128]{1,0:T(8,128)(2,1)S(1)}, bf16[1312,128]{1,0:T(8,128)(2,1)S(1)}, u32[]{:S(2)}, u32[]{:S(2)}) %collective-permute-start.55) | collective-permute-done | bytes 335904 | tf_op jit(solution)/shard_map/ppermute | solution.py:111
  269.2 7.9 %collective-permute-done.49 = bf16[4,624,128]{2,1,0:T(8,128)(2,1)S(1)} collective-permute-done((bf16[4,624,128]{2,1,0:T(8,128)(2,1)S(1)}, bf16[4,624,128]{2,1,0:T(8,128)(2,1)S(1)}, u32[]{:S(2)}, u32[]{:S(2)}) %collective-permute-start.49) | collective-permute-done | bytes 639008 | tf_op jit(solution)/shard_map/ppermute | solution.py:111
  277.8 1.5 collective-permute-start.52
  279.3 2.9 collective-permute-start.53
  282.2 0.9 collective-permute-start.54
  284.1 8.6 %collective-permute-done.53 = bf16[624,128]{1,0:T(8,128)(2,1)S(1)} collective-permute-done((bf16[624,128]{1,0:T(8,128)(2,1)S(1)}, bf16[624,128]{1,0:T(8,128)(2,1)S(1)}, u32[]{:S(2)}, u32[]{:S(2)}) %collective-permute-start.53) | collective-permute-done | bytes 159776 | tf_op jit(solution)/shard_map/ppermute | solution.py:111
  294.8 0.9 collective-permute-start.58
  296.7 2.0 collective-permute-start.59
  298.7 1.5 collective-permute-done.59
  300.9 2.1 collective-permute-start.60
  303.0 1.4 collective-permute-done.60
  305.2 3.6 %collective-permute-start.61 = (f32[]{:T(128)}, f32[]{:T(128)}, u32[]{:S(2)}, u32[]{:S(2)}) collective-permute-start(f32[]{:T(128)} %add.207), channel_id=1, source_target_pairs={{0,8},{1,9},{2,10},{3,11},{4,12},{5,13},{6,14},{7,15},{8,0},{9,1},... | collective-permute-start | bytes 20 | tf_op jit(solution)/shard_map/ppermute | solution.py:111
  309.6 4.9 %collective-permute-start.62 = (f32[]{:T(128)}, f32[]{:T(128)}, u32[]{:S(2)}, u32[]{:S(2)}) collective-permute-start(f32[]{:T(128)} %add.208), channel_id=1, source_target_pairs={{0,16},{1,17},{2,18},{3,19},{4,20},{5,21},{6,22},{7,23},{8,24},{9,... | collective-permute-start | bytes 20 | tf_op jit(solution)/shard_map/ppermute | solution.py:111
  315.5 3.1 multiply_add_fusion.1
  318.7 1.2 multiply_add_fusion.3
  (221 shorter events, 28.4 us)
Async XLA Ops:
  2.0 9.6 %collective-permute-start = (bf16[624,128]{1,0:T(8,128)(2,1)S(1)}, bf16[624,128]{1,0:T(8,128)(2,1)S(1)}, u32[]{:S(2)}, u32[]{:S(2)}) collective-permute-start(bf16[624,128]{1,0:T(8,128)(2,1)S(1)} %fusion.5), channel_id=1, source_target_pairs={{0,8},{1,9},{2,10},{3,11},{4,12},{5,13},{6,14},{7,15},{8,0},{9,1},... | collective-permute-start | bytes 479240 | tf_op jit(solution)/shard_map/ppermute | solution.py:111
  5.1 14.8 %collective-permute-start.1 = (bf16[624,128]{1,0:T(8,128)(2,1)S(1)}, bf16[624,128]{1,0:T(8,128)(2,1)S(1)}, u32[]{:S(2)}, u32[]{:S(2)}) collective-permute-start(bf16[624,128]{1,0:T(8,128)(2,1)S(1)} %fusion.5), channel_id=1, source_target_pairs={{0,16},{1,17},{2,18},{3,19},{4,20},{5,21},{6,22},{7,23},{8,24},{9,... | collective-permute-start | bytes 479240 | tf_op jit(solution)/shard_map/ppermute | solution.py:111
  7.7 12.2 %collective-permute-start.2 = (bf16[624,128]{1,0:T(8,128)(2,1)S(1)}, bf16[624,128]{1,0:T(8,128)(2,1)S(1)}, u32[]{:S(2)}, u32[]{:S(2)}) collective-permute-start(bf16[624,128]{1,0:T(8,128)(2,1)S(1)} %fusion.5), channel_id=1, source_target_pairs={{0,24},{1,25},{2,26},{3,27},{4,28},{5,29},{6,30},{7,31},{8,16},{9,... | collective-permute-start | bytes 479240 | tf_op jit(solution)/shard_map/ppermute | solution.py:111
  20.0 35.8 %copy-start.28 = (bf16[4,624,128]{2,1,0:T(8,128)(2,1)}, bf16[4,624,128]{2,1,0:T(8,128)(2,1)S(1)}, u32[]{:S(2)}) copy-start(bf16[4,624,128]{2,1,0:T(8,128)(2,1)S(1)} %pad_maximum_fusion.1.refs_0_) | copy-start | bytes 1916932
  20.0 13.7 %collective-permute-start.4 = (bf16[4,624,128]{2,1,0:T(8,128)(2,1)S(1)}, bf16[4,624,128]{2,1,0:T(8,128)(2,1)S(1)}, u32[]{:S(2)}, u32[]{:S(2)}) collective-permute-start(bf16[4,624,128]{2,1,0:T(8,128)(2,1)S(1)} %pad_maximum_fusion.1.refs_0_), channel_id=1, source_target_pairs={{0,4},{1,5},{2,6},{3,7},{4,0},{5,1},{6,2},{7,3},{8,12},{9,13},{10,... | collective-permute-start | bytes 1916936 | tf_op jit(solution)/shard_map/ppermute | solution.py:111
  21.6 15.4 %collective-permute-start.3 = (bf16[4,624,128]{2,1,0:T(8,128)(2,1)S(1)}, bf16[4,624,128]{2,1,0:T(8,128)(2,1)S(1)}, u32[]{:S(2)}, u32[]{:S(2)}) collective-permute-start(bf16[4,624,128]{2,1,0:T(8,128)(2,1)S(1)} %pad_maximum_fusion.1.refs_0_), channel_id=1, source_target_pairs={{0,2},{1,3},{2,0},{3,1},{4,6},{5,7},{6,4},{7,5},{8,10},{9,11},{10,... | collective-permute-start | bytes 1916936 | tf_op jit(solution)/shard_map/ppermute | solution.py:111
  23.4 14.0 %collective-permute-start.14 = (bf16[1312,128]{1,0:T(8,128)(2,1)S(1)}, bf16[1312,128]{1,0:T(8,128)(2,1)S(1)}, u32[]{:S(2)}, u32[]{:S(2)}) collective-permute-start(bf16[1312,128]{1,0:T(8,128)(2,1)S(1)} %fusion), channel_id=1, source_target_pairs={{0,24},{1,25},{2,26},{3,27},{4,28},{5,29},{6,30},{7,31},{8,16},{9,... | collective-permute-start | bytes 1007624 | tf_op jit(solution)/shard_map/ppermute | solution.py:111
  25.7 15.2 %collective-permute-start.12 = (bf16[1312,128]{1,0:T(8,128)(2,1)S(1)}, bf16[1312,128]{1,0:T(8,128)(2,1)S(1)}, u32[]{:S(2)}, u32[]{:S(2)}) collective-permute-start(bf16[1312,128]{1,0:T(8,128)(2,1)S(1)} %fusion), channel_id=1, source_target_pairs={{0,8},{1,9},{2,10},{3,11},{4,12},{5,13},{6,14},{7,15},{8,0},{9,1},... | collective-permute-start | bytes 1007624 | tf_op jit(solution)/shard_map/ppermute | solution.py:111
  27.6 25.9 %collective-permute-start.13 = (bf16[1312,128]{1,0:T(8,128)(2,1)S(1)}, bf16[1312,128]{1,0:T(8,128)(2,1)S(1)}, u32[]{:S(2)}, u32[]{:S(2)}) collective-permute-start(bf16[1312,128]{1,0:T(8,128)(2,1)S(1)} %fusion), channel_id=1, source_target_pairs={{0,16},{1,17},{2,18},{3,19},{4,20},{5,21},{6,22},{7,23},{8,24},{9,... | collective-permute-start | bytes 1007624 | tf_op jit(solution)/shard_map/ppermute | solution.py:111
  33.7 21.0 %collective-permute-start.5 = (bf16[2,624,128]{2,1,0:T(8,128)(2,1)S(1)}, bf16[2,624,128]{2,1,0:T(8,128)(2,1)S(1)}, u32[]{:S(2)}, u32[]{:S(2)}) collective-permute-start(bf16[2,624,128]{2,1,0:T(8,128)(2,1)S(1)} %slice.82), channel_id=1, source_target_pairs={{0,2},{1,3},{2,0},{3,1},{4,6},{5,7},{6,4},{7,5},{8,10},{9,11},{10,... | collective-permute-start | bytes 958472 | tf_op jit(solution)/shard_map/ppermute | solution.py:111
  37.0 17.7 %collective-permute-start.6 = (bf16[2,624,128]{2,1,0:T(8,128)(2,1)S(1)}, bf16[2,624,128]{2,1,0:T(8,128)(2,1)}, u32[]{:S(2)}, u32[]{:S(2)}) collective-permute-start(bf16[2,624,128]{2,1,0:T(8,128)(2,1)S(1)} %slice.83), channel_id=1, source_target_pairs={{0,4},{1,5},{2,6},{3,7},{4,0},{5,1},{6,2},{7,3},{8,12},{9,13},{10,... | collective-permute-start | bytes 958472 | tf_op jit(solution)/shard_map/ppermute | solution.py:111
  54.7 31.1 %collective-permute-start.15 = (bf16[4,1312,128]{2,1,0:T(8,128)(2,1)}, bf16[4,1312,128]{2,1,0:T(8,128)(2,1)}, u32[]{:S(2)}, u32[]{:S(2)}) collective-permute-start(bf16[4,1312,128]{2,1,0:T(8,128)(2,1)} %pad_maximum_fusion.refs_0_), channel_id=1, source_target_pairs={{0,2},{1,3},{2,0},{3,1},{4,6},{5,7},{6,4},{7,5},{8,10},{9,11},{10,... | collective-permute-start | bytes 4030472 | tf_op jit(solution)/shard_map/ppermute | solution.py:111
  55.3 30.8 %collective-permute-start.16 = (bf16[4,1312,128]{2,1,0:T(8,128)(2,1)}, bf16[4,1312,128]{2,1,0:T(8,128)(2,1)}, u32[]{:S(2)}, u32[]{:S(2)}) collective-permute-start(bf16[4,1312,128]{2,1,0:T(8,128)(2,1)} %pad_maximum_fusion.refs_0_), channel_id=1, source_target_pairs={{0,4},{1,5},{2,6},{3,7},{4,0},{5,1},{6,2},{7,3},{8,12},{9,13},{10,... | collective-permute-start | bytes 4030472 | tf_op jit(solution)/shard_map/ppermute | solution.py:111
  55.8 2.1 collective-permute-start.7
  55.8 3.9 %collective-permute-start.8 = (bf16[4,624,128]{2,1,0:T(8,128)(2,1)S(1)}, bf16[4,624,128]{2,1,0:T(8,128)(2,1)S(1)}, u32[]{:S(2)}, u32[]{:S(2)}) collective-permute-start(bf16[4,624,128]{2,1,0:T(8,128)(2,1)S(1)} %collective-permute-done.3.refs_1_), channel_id=1, source_target_pairs={{0,1},{1,0},{2,3},{3,2},{4,5},{5,4},{6,7},{7,6},{8,9},{9,8},{10,11... | collective-permute-start | bytes 1916936 | tf_op jit(solution)/shard_map/ppermute | solution.py:111
  56.3 4.3 %collective-permute-start.9 = (bf16[4,624,128]{2,1,0:T(8,128)(2,1)S(1)}, bf16[4,624,128]{2,1,0:T(8,128)(2,1)}, u32[]{:S(2)}, u32[]{:S(2)}) collective-permute-start(bf16[4,624,128]{2,1,0:T(8,128)(2,1)S(1)} %collective-permute-done.4.refs_2_), channel_id=1, source_target_pairs={{0,1},{1,0},{2,3},{3,2},{4,5},{5,4},{6,7},{7,6},{8,9},{9,8},{10,11... | collective-permute-start | bytes 1916936 | tf_op jit(solution)/shard_map/ppermute | solution.py:111
  57.9 3.1 collective-permute-start.10
  59.7 1.8 collective-permute-start.11
  60.6 49.6 %collective-permute-start.19 = (bf16[4,1312,128]{2,1,0:T(8,128)(2,1)}, bf16[4,1312,128]{2,1,0:T(8,128)(2,1)}, u32[]{:S(2)}, u32[]{:S(2)}) collective-permute-start(bf16[4,1312,128]{2,1,0:T(8,128)(2,1)} %pad_maximum_fusion.refs_0_), channel_id=1, source_target_pairs={{0,1},{1,0},{2,3},{3,2},{4,5},{5,4},{6,7},{7,6},{8,9},{9,8},{10,11... | collective-permute-start | bytes 4030472 | tf_op jit(solution)/shard_map/ppermute | solution.py:111
  87.2 23.0 %collective-permute-start.20 = (bf16[4,1312,128]{2,1,0:T(8,128)(2,1)}, bf16[4,1312,128]{2,1,0:T(8,128)(2,1)}, u32[]{:S(2)}, u32[]{:S(2)}) collective-permute-start(bf16[4,1312,128]{2,1,0:T(8,128)(2,1)} %collective-permute-done.15.refs_1_), channel_id=1, source_target_pairs={{0,1},{1,0},{2,3},{3,2},{4,5},{5,4},{6,7},{7,6},{8,9},{9,8},{10,11... | collective-permute-start | bytes 4030472 | tf_op jit(solution)/shard_map/ppermute | solution.py:111
  88.4 17.5 %collective-permute-start.17 = (bf16[2,1312,128]{2,1,0:T(8,128)(2,1)S(1)}, bf16[2,1312,128]{2,1,0:T(8,128)(2,1)S(1)}, u32[]{:S(2)}, u32[]{:S(2)}) collective-permute-start(bf16[2,1312,128]{2,1,0:T(8,128)(2,1)S(1)} %slice.64), channel_id=1, source_target_pairs={{0,2},{1,3},{2,0},{3,1},{4,6},{5,7},{6,4},{7,5},{8,10},{9,11},{10,... | collective-permute-start | bytes 2015240 | tf_op jit(solution)/shard_map/ppermute | solution.py:111
  90.0 20.3 %collective-permute-start.21 = (bf16[4,1312,128]{2,1,0:T(8,128)(2,1)}, bf16[4,1312,128]{2,1,0:T(8,128)(2,1)}, u32[]{:S(2)}, u32[]{:S(2)}) collective-permute-start(bf16[4,1312,128]{2,1,0:T(8,128)(2,1)} %collective-permute-done.16.refs_2_), channel_id=1, source_target_pairs={{0,1},{1,0},{2,3},{3,2},{4,5},{5,4},{6,7},{7,6},{8,9},{9,8},{10,11... | collective-permute-start | bytes 4030472 | tf_op jit(solution)/shard_map/ppermute | solution.py:111
  90.2 17.3 %collective-permute-start.18 = (bf16[2,1312,128]{2,1,0:T(8,128)(2,1)S(1)}, bf16[2,1312,128]{2,1,0:T(8,128)(2,1)S(1)}, u32[]{:S(2)}, u32[]{:S(2)}) collective-permute-start(bf16[2,1312,128]{2,1,0:T(8,128)(2,1)S(1)} %slice.65), channel_id=1, source_target_pairs={{0,4},{1,5},{2,6},{3,7},{4,0},{5,1},{6,2},{7,3},{8,12},{9,13},{10,... | collective-permute-start | bytes 2015240 | tf_op jit(solution)/shard_map/ppermute | solution.py:111
  106.0 4.3 %collective-permute-start.22 = (bf16[2,1312,128]{2,1,0:T(8,128)(2,1)S(1)}, bf16[2,1312,128]{2,1,0:T(8,128)(2,1)}, u32[]{:S(2)}, u32[]{:S(2)}) collective-permute-start(bf16[2,1312,128]{2,1,0:T(8,128)(2,1)S(1)} %collective-permute-done.17.refs_3_), channel_id=1, source_target_pairs={{0,1},{1,0},{2,3},{3,2},{4,5},{5,4},{6,7},{7,6},{8,9},{9,8},{10,11... | collective-permute-start | bytes 2015240 | tf_op jit(solution)/shard_map/ppermute | solution.py:111
  107.5 2.8 collective-permute-start.23
  121.9 17.9 %collective-permute-start.27 = (f32[16,5376]{1,0:T(8,128)S(1)}, f32[16,5376]{1,0:T(8,128)S(1)}, u32[]{:S(2)}, u32[]{:S(2)}) collective-permute-start(f32[16,5376]{1,0:T(8,128)S(1)} %get-tuple-element.131.cls_own), channel_id=1, source_target_pairs={{0,1},{1,0},{2,3},{3,2},{4,5},{5,4},{6,7},{7,6},{8,9},{9,8},{10,11... | collective-permute-start | bytes 1032200 | tf_op jit(solution)/shard_map/ppermute | solution.py:111
  122.5 17.3 %collective-permute-start.24 = (bf16[16,768]{1,0:T(8,128)(2,1)S(1)}, bf16[16,768]{1,0:T(8,128)(2,1)S(1)}, u32[]{:S(2)}, u32[]{:S(2)}) collective-permute-start(bf16[16,768]{1,0:T(8,128)(2,1)S(1)} %get-tuple-element.138), channel_id=1, source_target_pairs={{0,8},{1,9},{2,10},{3,11},{4,12},{5,13},{6,14},{7,15},{8,0},{9,1},... | collective-permute-start | bytes 73736 | tf_op jit(solution)/shard_map/ppermute | solution.py:111
  122.5 17.2 %collective-permute-start.25 = (bf16[16,768]{1,0:T(8,128)(2,1)S(1)}, bf16[16,768]{1,0:T(8,128)(2,1)S(1)}, u32[]{:S(2)}, u32[]{:S(2)}) collective-permute-start(bf16[16,768]{1,0:T(8,128)(2,1)S(1)} %get-tuple-element.138), channel_id=1, source_target_pairs={{0,16},{1,17},{2,18},{3,19},{4,20},{5,21},{6,22},{7,23},{8,24},{9,... | collective-permute-start | bytes 73736 | tf_op jit(solution)/shard_map/ppermute | solution.py:111
  126.9 12.9 %collective-permute-start.26 = (bf16[16,768]{1,0:T(8,128)(2,1)S(1)}, bf16[16,768]{1,0:T(8,128)(2,1)S(1)}, u32[]{:S(2)}, u32[]{:S(2)}) collective-permute-start(bf16[16,768]{1,0:T(8,128)(2,1)S(1)} %get-tuple-element.138), channel_id=1, source_target_pairs={{0,24},{1,25},{2,26},{3,27},{4,28},{5,29},{6,30},{7,31},{8,16},{9,... | collective-permute-start | bytes 73736 | tf_op jit(solution)/shard_map/ppermute | solution.py:111
  139.8 15.0 %collective-permute-start.32 = (bf16[512,3072]{1,0:T(8,128)(2,1)S(1)}, bf16[512,3072]{1,0:T(8,128)(2,1)S(1)}, u32[]{:S(2)}, u32[]{:S(2)}) collective-permute-start(bf16[512,3072]{1,0:T(8,128)(2,1)S(1)} %get-tuple-element.142.refs_6_), channel_id=1, source_target_pairs={{0,1},{1,0},{2,3},{3,2},{4,5},{5,4},{6,7},{7,6},{8,9},{9,8},{10,11... | collective-permute-start | bytes 9437192 | tf_op jit(solution)/shard_map/ppermute | solution.py:111
  139.9 14.9 %collective-permute-start.33 = (bf16[512,768]{1,0:T(8,128)(2,1)S(1)}, bf16[512,768]{1,0:T(8,128)(2,1)S(1)}, u32[]{:S(2)}, u32[]{:S(2)}) collective-permute-start(bf16[512,768]{1,0:T(8,128)(2,1)S(1)} %get-tuple-element.132.down_ref.refs_4_), channel_id=1, source_target_pairs={{0,1},{1,0},{2,3},{3,2},{4,5},{5,4},{6,7},{7,6},{8,9},{9,8},{10,11... | collective-permute-start | bytes 2359304 | tf_op jit(solution)/shard_map/ppermute | solution.py:111
  140.4 14.4 %collective-permute-start.29 = (bf16[4,16,768]{2,1,0:T(8,128)(2,1)S(1)}, bf16[4,16,768]{2,1,0:T(8,128)(2,1)S(1)}, u32[]{:S(2)}, u32[]{:S(2)}) collective-permute-start(bf16[4,16,768]{2,1,0:T(8,128)(2,1)S(1)} %pad_maximum_fusion.5), channel_id=1, source_target_pairs={{0,2},{1,3},{2,0},{3,1},{4,6},{5,7},{6,4},{7,5},{8,10},{9,11},{10,... | collective-permute-start | bytes 294920 | tf_op jit(solution)/shard_map/ppermute | solution.py:111
  141.2 13.7 %collective-permute-start.30 = (bf16[4,16,768]{2,1,0:T(8,128)(2,1)S(1)}, bf16[4,16,768]{2,1,0:T(8,128)(2,1)S(1)}, u32[]{:S(2)}, u32[]{:S(2)}) collective-permute-start(bf16[4,16,768]{2,1,0:T(8,128)(2,1)S(1)} %pad_maximum_fusion.5), channel_id=1, source_target_pairs={{0,4},{1,5},{2,6},{3,7},{4,0},{5,1},{6,2},{7,3},{8,12},{9,13},{10,... | collective-permute-start | bytes 294920 | tf_op jit(solution)/shard_map/ppermute | solution.py:111
  141.9 12.9 %collective-permute-start.31 = (bf16[4,16,768]{2,1,0:T(8,128)(2,1)S(1)}, bf16[4,16,768]{2,1,0:T(8,128)(2,1)S(1)}, u32[]{:S(2)}, u32[]{:S(2)}) collective-permute-start(bf16[4,16,768]{2,1,0:T(8,128)(2,1)S(1)} %pad_maximum_fusion.5), channel_id=1, source_target_pairs={{0,6},{1,7},{2,4},{3,5},{4,2},{5,3},{6,0},{7,1},{8,14},{9,15},{10,... | collective-permute-start | bytes 294920 | tf_op jit(solution)/shard_map/ppermute | solution.py:111
  154.9 1.8 collective-permute-start.34
  156.7 15.5 %collective-permute-start.35 = (bf16[512,3072]{1,0:T(8,128)(2,1)}, bf16[512,3072]{1,0:T(8,128)(2,1)}, u32[]{:S(2)}, u32[]{:S(2)}) collective-permute-start(bf16[512,3072]{1,0:T(8,128)(2,1)} %get-tuple-element.148.refs_2_), channel_id=1, source_target_pairs={{0,1},{1,0},{2,3},{3,2},{4,5},{5,4},{6,7},{7,6},{8,9},{9,8},{10,11... | collective-permute-start | bytes 9437192 | tf_op jit(solution)/shard_map/ppermute | solution.py:111
  156.9 15.3 %collective-permute-start.28 = (bf16[512,768]{1,0:T(8,128)(2,1)S(1)}, bf16[512,768]{1,0:T(8,128)(2,1)}, u32[]{:S(2)}, u32[]{:S(2)}) collective-permute-start(bf16[512,768]{1,0:T(8,128)(2,1)S(1)} %copy-done.2), channel_id=1, source_target_pairs={{0,1},{1,0},{2,3},{3,2},{4,5},{5,4},{6,7},{7,6},{8,9},{9,8},{10,11... | collective-permute-start | bytes 2359304 | tf_op jit(solution)/shard_map/ppermute | solution.py:111
  160.1 12.1 %collective-permute-start.36 = (f32[8,768]{1,0:T(8,128)S(1)}, f32[8,768]{1,0:T(8,128)S(1)}, u32[]{:S(2)}, u32[]{:S(2)}) collective-permute-start(f32[8,768]{1,0:T(8,128)S(1)} %get-tuple-element.155.refs_11_), channel_id=1, source_target_pairs={{0,1},{1,0},{2,3},{3,2},{4,5},{5,4},{6,7},{7,6},{8,9},{9,8},{10,11... | collective-permute-start | bytes 73736 | tf_op jit(solution)/shard_map/ppermute | solution.py:111
  189.7 17.7 %collective-permute-start.37 = (bf16[2,1312,128]{2,1,0:T(8,128)(2,1)S(1)}, bf16[2,1312,128]{2,1,0:T(8,128)(2,1)S(1)}, u32[]{:S(2)}, u32[]{:S(2)}) collective-permute-start(bf16[2,1312,128]{2,1,0:T(8,128)(2,1)S(1)} %get-tuple-element.174), channel_id=1, source_target_pairs={{0,2},{1,3},{2,0},{3,1},{4,6},{5,7},{6,4},{7,5},{8,10},{9,11},{10,... | collective-permute-start | bytes 2015240 | tf_op jit(solution)/shard_map/ppermute | solution.py:111
  190.3 17.9 %collective-permute-start.38 = (bf16[2,1312,128]{2,1,0:T(8,128)(2,1)S(1)}, bf16[2,1312,128]{2,1,0:T(8,128)(2,1)S(1)}, u32[]{:S(2)}, u32[]{:S(2)}) collective-permute-start(bf16[2,1312,128]{2,1,0:T(8,128)(2,1)S(1)} %get-tuple-element.175), channel_id=1, source_target_pairs={{0,4},{1,5},{2,6},{3,7},{4,0},{5,1},{6,2},{7,3},{8,12},{9,13},{10,... | collective-permute-start | bytes 2015240 | tf_op jit(solution)/shard_map/ppermute | solution.py:111
  191.1 40.4 %collective-permute-start.40 = (bf16[2,1312,128]{2,1,0:T(8,128)(2,1)}, bf16[2,1312,128]{2,1,0:T(8,128)(2,1)S(1)}, u32[]{:S(2)}, u32[]{:S(2)}) collective-permute-start(bf16[2,1312,128]{2,1,0:T(8,128)(2,1)} %get-tuple-element.199), channel_id=1, source_target_pairs={{0,4},{1,5},{2,6},{3,7},{4,0},{5,1},{6,2},{7,3},{8,12},{9,13},{10,... | collective-permute-start | bytes 2015240 | tf_op jit(solution)/shard_map/ppermute | solution.py:111
  209.2 22.2 %collective-permute-start.39 = (bf16[2,1312,128]{2,1,0:T(8,128)(2,1)}, bf16[2,1312,128]{2,1,0:T(8,128)(2,1)}, u32[]{:S(2)}, u32[]{:S(2)}) collective-permute-start(bf16[2,1312,128]{2,1,0:T(8,128)(2,1)} %add_convert_fusion.3), channel_id=1, source_target_pairs={{0,2},{1,3},{2,0},{3,1},{4,6},{5,7},{6,4},{7,5},{8,10},{9,11},{10,... | collective-permute-start | bytes 2015240 | tf_op jit(solution)/shard_map/ppermute | solution.py:111
  231.7 16.0 %collective-permute-start.47 = (bf16[2,1312,128]{2,1,0:T(8,128)(2,1)S(1)}, bf16[2,1312,128]{2,1,0:T(8,128)(2,1)S(1)}, u32[]{:S(2)}, u32[]{:S(2)}) collective-permute-start(bf16[2,1312,128]{2,1,0:T(8,128)(2,1)S(1)} %add_convert_fusion.2), channel_id=1, source_target_pairs={{0,4},{1,5},{2,6},{3,7},{4,0},{5,1},{6,2},{7,3},{8,12},{9,13},{10,... | collective-permute-start | bytes 2015240 | tf_op jit(solution)/shard_map/ppermute | solution.py:111
  232.5 2.5 collective-permute-start.45
  232.5 2.6 collective-permute-start.44
  233.0 3.7 %collective-permute-start.43 = (bf16[4,624,128]{2,1,0:T(8,128)(2,1)S(1)}, bf16[4,624,128]{2,1,0:T(8,128)(2,1)S(1)}, u32[]{:S(2)}, u32[]{:S(2)}) collective-permute-start(bf16[4,624,128]{2,1,0:T(8,128)(2,1)S(1)} %get-tuple-element.205), channel_id=1, source_target_pairs={{0,1},{1,0},{2,3},{3,2},{4,5},{5,4},{6,7},{7,6},{8,9},{9,8},{10,11... | collective-permute-start | bytes 1916936 | tf_op jit(solution)/shard_map/ppermute | solution.py:111
  233.0 5.4 %collective-permute-start.42 = (bf16[4,624,128]{2,1,0:T(8,128)(2,1)S(1)}, bf16[4,624,128]{2,1,0:T(8,128)(2,1)S(1)}, u32[]{:S(2)}, u32[]{:S(2)}) collective-permute-start(bf16[4,624,128]{2,1,0:T(8,128)(2,1)S(1)} %get-tuple-element.203), channel_id=1, source_target_pairs={{0,1},{1,0},{2,3},{3,2},{4,5},{5,4},{6,7},{7,6},{8,9},{9,8},{10,11... | collective-permute-start | bytes 1916936 | tf_op jit(solution)/shard_map/ppermute | solution.py:111
  235.0 6.1 %collective-permute-start.41 = (bf16[4,624,128]{2,1,0:T(8,128)(2,1)S(1)}, bf16[4,624,128]{2,1,0:T(8,128)(2,1)S(1)}, u32[]{:S(2)}, u32[]{:S(2)}) collective-permute-start(bf16[4,624,128]{2,1,0:T(8,128)(2,1)S(1)} %get-tuple-element.201), channel_id=1, source_target_pairs={{0,1},{1,0},{2,3},{3,2},{4,5},{5,4},{6,7},{7,6},{8,9},{9,8},{10,11... | collective-permute-start | bytes 1916936 | tf_op jit(solution)/shard_map/ppermute | solution.py:111
  236.0 17.0 %collective-permute-start.46 = (bf16[2,1312,128]{2,1,0:T(8,128)(2,1)S(1)}, bf16[2,1312,128]{2,1,0:T(8,128)(2,1)S(1)}, u32[]{:S(2)}, u32[]{:S(2)}) collective-permute-start(bf16[2,1312,128]{2,1,0:T(8,128)(2,1)S(1)} %copy-done.24), channel_id=1, source_target_pairs={{0,2},{1,3},{2,0},{3,1},{4,6},{5,7},{6,4},{7,5},{8,10},{9,11},{10,... | collective-permute-start | bytes 2015240 | tf_op jit(solution)/shard_map/ppermute | solution.py:111
  236.8 27.7 %collective-permute-start.56 = (bf16[1312,128]{1,0:T(8,128)(2,1)S(1)}, bf16[1312,128]{1,0:T(8,128)(2,1)S(1)}, u32[]{:S(2)}, u32[]{:S(2)}) collective-permute-start(bf16[1312,128]{1,0:T(8,128)(2,1)S(1)} %get-tuple-element.240), channel_id=1, source_target_pairs={{0,16},{1,17},{2,18},{3,19},{4,20},{5,21},{6,22},{7,23},{8,24},{9,... | collective-permute-start | bytes 1007624 | tf_op jit(solution)/shard_map/ppermute | solution.py:111
  238.4 26.0 %collective-permute-start.57 = (bf16[1312,128]{1,0:T(8,128)(2,1)S(1)}, bf16[1312,128]{1,0:T(8,128)(2,1)S(1)}, u32[]{:S(2)}, u32[]{:S(2)}) collective-permute-start(bf16[1312,128]{1,0:T(8,128)(2,1)S(1)} %get-tuple-element.241), channel_id=1, source_target_pairs={{0,24},{1,25},{2,26},{3,27},{4,28},{5,29},{6,30},{7,31},{8,16},{9,... | collective-permute-start | bytes 1007624 | tf_op jit(solution)/shard_map/ppermute | solution.py:111
  253.0 8.6 %collective-permute-start.48 = (bf16[2,624,128]{2,1,0:T(8,128)(2,1)S(1)}, bf16[2,624,128]{2,1,0:T(8,128)(2,1)S(1)}, u32[]{:S(2)}, u32[]{:S(2)}) collective-permute-start(bf16[2,624,128]{2,1,0:T(8,128)(2,1)S(1)} %add_convert_fusion.10), channel_id=1, source_target_pairs={{0,4},{1,5},{2,6},{3,7},{4,0},{5,1},{6,2},{7,3},{8,12},{9,13},{10,... | collective-permute-start | bytes 958472 | tf_op jit(solution)/shard_map/ppermute | solution.py:111
  254.6 14.3 %collective-permute-start.55 = (bf16[1312,128]{1,0:T(8,128)(2,1)S(1)}, bf16[1312,128]{1,0:T(8,128)(2,1)S(1)}, u32[]{:S(2)}, u32[]{:S(2)}) collective-permute-start(bf16[1312,128]{1,0:T(8,128)(2,1)S(1)} %get-tuple-element.238), channel_id=1, source_target_pairs={{0,8},{1,9},{2,10},{3,11},{4,12},{5,13},{6,14},{7,15},{8,0},{9,1},... | collective-permute-start | bytes 1007624 | tf_op jit(solution)/shard_map/ppermute | solution.py:111
  255.2 8.7 %collective-permute-start.50 = (bf16[2,624,128]{2,1,0:T(8,128)(2,1)S(1)}, bf16[2,624,128]{2,1,0:T(8,128)(2,1)S(1)}, u32[]{:S(2)}, u32[]{:S(2)}) collective-permute-start(bf16[2,624,128]{2,1,0:T(8,128)(2,1)S(1)} %add_convert_fusion.11), channel_id=1, source_target_pairs={{0,2},{1,3},{2,0},{3,1},{4,6},{5,7},{6,4},{7,5},{8,10},{9,11},{10,... | collective-permute-start | bytes 958472 | tf_op jit(solution)/shard_map/ppermute | solution.py:111
  261.7 15.3 %collective-permute-start.49 = (bf16[4,624,128]{2,1,0:T(8,128)(2,1)S(1)}, bf16[4,624,128]{2,1,0:T(8,128)(2,1)S(1)}, u32[]{:S(2)}, u32[]{:S(2)}) collective-permute-start(bf16[4,624,128]{2,1,0:T(8,128)(2,1)S(1)} %pad_maximum_fusion.2), channel_id=1, source_target_pairs={{0,2},{1,3},{2,0},{3,1},{4,6},{5,7},{6,4},{7,5},{8,10},{9,11},{10,... | collective-permute-start | bytes 1916936 | tf_op jit(solution)/shard_map/ppermute | solution.py:111
  264.1 13.4 %collective-permute-start.51 = (bf16[4,624,128]{2,1,0:T(8,128)(2,1)S(1)}, bf16[4,624,128]{2,1,0:T(8,128)(2,1)S(1)}, u32[]{:S(2)}, u32[]{:S(2)}) collective-permute-start(bf16[4,624,128]{2,1,0:T(8,128)(2,1)S(1)} %pad_maximum_fusion.3), channel_id=1, source_target_pairs={{0,4},{1,5},{2,6},{3,7},{4,0},{5,1},{6,2},{7,3},{8,12},{9,13},{10,... | collective-permute-start | bytes 1916936 | tf_op jit(solution)/shard_map/ppermute | solution.py:111
  277.8 6.3 %collective-permute-start.52 = (bf16[624,128]{1,0:T(8,128)(2,1)S(1)}, bf16[624,128]{1,0:T(8,128)(2,1)S(1)}, u32[]{:S(2)}, u32[]{:S(2)}) collective-permute-start(bf16[624,128]{1,0:T(8,128)(2,1)S(1)} %get-tuple-element.242), channel_id=1, source_target_pairs={{0,8},{1,9},{2,10},{3,11},{4,12},{5,13},{6,14},{7,15},{8,0},{9,1},... | collective-permute-start | bytes 479240 | tf_op jit(solution)/shard_map/ppermute | solution.py:111
  279.3 13.3 %collective-permute-start.53 = (bf16[624,128]{1,0:T(8,128)(2,1)S(1)}, bf16[624,128]{1,0:T(8,128)(2,1)S(1)}, u32[]{:S(2)}, u32[]{:S(2)}) collective-permute-start(bf16[624,128]{1,0:T(8,128)(2,1)S(1)} %get-tuple-element.244), channel_id=1, source_target_pairs={{0,16},{1,17},{2,18},{3,19},{4,20},{5,21},{6,22},{7,23},{8,24},{9,... | collective-permute-start | bytes 479240 | tf_op jit(solution)/shard_map/ppermute | solution.py:111
  282.2 10.4 %collective-permute-start.54 = (bf16[624,128]{1,0:T(8,128)(2,1)S(1)}, bf16[624,128]{1,0:T(8,128)(2,1)S(1)}, u32[]{:S(2)}, u32[]{:S(2)}) collective-permute-start(bf16[624,128]{1,0:T(8,128)(2,1)S(1)} %get-tuple-element.243), channel_id=1, source_target_pairs={{0,24},{1,25},{2,26},{3,27},{4,28},{5,29},{6,30},{7,31},{8,16},{9,... | collective-permute-start | bytes 479240 | tf_op jit(solution)/shard_map/ppermute | solution.py:111
  294.8 1.2 collective-permute-start.58
  296.7 3.6 %collective-permute-start.59 = (f32[]{:T(128)}, f32[]{:T(128)}, u32[]{:S(2)}, u32[]{:S(2)}) collective-permute-start(f32[]{:T(128)} %add.205), channel_id=1, source_target_pairs={{0,2},{1,3},{2,0},{3,1},{4,6},{5,7},{6,4},{7,5},{8,10},{9,11},{10,... | collective-permute-start | bytes 20 | tf_op jit(solution)/shard_map/ppermute | solution.py:111
  300.9 3.6 %collective-permute-start.60 = (f32[]{:T(128)}, f32[]{:T(128)}, u32[]{:S(2)}, u32[]{:S(2)}) collective-permute-start(f32[]{:T(128)} %add.206), channel_id=1, source_target_pairs={{0,4},{1,5},{2,6},{3,7},{4,0},{5,1},{6,2},{7,3},{8,12},{9,13},{10,... | collective-permute-start | bytes 20 | tf_op jit(solution)/shard_map/ppermute | solution.py:111
  305.2 3.8 %collective-permute-start.61 = (f32[]{:T(128)}, f32[]{:T(128)}, u32[]{:S(2)}, u32[]{:S(2)}) collective-permute-start(f32[]{:T(128)} %add.207), channel_id=1, source_target_pairs={{0,8},{1,9},{2,10},{3,11},{4,12},{5,13},{6,14},{7,15},{8,0},{9,1},... | collective-permute-start | bytes 20 | tf_op jit(solution)/shard_map/ppermute | solution.py:111
  309.6 5.0 %collective-permute-start.62 = (f32[]{:T(128)}, f32[]{:T(128)}, u32[]{:S(2)}, u32[]{:S(2)}) collective-permute-start(f32[]{:T(128)} %add.208), channel_id=1, source_target_pairs={{0,16},{1,17},{2,18},{3,19},{4,20},{5,21},{6,22},{7,23},{8,24},{9,... | collective-permute-start | bytes 20 | tf_op jit(solution)/shard_map/ppermute | solution.py:111
  (48 other events, 478.6 us)
where the time goes:
time: 326 us; the launch traced here: 322 us
  Pallas kernels  113 us (35%)
  waiting for transfers between devices  107 us (33%)
  starting transfers between devices  62.9 us (19%)
  other arithmetic  15.7 us (5%)
  between operations  14.2 us (4%)
  local copies, waits for them, and re-layouts  9.93 us (3%)
    ppermute x63, waiting for transfers between devices, swap(): return lax.ppermute(value, 'sent', [(i, i ^ bit) for i in range(count)])  107 us
    ppermute x63, starting transfers between devices, swap(): return lax.ppermute(value, 'sent', [(i, i ^ bit) for i in range(count)])  62.9 us
    pallas_call x1, Pallas kernels, attn_forward(): pl.pallas_call(functools.partial(attn_kernel, shard), out_shape=tuple((ja...  20.3 us
    pallas_call x1, Pallas kernels, attn_grads(): pl.pallas_call(functools.partial(attn_grad_kernel, shard), out_shape=(jax...  18.8 us
    pallas_call x1, Pallas kernels, head_grads(): pl.pallas_call(functools.partial(head_grad_kernel, shard), out_shape=tupl...  16.6 us
    pallas_call x1, Pallas kernels, head_forward(): pl.pallas_call(forward_kernel, out_shape=(result((both, 4 * D), low, True...  12.8 us
    pallas_call x1, Pallas kernels, make_head(): pl.pallas_call(functools.partial(head_kernel, shard), out_shape=(result((...  11.6 us
    pallas_call x1, Pallas kernels, head_backward(): pl.pallas_call(backward_kernel, out_shape=(result((both, 4 * D), low, Tru...  9.64 us
  transfers between devices with their start and end apart: 63, of which 30 were waited for; matrix products, arithmetic and copies ran while one was open for 4% of the time, Pallas kernels for 26%

commit v1 on v0

--- a/solution.py
+++ b/solution.py
@@ -181,8 +181,8 @@
     return [block] + [swap(block, bit) for bit in ZBITS]
 
 
-def gather_head(line, x, y):
-    return with_sibling((line, x, y, swap(y[:2], XBIT), swap(x[2:], YBIT)))
+def gather_head(low, high, x_low, x_high, y_low, y_high):
+    return with_sibling((low, high, x_low, x_high, y_low, y_high, swap(y_low, XBIT), swap(x_high, YBIT)))
 
 
 def low_sum(*terms):
@@ -583,7 +583,7 @@
     vmem = pl.BlockSpec(memory_space=pltpu.VMEM)
     return pl.pallas_call(
         attn_back_kernel,
-        out_shape=(result(qkv.shape, jnp.bfloat16, True), result((8, D), jnp.float32)),
+        out_shape=(result(qkv.shape, jnp.bfloat16, True), pltpu.HBM((8, D), jnp.float32)),
         in_specs=[vmem] * 3,
         out_specs=(vmem,) * 2,
         compiler_params=room(16),
@@ -667,7 +667,7 @@
     return pl.pallas_call(
         functools.partial(attn_grad_kernel, shard),
         out_shape=(jax.ShapeDtypeStruct((tokens, D), f32),)
-        + tuple(jax.ShapeDtypeStruct((n, rows, LANES), low) for n in counts),
+        + tuple(pltpu.HBM((n, rows, LANES), low) for n in counts),
         in_specs=[smem, smem, vmem] + [any_space] * 9,
         out_specs=(vmem,) + (any_space,) * len(counts),
         scratch_shapes=[
@@ -698,9 +698,9 @@
 
 
 def head_kernel(shard, me_ref, pick_ref, *refs):
-    pieces, (first_hbm, mask_hbm) = refs[:10], refs[10:12]
-    w_ref, vec_ref, unit_ref, cls_ref = refs[12:16]
-    stage, flat, first_all, picked, mask, sems, in_sems = refs[16:]
+    pieces, (first_hbm, mask_hbm) = refs[:16], refs[16:18]
+    w_ref, vec_ref, unit_ref, cls_ref = refs[18:22]
+    stage, flat, first_all, picked, mask, sems, in_sems = refs[22:]
     cols = w_ref.shape[1] // LANES
     tokens = mask.shape[1]
     loads = [pltpu.make_async_copy(first_hbm, first_all, in_sems.at[2])]
@@ -708,7 +708,7 @@
         loads.append(pltpu.make_async_copy(mask_hbm.at[view, 2], mask.at[view], in_sems.at[view]))
     for load in loads:
         load.start()
-    place_blocks(shard, WHOLE, pieces, me_ref[0], stage, flat, sems)
+    place_blocks(shard, HALVES, pieces, me_ref[0], stage, flat, sems)
     gather_matrix(flat, w_ref)
     for load in loads:
         load.wait()
@@ -891,7 +891,7 @@
         backward_kernel,
         out_shape=(
             result((both, 4 * D), low, True),
-            result((both, D), f32),
+            pltpu.HBM((both, D), f32),
             result((8, D), f32, True),
         ),
         in_specs=[vmem] * 5,
@@ -910,9 +910,9 @@
     return (wanted == lax.broadcasted_iota(jnp.int32, shape, 1)).astype(jnp.bfloat16)
 
 
-def pooled_kernel(me_ref, own_ref, sib_ref, w_hbm, cls_own, cls_sib, vrow_in, vcol_in, vec_in,
+def pooled_kernel(me_ref, own_ref, sib_ref, w_hbm, cls_own, cls_sib, valid_in, vec_in,
                   loss_ref, first_ref, out_ref, low_ref, part_ref,
-                  units, sims, back, cls, vrow_ref, vcol_ref, vec_ref, w_ref, sems, w_sems):
+                  units, sims, back, cls, valid_ref, vec_ref, w_ref, sems, w_sems):
     me = me_ref[0]
     core = me & 1
     n = units.shape[1]
@@ -923,7 +923,7 @@
                 pairs.append((ref.at[across, k], units.at[me ^ (side + 2 * across + 8 * k)]))
     place = pl.multiple_of(core * n, n)
     pairs += [(cls_own, cls.at[pl.ds(place, n)]), (cls_sib, cls.at[pl.ds(n - place, n)])]
-    pairs += [(vrow_in, vrow_ref), (vcol_in, vcol_ref), (vec_in, vec_ref)]
+    pairs += [(valid_in, valid_ref), (vec_in, vec_ref)]
     copies = bring(pairs, sems)
     w_copies = bring(
         [
@@ -939,14 +939,13 @@
     table = plain_rows(everyone, everyone, NT) * (1.0 / logit_divisor)
     row = lax.broadcasted_iota(jnp.int32, (total, total), 0)
     col = lax.broadcasted_iota(jnp.int32, (total, total), 1)
-    valid_row = vrow_ref[...] > 0
-    table = jnp.where(((col & (n - 1)) >= half) & (vcol_ref[...] > 0), table, masked_scores)
+    table = jnp.where(((col & (n - 1)) >= half) & (valid_ref[...] > 0), table, masked_scores)
     top = jnp.max(table, axis=-1, keepdims=True)
     row_lse = top + jnp.log(jnp.sum(jnp.exp(table - top), axis=-1, keepdims=True))
     diagonal = col == row + half
     positive = jnp.sum(jnp.where(diagonal, table, 0.0), axis=-1, keepdims=True)
     row_one = lax.broadcasted_iota(jnp.int32, (total, 1), 0)
-    anchors = ((row_one & (n - 1)) < half) & valid_row
+    anchors = ((row_one & (n - 1)) < half) & (positive > 0.5 * masked_scores)
     loss_ref[0, 0] = jnp.sum(jnp.where(anchors, row_lse - positive, 0.0))
     slope = (jnp.exp(table - row_lse) - jnp.where(diagonal, 1.0, 0.0)) * (1.0 / logit_divisor)
     sims[...] = jnp.where(anchors, slope, 0.0).astype(jnp.bfloat16)
@@ -983,7 +982,7 @@
 
 def pooled_backward(me, units, w_head, cls, valid, vecs):
     n = cls[0].shape[0]
-    total = valid.shape[0]
+    total = valid.shape[1]
     hbm, vmem = pl.BlockSpec(memory_space=pltpu.HBM), pl.BlockSpec(memory_space=pltpu.VMEM)
     smem = pl.BlockSpec(memory_space=pltpu.SMEM)
     f32, low = jnp.float32, jnp.bfloat16
@@ -991,27 +990,26 @@
         pooled_kernel,
         out_shape=(
             result((1, 1), f32),
-            result((n, D), f32),
+            pltpu.HBM((n, D), f32),
             result((2 * n, 5 * D), f32, True),
             result((2 * n, 2 * D), low, True),
             result((8, D), f32, True),
         ),
-        in_specs=[smem] + [hbm] * 8,
+        in_specs=[smem] + [hbm] * 7,
         out_specs=(smem,) + (vmem,) * 4,
         scratch_shapes=[
             pltpu.VMEM((32, n, D), low),
             pltpu.VMEM((total, total), low),
             pltpu.VMEM((total, D), f32),
             pltpu.VMEM((2 * n, 7 * D), f32),
-            pltpu.VMEM((total, 1), f32),
             pltpu.VMEM((1, total), f32),
             pltpu.VMEM((8, D), f32),
             pltpu.VMEM((D, 9 * D), low),
-            pltpu.SemaphoreType.DMA((37,)),
+            pltpu.SemaphoreType.DMA((36,)),
             pltpu.SemaphoreType.DMA((3,)),
         ],
         compiler_params=room(25),
-    )(jnp.reshape(me, (1,)), *units, *far(w_head), *cls, valid[:, None], valid[None, :], vecs)
+    )(jnp.reshape(me, (1,)), *far(*units, w_head, *cls, valid, vecs))
 
 
 def head_grad_kernel(shard, me_ref, pick_ref, *refs):
@@ -1091,7 +1089,7 @@
     f32, low = jnp.float32, jnp.bfloat16
     return pl.pallas_call(
         functools.partial(head_grad_kernel, shard),
-        out_shape=tuple(result((2, rows, LANES), low) for _ in HALVES),
+        out_shape=tuple(pltpu.HBM((2, rows, LANES), low) for _ in HALVES),
         in_specs=[smem] * 2 + [hbm] * 8 + [vmem] * 3 + [hbm] * 2,
         out_specs=(hbm,) * len(HALVES),
         scratch_shapes=[
@@ -1165,8 +1163,11 @@
 
     picks = picks_of(bucket_len)
     both_picks = jnp.stack([picks, picks_of(bucket_all[device ^ CORE])])
-    head_line = after(jnp.stack(head_zs), *attn_last)
-    head_x, head_y = swap(head_line, XBIT), swap(head_line, YBIT)
+    head_zs = after(head_zs, *attn_last)
+    z_low, z_high = jnp.stack(head_zs[:2]), jnp.stack(head_zs[2:])
+    y_low, x_high = swap(z_low, YBIT), swap(z_high, XBIT)
+    x_low, y_high = swap(z_low, XBIT), swap(z_high, YBIT)
+    head_xy = (x_low, x_high, y_low, y_high)
     (
         attn_mats,
         attn_vecs,
@@ -1179,8 +1180,14 @@
         first_norm,
         first_low,
     ) = attn_forward(attn_pieces, device, shards[0], bucket_len, lengths, embeddings, drop_masks)
-    head_x, head_y, first_norm = lax.optimization_barrier((head_x, head_y, first_norm))
-    head_pieces = gather_head(head_line, head_x, head_y)
+    valid_views = jnp.broadcast_to(
+        valid_everything.reshape(-1, 1, slot_count), (bucket_all.shape[0], 2, slot_count)
+    ).reshape(-1)
+    valid_row = valid_views[None, :]
+    head_xy, first_norm, valid_row, picks, both_picks = lax.optimization_barrier(
+        (head_xy, first_norm, valid_row, picks, both_picks)
+    )
+    head_pieces = gather_head(z_low, z_high, *head_xy)
     first_sib = swap(first_low, CORE)
     head_mats, head_vecs, unit_low, cls = make_head(
         head_pieces, device, shards[1], picks, first_norm, drop_masks
@@ -1203,11 +1210,8 @@
     units = jnp.stack(unit_lines)
     units_sib = swap(units, CORE)
     up_sib, parts_sib = swap(after(up_low, units_sib), CORE), swap(parts, CORE)
-    valid_views = jnp.broadcast_to(
-        valid_everything.reshape(-1, 1, slot_count), (bucket_all.shape[0], 2, slot_count)
-    ).reshape(-1)
     loss_sum, d_first_cls, cls_grads, cls_low, cls_part = pooled_backward(
-        device, (units, units_sib), head_mats, (cls, cls_sib), valid_views, head_vecs
+        device, (units, units_sib), head_mats, (cls, cls_sib), valid_row, head_vecs
     )
     head_pieces = head_grads(
         device,
@@ -1229,6 +1233,8 @@
     d_qkv, attn_parts = attn_backward(d_mixed, qkv_low, probs)
     d_qkv, d_low, d_high = lax.optimization_barrier((d_qkv, d_low, d_high))
     x_high, y_high = swap(low_sum(x_high, d_high), XBIT), swap(y_high, YBIT)
+    y_low = low_sum(y_low, d_low)
+    d_qkv, y_low = lax.optimization_barrier((d_qkv, y_low))
     input_grad, *attn_pieces = attn_grads(
         device,
         shards[0],
@@ -1244,11 +1250,11 @@
         attn_parts,
         norm_parts_in,
     )
-    attn_pieces, d_low, x_low, x_high, y_high = lax.optimization_barrier(
-        (attn_pieces, d_low, x_low, x_high, y_high)
+    attn_pieces, x_low, y_low, x_high, y_high = lax.optimization_barrier(
+        (attn_pieces, x_low, y_low, x_high, y_high)
     )
     line_high = low_sum(line_high, x_high, y_high)
-    x_low, y_low = swap(x_low, XBIT), swap(low_sum(y_low, d_low), YBIT)
+    x_low, y_low = swap(x_low, XBIT), swap(y_low, YBIT)
     attn_sums = scatter_core(attn_pieces)
     attn_sums, x_low, y_low = lax.optimization_barrier((attn_sums, x_low, y_low))
     line_low = low_sum(line_low, x_low, y_low)

time: 326 us -> 313 us (0.960)
  waiting for transfers between devices: 107 us -> 92.4 us
  starting transfers between devices: 62.9 us -> 74.7 us
  Pallas kernels: 113 us -> 104 us
  local copies, waits for them, and re-layouts: 9.93 us -> 6.23 us
    ppermute x63 -> x68, waiting for transfers between devices: 107 us -> 92.4 us  [swap(): return lax.ppermute(value, 'sent', [(i, i ^ bit) for i in range(count)])]
    ppermute x63 -> x68, starting transfers between devices: 62.9 us -> 74.7 us  [swap(): return lax.ppermute(value, 'sent', [(i, i ^ bit) for i in range(count)])]
    pallas_call x1, Pallas kernels: 18.8 us -> 12.8 us  [attn_grads(): pl.pallas_call(functools.partial(attn_grad_kernel, shard), out_shape=(jax...]
    unnamed x98 -> x108, local copies, waits for them, and re-layouts: 6.37 us -> 2.94 us
  transfers between devices with their start and end apart: 63 -> 68, of which waited for: 30 -> 29; matrix products, arithmetic and copies ran while one was open for 4% -> 5% of each run, Pallas kernels for 26% -> 26%
where the time goes in v1:
time: 313 us; the launch traced here: 309 us
  Pallas kernels  104 us (33%)
  waiting for transfers between devices  92.4 us (30%)
  starting transfers between devices  74.7 us (24%)
  other arithmetic  18 us (6%)
  between operations  13.7 us (4%)
  local copies, waits for them, and re-layouts  6.23 us (2%)
    ppermute x68, waiting for transfers between devices, swap(): return lax.ppermute(value, 'sent', [(i, i ^ bit) for i in range(count)])  92.4 us
    ppermute x68, starting transfers between devices, swap(): return lax.ppermute(value, 'sent', [(i, i ^ bit) for i in range(count)])  74.7 us
    pallas_call x1, Pallas kernels, attn_forward(): pl.pallas_call(functools.partial(attn_kernel, shard), out_shape=tuple((ja...  20.3 us
    pallas_call x1, Pallas kernels, head_grads(): pl.pallas_call(functools.partial(head_grad_kernel, shard), out_shape=tupl...  13.9 us
    pallas_call x1, Pallas kernels, attn_grads(): pl.pallas_call(functools.partial(attn_grad_kernel, shard), out_shape=(jax...  12.8 us
    pallas_call x1, Pallas kernels, head_forward(): pl.pallas_call(forward_kernel, out_shape=(result((both, 4 * D), low, True...  12.4 us
    pallas_call x1, Pallas kernels, make_head(): pl.pallas_call(functools.partial(head_kernel, shard), out_shape=(result((...  11.4 us
    pallas_call x1, Pallas kernels, head_backward(): pl.pallas_call(backward_kernel, out_shape=(result((both, 4 * D), low, Tru...  9.4 us
  transfers between devices with their start and end apart: 68, of which 29 were waited for; matrix products, arithmetic and copies ran while one was open for 5% of the time, Pallas kernels for 26%

profile of v1, /device:TPU:0, one launch (start us, length us, event | category | flops | bytes accessed | tf_op | source)
XLA Modules:
  0.0 309.3 jit_solution(4443974300602771382)
XLA Ops:
  0.7 1.2 select_bitcast_fusion.1
  2.0 3.1 collective-permute-start
  5.1 2.6 collective-permute-start.1
  7.7 3.8 %collective-permute-done = bf16[624,128]{1,0:T(8,128)(2,1)S(1)} collective-permute-done((bf16[624,128]{1,0:T(8,128)(2,1)S(1)}, bf16[624,128]{1,0:T(8,128)(2,1)S(1)}, u32[]{:S(2)}, u32[]{:S(2)}) %collective-permute-start) | collective-permute-done | bytes 159776 | tf_op jit(solution)/shard_map/ppermute | solution.py:111
  11.6 8.3 %collective-permute-done.1 = bf16[624,128]{1,0:T(8,128)(2,1)S(1)} collective-permute-done((bf16[624,128]{1,0:T(8,128)(2,1)S(1)}, bf16[624,128]{1,0:T(8,128)(2,1)S(1)}, u32[]{:S(2)}, u32[]{:S(2)}) %collective-permute-start.1) | collective-permute-done | bytes 159776 | tf_op jit(solution)/shard_map/ppermute | solution.py:111
  20.0 1.6 collective-permute-start.4
  21.6 1.5 collective-permute-start.3
  23.3 2.6 collective-permute-start.12
  26.0 1.1 collective-permute-start.13
  27.1 1.4 collective-permute-start.14
  28.4 5.2 %collective-permute-done.4.refs_2_ = bf16[4,624,128]{2,1,0:T(8,128)(2,1)S(1)} collective-permute-done((bf16[4,624,128]{2,1,0:T(8,128)(2,1)S(1)}, bf16[4,624,128]{2,1,0:T(8,128)(2,1)S(1)}, u32[]{:S(2)}, u32[]{:S(2)}) %collective-permute-start.4) | collective-permute-done | bytes 639008 | tf_op jit(solution)/shard_map/ppermute | solution.py:111
  34.5 1.5 collective-permute-start.5
  36.9 1.4 collective-permute-start.6
  43.0 9.1 %collective-permute-done.13 = bf16[1312,128]{1,0:T(8,128)(2,1)S(1)} collective-permute-done((bf16[1312,128]{1,0:T(8,128)(2,1)S(1)}, bf16[1312,128]{1,0:T(8,128)(2,1)S(1)}, u32[]{:S(2)}, u32[]{:S(2)}) %collective-permute-start.13) | collective-permute-done | bytes 335904 | tf_op jit(solution)/shard_map/ppermute | solution.py:111
  53.4 1.0 pad_maximum_fusion.1.refs_1_
  56.6 1.6 collective-permute-start.15
  58.2 1.5 collective-permute-start.17
  64.1 20.3 %shard_map.220 = (bf16[768,3072]{1,0:T(8,128)(2,1)}, f32[8,768]{1,0:T(8,128)}, f32[256,768]{1,0:T(8,128)}, bf16[512,768]{1,0:T(8,128)(2,1)}, bf16[512,2304]{1,0:...) custom-call(s32[1]{0:T(128)} %bitcast.me_ref, ...), custom_call_target="tpu_custom_call" | custom-call | tf_op jit(solution)/shard_map/pallas_call | solution.py:454
  84.7 1.3 collective-permute-done.15.refs_2_
  86.3 1.5 collective-permute-start.19
  89.0 13.6 %collective-permute-done.19.refs_6_ = bf16[2,1312,128]{2,1,0:T(8,128)(2,1)S(1)} collective-permute-done((bf16[2,1312,128]{2,1,0:T(8,128)(2,1)}, bf16[2,1312,128]{2,1,0:T(8,128)(2,1)S(1)}, u32[]{:S(2)}, u32[]{:S(2)}) %collective-permute-start.19) | collective-permute-done | bytes 671776 | tf_op jit(solution)/shard_map/ppermute | solution.py:111
  102.6 1.1 collective-permute-done.20.refs_7_
  106.9 11.4 %shard_map.221 = (bf16[768,6912]{1,0:T(8,128)(2,1)S(1)}, f32[8,768]{1,0:T(8,128)S(1)}, bf16[16,768]{1,0:T(8,128)(2,1)S(1)}, f32[16,5376]{1,0:T(8,128)S(1)}) custom-call(s32[1]{0:T(128)} %bitcast.me_ref, s32[9]{0:T(128)S(1)} %pad_add_fusion.1.pick_ref, bf16[2,1312,128]{2,1,0:T(8,128)(2,1)} %copy-done.14, bf16[2,1312,128]{2,1,0:T(8,128)(2,1)} %copy-done.13, ...), custom_call_target="tpu_custom_call" | custom-call | tf_op jit(solution)/shard_map/pallas_call | solution.py:744
  118.6 5.5 %collective-permute-start.29 = (bf16[16,768]{1,0:T(8,128)(2,1)S(1)}, bf16[16,768]{1,0:T(8,128)(2,1)S(1)}, u32[]{:S(2)}, u32[]{:S(2)}) collective-permute-start(bf16[16,768]{1,0:T(8,128)(2,1)S(1)} %get-tuple-element.155), channel_id=1, source_target_pairs={{0,8},{1,9},{2,10},{3,11},{4,12},{5,13},{6,14},{7,15},{8,0},{9,1},... | collective-permute-start | bytes 73736 | tf_op jit(solution)/shard_map/ppermute | solution.py:111
  124.1 1.7 collective-permute-start.30
  125.9 1.5 collective-permute-start.31
  127.4 1.1 copy-done.8
  128.5 12.4 %shard_map.222 = (bf16[512,3072]{1,0:T(8,128)(2,1)S(1)}, bf16[512,3072]{1,0:T(8,128)(2,1)S(1)}, bf16[2,256,768]{2,1,0:T(8,128)(2,1)}, f32[512,768]{1,0:T(8,128)S...) custom-call(bf16[512,768]{1,0:T(8,128)(2,1)S(1)} %copy-done.2, f32[512,768]{1,0:T(8,128)S(1)} %copy-done.1, ...), custom_call_target="tpu_custom_call" | custom-call | tf_op jit(solution)/shard_map/pallas_call | solution.py:843
  141.6 2.2 collective-permute-start.34
  145.3 9.4 %shard_map.223 = (bf16[512,3072]{1,0:T(8,128)(2,1)S(1)}, f32[512,768]{1,0:T(8,128)}, f32[8,768]{1,0:T(8,128)S(1)}) custom-call(bf16[512,768]{1,0:T(8,128)(2,1)S(1)} %get-tuple-element.148.down_ref.refs_4_, bf16[512,3072]{1,0:T(8,128)(2,1)S(1)} %get-tuple-element.149.slope_ref, f32[512,768]{1,0:T(8,128)S(1)} %get-tuple-element.150.d_res_ref, ...), custom_call_target="tpu_custom_call" | custom-call | tf_op jit(solution)/shard_map/pallas_call | solution.py:890
  154.9 1.7 collective-permute-done.39.sib_ref
  157.4 9.2 %shard_map.224 = (f32[1,1]{1,0:T(1,128)}, f32[16,768]{1,0:T(8,128)}, f32[32,3840]{1,0:T(8,128)S(1)}, bf16[32,1536]{1,0:T(8,128)(2,1)S(1)}, f32[8,768]{1,0:T(8,128)S(1)}) custom-call(s32[1]{0:T(128)} %bitcast.me_ref, bf16[4,4,16,768]{3,2,1,0:T(8,128)(2,1)} %copy-done.18, bf16[4,4,16,768]{3,2,1,0:T(8,128)(2,1)} %copy-done.39, bf16[768,6912]{1,0:T(8,128)(2,1)} %copy-done, ...), custom_call_target="tpu_custom_call" | custom-call | tf_op jit(solution)/shard_map/pallas_call | solution.py:989
  166.6 13.9 %shard_map.225 = (bf16[2,1312,128]{2,1,0:T(8,128)(2,1)}, bf16[2,1312,128]{2,1,0:T(8,128)(2,1)}, bf16[2,1312,128]{2,1,0:T(8,128)(2,1)}, bf16[2,1312,128]{2,1,0:T(...) custom-call(s32[1]{0:T(128)} %bitcast.me_ref, ...), custom_call_target="tpu_custom_call" | custom-call | tf_op jit(solution)/shard_map/pallas_call | solution.py:1090
  180.5 2.0 collective-permute-start.42
  183.3 1.3 collective-permute-start.45
  184.6 6.1 %shard_map.226 = (f32[512,768]{1,0:T(8,128)S(1)}, bf16[768,768]{1,0:T(8,128)(2,1)S(1)}, bf16[512,768]{1,0:T(8,128)(2,1)S(1)}, f32[8,768]{1,0:T(8,128)S(1)}) custom-call(s32[9]{0:T(128)S(1)} %pad_add_fusion.1.pick_ref, f32[512,768]{1,0:T(8,128)} %get-tuple-element.182.d_first, f32[16,768]{1,0:T(8,128)} %get-tuple-element.183.d_cls_in, ...), custom_call_target="tpu_custom_call" | custom-call | tf_op jit(solution)/shard_map/pallas_call | solution.py:529
  190.7 8.8 %shard_map.227 = (bf16[512,2304]{1,0:T(8,128)(2,1)S(1)}, f32[8,768]{1,0:T(8,128)}) custom-call(bf16[512,768]{1,0:T(8,128)(2,1)S(1)} %get-tuple-element.188.d_mixed, bf16[512,2304]{1,0:T(8,128)(2,1)S(1)} %copy-done.5, f32[4,6,256,128]{3,2,1,0:T(8,128)S(1)} %copy-done.4), custom_call_target="tpu_custom_call" | custom-call | tf_op jit(solution)/shard_map/pallas_call | solution.py:584
  199.6 1.1 collective-permute-done.43
  200.7 1.1 add_convert_fusion.2
  203.9 1.5 add_convert_fusion.3
  205.4 12.8 %shard_map.228 = (f32[256,768]{1,0:T(8,128)}, bf16[4,624,128]{2,1,0:T(8,128)(2,1)}, bf16[4,624,128]{2,1,0:T(8,128)(2,1)}, bf16[4,624,128]{2,1,0:T(8,128)(2,1)}, ...) custom-call(s32[1]{0:T(128)} %bitcast.me_ref, ...), custom_call_target="tpu_custom_call" | custom-call | tf_op jit(solution)/shard_map/pallas_call | solution.py:667
  219.4 1.5 add_convert_fusion
  221.0 2.0 collective-permute-start.51
  224.0 2.1 collective-permute-start.61
  227.7 11.0 %collective-permute-done.51 = bf16[2,1312,128]{2,1,0:T(8,128)(2,1)S(1)} collective-permute-done((bf16[2,1312,128]{2,1,0:T(8,128)(2,1)S(1)}, bf16[2,1312,128]{2,1,0:T(8,128)(2,1)S(1)}, u32[]{:S(2)}, u32[]{:S(2)}) %collective-permute-start.51) | collective-permute-done | bytes 671776 | tf_op jit(solution)/shard_map/ppermute | solution.py:111
  238.6 1.7 collective-permute-done.52
  242.0 1.1 collective-permute-start.55
  243.2 5.8 %collective-permute-done.53 = bf16[2,624,128]{2,1,0:T(8,128)(2,1)S(1)} collective-permute-done((bf16[2,624,128]{2,1,0:T(8,128)(2,1)S(1)}, bf16[2,624,128]{2,1,0:T(8,128)(2,1)S(1)}, u32[]{:S(2)}, u32[]{:S(2)}) %collective-permute-start.53) | collective-permute-done | bytes 319520 | tf_op jit(solution)/shard_map/ppermute | solution.py:111
  249.2 1.5 collective-permute-start.54
  250.8 1.4 collective-permute-start.56
  252.3 4.0 %collective-permute-done.60 = bf16[1312,128]{1,0:T(8,128)(2,1)S(1)} collective-permute-done((bf16[1312,128]{1,0:T(8,128)(2,1)S(1)}, bf16[1312,128]{1,0:T(8,128)(2,1)S(1)}, u32[]{:S(2)}, u32[]{:S(2)}) %collective-permute-start.60) | collective-permute-done | bytes 335904 | tf_op jit(solution)/shard_map/ppermute | solution.py:111
  256.6 7.5 %collective-permute-done.54 = bf16[4,624,128]{2,1,0:T(8,128)(2,1)S(1)} collective-permute-done((bf16[4,624,128]{2,1,0:T(8,128)(2,1)S(1)}, bf16[4,624,128]{2,1,0:T(8,128)(2,1)S(1)}, u32[]{:S(2)}, u32[]{:S(2)}) %collective-permute-start.54) | collective-permute-done | bytes 639008 | tf_op jit(solution)/shard_map/ppermute | solution.py:111
  264.0 1.7 collective-permute-done.56
  266.6 2.3 collective-permute-start.58
  269.0 1.5 collective-permute-start.59
  271.3 1.6 collective-permute-done.57
  272.9 6.6 %collective-permute-done.58 = bf16[624,128]{1,0:T(8,128)(2,1)S(1)} collective-permute-done((bf16[624,128]{1,0:T(8,128)(2,1)S(1)}, bf16[624,128]{1,0:T(8,128)(2,1)S(1)}, u32[]{:S(2)}, u32[]{:S(2)}) %collective-permute-start.58) | collective-permute-done | bytes 159776 | tf_op jit(solution)/shard_map/ppermute | solution.py:111
  283.6 2.7 collective-permute-start.64
  287.9 2.6 collective-permute-start.65
  290.4 1.1 collective-permute-done.65
  292.1 3.6 %collective-permute-start.66 = (f32[]{:T(128)}, f32[]{:T(128)}, u32[]{:S(2)}, u32[]{:S(2)}) collective-permute-start(f32[]{:T(128)} %add.207), channel_id=1, source_target_pairs={{0,8},{1,9},{2,10},{3,11},{4,12},{5,13},{6,14},{7,15},{8,0},{9,1},... | collective-permute-start | bytes 20 | tf_op jit(solution)/shard_map/ppermute | solution.py:111
  296.7 4.5 %collective-permute-start.67 = (f32[]{:T(128)}, f32[]{:T(128)}, u32[]{:S(2)}, u32[]{:S(2)}) collective-permute-start(f32[]{:T(128)} %add.208), channel_id=1, source_target_pairs={{0,16},{1,17},{2,18},{3,19},{4,20},{5,21},{6,22},{7,23},{8,24},{9,... | collective-permute-start | bytes 20 | tf_op jit(solution)/shard_map/ppermute | solution.py:111
  302.2 3.1 %multiply_add_fusion.1 = (f32[166080]{0:T(1024)}, f32[166080]{0:T(1024)}, f32[166080]{0:T(1024)}, f32[166080]{0:T(1024)}) fusion(f32[166080]{0:T(1024)S(1)} %copy-done.34, f32[166080]{0:T(1024)S(1)} %copy-done.16, f32[166080]{0:T(1024)S(1)} %get-tuple-element.253, f32[]{:T(128)S(6)} %min_shard_map.3, f32[166080]{0:T(1024)S(1)} %copy-done.35, f32[166080]{0:T(1024)} %param.23), kind=kLoop, calls=%fused_computation.21 | loop fusion | flops 2989440 | bytes 5978884 | tf_op jit(solution)/shard_map/add | solution.py:75
  305.4 1.2 multiply_add_fusion.3
  (239 shorter events, 32.4 us)
Async XLA Ops:
  2.0 9.6 %collective-permute-start = (bf16[624,128]{1,0:T(8,128)(2,1)S(1)}, bf16[624,128]{1,0:T(8,128)(2,1)S(1)}, u32[]{:S(2)}, u32[]{:S(2)}) collective-permute-start(bf16[624,128]{1,0:T(8,128)(2,1)S(1)} %fusion.5), channel_id=1, source_target_pairs={{0,8},{1,9},{2,10},{3,11},{4,12},{5,13},{6,14},{7,15},{8,0},{9,1},... | collective-permute-start | bytes 479240 | tf_op jit(solution)/shard_map/ppermute | solution.py:111
  5.1 14.8 %collective-permute-start.1 = (bf16[624,128]{1,0:T(8,128)(2,1)S(1)}, bf16[624,128]{1,0:T(8,128)(2,1)S(1)}, u32[]{:S(2)}, u32[]{:S(2)}) collective-permute-start(bf16[624,128]{1,0:T(8,128)(2,1)S(1)} %fusion.5), channel_id=1, source_target_pairs={{0,16},{1,17},{2,18},{3,19},{4,20},{5,21},{6,22},{7,23},{8,24},{9,... | collective-permute-start | bytes 479240 | tf_op jit(solution)/shard_map/ppermute | solution.py:111
  7.7 12.2 %collective-permute-start.2 = (bf16[624,128]{1,0:T(8,128)(2,1)S(1)}, bf16[624,128]{1,0:T(8,128)(2,1)S(1)}, u32[]{:S(2)}, u32[]{:S(2)}) collective-permute-start(bf16[624,128]{1,0:T(8,128)(2,1)S(1)} %fusion.5), channel_id=1, source_target_pairs={{0,24},{1,25},{2,26},{3,27},{4,28},{5,29},{6,30},{7,31},{8,16},{9,... | collective-permute-start | bytes 479240 | tf_op jit(solution)/shard_map/ppermute | solution.py:111
  20.0 13.7 %collective-permute-start.4 = (bf16[4,624,128]{2,1,0:T(8,128)(2,1)S(1)}, bf16[4,624,128]{2,1,0:T(8,128)(2,1)S(1)}, u32[]{:S(2)}, u32[]{:S(2)}) collective-permute-start(bf16[4,624,128]{2,1,0:T(8,128)(2,1)S(1)} %pad_maximum_fusion.2.refs_0_), channel_id=1, source_target_pairs={{0,4},{1,5},{2,6},{3,7},{4,0},{5,1},{6,2},{7,3},{8,12},{9,13},{10,... | collective-permute-start | bytes 1916936 | tf_op jit(solution)/shard_map/ppermute | solution.py:111
  21.6 14.5 %collective-permute-start.3 = (bf16[4,624,128]{2,1,0:T(8,128)(2,1)S(1)}, bf16[4,624,128]{2,1,0:T(8,128)(2,1)S(1)}, u32[]{:S(2)}, u32[]{:S(2)}) collective-permute-start(bf16[4,624,128]{2,1,0:T(8,128)(2,1)S(1)} %pad_maximum_fusion.2.refs_0_), channel_id=1, source_target_pairs={{0,2},{1,3},{2,0},{3,1},{4,6},{5,7},{6,4},{7,5},{8,10},{9,11},{10,... | collective-permute-start | bytes 1916936 | tf_op jit(solution)/shard_map/ppermute | solution.py:111
  23.3 19.6 %collective-permute-start.12 = (bf16[1312,128]{1,0:T(8,128)(2,1)S(1)}, bf16[1312,128]{1,0:T(8,128)(2,1)S(1)}, u32[]{:S(2)}, u32[]{:S(2)}) collective-permute-start(bf16[1312,128]{1,0:T(8,128)(2,1)S(1)} %fusion), channel_id=1, source_target_pairs={{0,8},{1,9},{2,10},{3,11},{4,12},{5,13},{6,14},{7,15},{8,0},{9,1},... | collective-permute-start | bytes 1007624 | tf_op jit(solution)/shard_map/ppermute | solution.py:111
  26.0 26.1 %collective-permute-start.13 = (bf16[1312,128]{1,0:T(8,128)(2,1)S(1)}, bf16[1312,128]{1,0:T(8,128)(2,1)S(1)}, u32[]{:S(2)}, u32[]{:S(2)}) collective-permute-start(bf16[1312,128]{1,0:T(8,128)(2,1)S(1)} %fusion), channel_id=1, source_target_pairs={{0,16},{1,17},{2,18},{3,19},{4,20},{5,21},{6,22},{7,23},{8,24},{9,... | collective-permute-start | bytes 1007624 | tf_op jit(solution)/shard_map/ppermute | solution.py:111
  27.1 25.0 %collective-permute-start.14 = (bf16[1312,128]{1,0:T(8,128)(2,1)S(1)}, bf16[1312,128]{1,0:T(8,128)(2,1)S(1)}, u32[]{:S(2)}, u32[]{:S(2)}) collective-permute-start(bf16[1312,128]{1,0:T(8,128)(2,1)S(1)} %fusion), channel_id=1, source_target_pairs={{0,24},{1,25},{2,26},{3,27},{4,28},{5,29},{6,30},{7,31},{8,16},{9,... | collective-permute-start | bytes 1007624 | tf_op jit(solution)/shard_map/ppermute | solution.py:111
  34.5 18.9 %collective-permute-start.5 = (bf16[2,624,128]{2,1,0:T(8,128)(2,1)}, bf16[2,624,128]{2,1,0:T(8,128)(2,1)}, u32[]{:S(2)}, u32[]{:S(2)}) collective-permute-start(bf16[2,624,128]{2,1,0:T(8,128)(2,1)} %slice.74), channel_id=1, source_target_pairs={{0,2},{1,3},{2,0},{3,1},{4,6},{5,7},{6,4},{7,5},{8,10},{9,11},{10,... | collective-permute-start | bytes 958472 | tf_op jit(solution)/shard_map/ppermute | solution.py:111
  36.9 16.5 %collective-permute-start.6 = (bf16[2,624,128]{2,1,0:T(8,128)(2,1)}, bf16[2,624,128]{2,1,0:T(8,128)(2,1)}, u32[]{:S(2)}, u32[]{:S(2)}) collective-permute-start(bf16[2,624,128]{2,1,0:T(8,128)(2,1)} %slice.75), channel_id=1, source_target_pairs={{0,4},{1,5},{2,6},{3,7},{4,0},{5,1},{6,2},{7,3},{8,12},{9,13},{10,... | collective-permute-start | bytes 958472 | tf_op jit(solution)/shard_map/ppermute | solution.py:111
  43.0 13.7 %collective-permute-start.7 = (bf16[4,624,128]{2,1,0:T(8,128)(2,1)S(1)}, bf16[4,624,128]{2,1,0:T(8,128)(2,1)}, u32[]{:S(2)}, u32[]{:S(2)}) collective-permute-start(bf16[4,624,128]{2,1,0:T(8,128)(2,1)S(1)} %pad_maximum_fusion.2.refs_0_), channel_id=1, source_target_pairs={{0,1},{1,0},{2,3},{3,2},{4,5},{5,4},{6,7},{7,6},{8,9},{9,8},{10,11... | collective-permute-start | bytes 1916936 | tf_op jit(solution)/shard_map/ppermute | solution.py:111
  52.1 6.1 %collective-permute-start.8 = (bf16[4,624,128]{2,1,0:T(8,128)(2,1)S(1)}, bf16[4,624,128]{2,1,0:T(8,128)(2,1)}, u32[]{:S(2)}, u32[]{:S(2)}) collective-permute-start(bf16[4,624,128]{2,1,0:T(8,128)(2,1)S(1)} %collective-permute-done.3.refs_1_), channel_id=1, source_target_pairs={{0,1},{1,0},{2,3},{3,2},{4,5},{5,4},{6,7},{7,6},{8,9},{9,8},{10,11... | collective-permute-start | bytes 1916936 | tf_op jit(solution)/shard_map/ppermute | solution.py:111
  52.1 7.6 %collective-permute-start.9 = (bf16[4,624,128]{2,1,0:T(8,128)(2,1)S(1)}, bf16[4,624,128]{2,1,0:T(8,128)(2,1)}, u32[]{:S(2)}, u32[]{:S(2)}) collective-permute-start(bf16[4,624,128]{2,1,0:T(8,128)(2,1)S(1)} %collective-permute-done.4.refs_2_), channel_id=1, source_target_pairs={{0,1},{1,0},{2,3},{3,2},{4,5},{5,4},{6,7},{7,6},{8,9},{9,8},{10,11... | collective-permute-start | bytes 1916936 | tf_op jit(solution)/shard_map/ppermute | solution.py:111
  54.5 30.0 %collective-permute-start.16 = (bf16[2,1312,128]{2,1,0:T(8,128)(2,1)S(1)}, bf16[2,1312,128]{2,1,0:T(8,128)(2,1)}, u32[]{:S(2)}, u32[]{:S(2)}) collective-permute-start(bf16[2,1312,128]{2,1,0:T(8,128)(2,1)S(1)} %pad_maximum_fusion.1.refs_1_), channel_id=1, source_target_pairs={{0,2},{1,3},{2,0},{3,1},{4,6},{5,7},{6,4},{7,5},{8,10},{9,11},{10,... | collective-permute-start | bytes 2015240 | tf_op jit(solution)/shard_map/ppermute | solution.py:111
  55.1 29.7 %collective-permute-start.18 = (bf16[2,1312,128]{2,1,0:T(8,128)(2,1)S(1)}, bf16[2,1312,128]{2,1,0:T(8,128)(2,1)}, u32[]{:S(2)}, u32[]{:S(2)}) collective-permute-start(bf16[2,1312,128]{2,1,0:T(8,128)(2,1)S(1)} %pad_maximum_fusion.1.refs_1_), channel_id=1, source_target_pairs={{0,4},{1,5},{2,6},{3,7},{4,0},{5,1},{6,2},{7,3},{8,12},{9,13},{10,... | collective-permute-start | bytes 2015240 | tf_op jit(solution)/shard_map/ppermute | solution.py:111
  56.6 29.4 %collective-permute-start.15 = (bf16[2,1312,128]{2,1,0:T(8,128)(2,1)S(1)}, bf16[2,1312,128]{2,1,0:T(8,128)(2,1)}, u32[]{:S(2)}, u32[]{:S(2)}) collective-permute-start(bf16[2,1312,128]{2,1,0:T(8,128)(2,1)S(1)} %pad_maximum_fusion.refs_0_), channel_id=1, source_target_pairs={{0,2},{1,3},{2,0},{3,1},{4,6},{5,7},{6,4},{7,5},{8,10},{9,11},{10,... | collective-permute-start | bytes 2015240 | tf_op jit(solution)/shard_map/ppermute | solution.py:111
  58.2 28.1 %collective-permute-start.17 = (bf16[2,1312,128]{2,1,0:T(8,128)(2,1)S(1)}, bf16[2,1312,128]{2,1,0:T(8,128)(2,1)}, u32[]{:S(2)}, u32[]{:S(2)}) collective-permute-start(bf16[2,1312,128]{2,1,0:T(8,128)(2,1)S(1)} %pad_maximum_fusion.refs_0_), channel_id=1, source_target_pairs={{0,4},{1,5},{2,6},{3,7},{4,0},{5,1},{6,2},{7,3},{8,12},{9,13},{10,... | collective-permute-start | bytes 2015240 | tf_op jit(solution)/shard_map/ppermute | solution.py:111
  63.4 25.0 %collective-permute-start.22 = (bf16[2,1312,128]{2,1,0:T(8,128)(2,1)S(1)}, bf16[2,1312,128]{2,1,0:T(8,128)(2,1)S(1)}, u32[]{:S(2)}, u32[]{:S(2)}) collective-permute-start(bf16[2,1312,128]{2,1,0:T(8,128)(2,1)S(1)} %pad_maximum_fusion.1.refs_1_), channel_id=1, source_target_pairs={{0,1},{1,0},{2,3},{3,2},{4,5},{5,4},{6,7},{7,6},{8,9},{9,8},{10,11... | collective-permute-start | bytes 2015240 | tf_op jit(solution)/shard_map/ppermute | solution.py:111
  84.5 4.4 %collective-permute-start.21 = (bf16[2,1312,128]{2,1,0:T(8,128)(2,1)S(1)}, bf16[2,1312,128]{2,1,0:T(8,128)(2,1)S(1)}, u32[]{:S(2)}, u32[]{:S(2)}) collective-permute-start(bf16[2,1312,128]{2,1,0:T(8,128)(2,1)S(1)} %pad_maximum_fusion.refs_0_), channel_id=1, source_target_pairs={{0,1},{1,0},{2,3},{3,2},{4,5},{5,4},{6,7},{7,6},{8,9},{9,8},{10,11... | collective-permute-start | bytes 2015240 | tf_op jit(solution)/shard_map/ppermute | solution.py:111
  86.3 16.2 %collective-permute-start.19 = (bf16[2,1312,128]{2,1,0:T(8,128)(2,1)}, bf16[2,1312,128]{2,1,0:T(8,128)(2,1)S(1)}, u32[]{:S(2)}, u32[]{:S(2)}) collective-permute-start(bf16[2,1312,128]{2,1,0:T(8,128)(2,1)} %collective-permute-done.17.refs_4_), channel_id=1, source_target_pairs={{0,2},{1,3},{2,0},{3,1},{4,6},{5,7},{6,4},{7,5},{8,10},{9,11},{10,... | collective-permute-start | bytes 2015240 | tf_op jit(solution)/shard_map/ppermute | solution.py:111
  87.8 15.8 %collective-permute-start.20 = (bf16[2,1312,128]{2,1,0:T(8,128)(2,1)}, bf16[2,1312,128]{2,1,0:T(8,128)(2,1)S(1)}, u32[]{:S(2)}, u32[]{:S(2)}) collective-permute-start(bf16[2,1312,128]{2,1,0:T(8,128)(2,1)} %collective-permute-done.16.refs_3_), channel_id=1, source_target_pairs={{0,4},{1,5},{2,6},{3,7},{4,0},{5,1},{6,2},{7,3},{8,12},{9,13},{10,... | collective-permute-start | bytes 2015240 | tf_op jit(solution)/shard_map/ppermute | solution.py:111
  88.3 15.3 %collective-permute-start.23 = (bf16[2,1312,128]{2,1,0:T(8,128)(2,1)}, bf16[2,1312,128]{2,1,0:T(8,128)(2,1)S(1)}, u32[]{:S(2)}, u32[]{:S(2)}) collective-permute-start(bf16[2,1312,128]{2,1,0:T(8,128)(2,1)} %collective-permute-done.15.refs_2_), channel_id=1, source_target_pairs={{0,1},{1,0},{2,3},{3,2},{4,5},{5,4},{6,7},{7,6},{8,9},{9,8},{10,11... | collective-permute-start | bytes 2015240 | tf_op jit(solution)/shard_map/ppermute | solution.py:111
  88.4 15.8 %collective-permute-start.24 = (bf16[2,1312,128]{2,1,0:T(8,128)(2,1)}, bf16[2,1312,128]{2,1,0:T(8,128)(2,1)S(1)}, u32[]{:S(2)}, u32[]{:S(2)}) collective-permute-start(bf16[2,1312,128]{2,1,0:T(8,128)(2,1)} %collective-permute-done.16.refs_3_), channel_id=1, source_target_pairs={{0,1},{1,0},{2,3},{3,2},{4,5},{5,4},{6,7},{7,6},{8,9},{9,8},{10,11... | collective-permute-start | bytes 2015240 | tf_op jit(solution)/shard_map/ppermute | solution.py:111
  88.9 15.3 %collective-permute-start.25 = (bf16[2,1312,128]{2,1,0:T(8,128)(2,1)}, bf16[2,1312,128]{2,1,0:T(8,128)(2,1)S(1)}, u32[]{:S(2)}, u32[]{:S(2)}) collective-permute-start(bf16[2,1312,128]{2,1,0:T(8,128)(2,1)} %collective-permute-done.17.refs_4_), channel_id=1, source_target_pairs={{0,1},{1,0},{2,3},{3,2},{4,5},{5,4},{6,7},{7,6},{8,9},{9,8},{10,11... | collective-permute-start | bytes 2015240 | tf_op jit(solution)/shard_map/ppermute | solution.py:111
  102.6 2.3 collective-permute-start.26
  103.7 2.2 collective-permute-start.27
  103.7 3.2 %collective-permute-start.28 = (bf16[2,1312,128]{2,1,0:T(8,128)(2,1)S(1)}, bf16[2,1312,128]{2,1,0:T(8,128)(2,1)}, u32[]{:S(2)}, u32[]{:S(2)}) collective-permute-start(bf16[2,1312,128]{2,1,0:T(8,128)(2,1)S(1)} %collective-permute-done.20.refs_7_), channel_id=1, source_target_pairs={{0,1},{1,0},{2,3},{3,2},{4,5},{5,4},{6,7},{7,6},{8,9},{9,8},{10,11... | collective-permute-start | bytes 2015240 | tf_op jit(solution)/shard_map/ppermute | solution.py:111
  118.3 22.6 %collective-permute-start.32 = (f32[16,5376]{1,0:T(8,128)S(1)}, f32[16,5376]{1,0:T(8,128)S(1)}, u32[]{:S(2)}, u32[]{:S(2)}) collective-permute-start(f32[16,5376]{1,0:T(8,128)S(1)} %get-tuple-element.147.cls_own), channel_id=1, source_target_pairs={{0,1},{1,0},{2,3},{3,2},{4,5},{5,4},{6,7},{7,6},{8,9},{9,8},{10,11... | collective-permute-start | bytes 1032200 | tf_op jit(solution)/shard_map/ppermute | solution.py:111
  118.6 22.3 %collective-permute-start.29 = (bf16[16,768]{1,0:T(8,128)(2,1)S(1)}, bf16[16,768]{1,0:T(8,128)(2,1)S(1)}, u32[]{:S(2)}, u32[]{:S(2)}) collective-permute-start(bf16[16,768]{1,0:T(8,128)(2,1)S(1)} %get-tuple-element.155), channel_id=1, source_target_pairs={{0,8},{1,9},{2,10},{3,11},{4,12},{5,13},{6,14},{7,15},{8,0},{9,1},... | collective-permute-start | bytes 73736 | tf_op jit(solution)/shard_map/ppermute | solution.py:111
  124.1 16.8 %collective-permute-start.30 = (bf16[16,768]{1,0:T(8,128)(2,1)S(1)}, bf16[16,768]{1,0:T(8,128)(2,1)S(1)}, u32[]{:S(2)}, u32[]{:S(2)}) collective-permute-start(bf16[16,768]{1,0:T(8,128)(2,1)S(1)} %get-tuple-element.155), channel_id=1, source_target_pairs={{0,16},{1,17},{2,18},{3,19},{4,20},{5,21},{6,22},{7,23},{8,24},{9,... | collective-permute-start | bytes 73736 | tf_op jit(solution)/shard_map/ppermute | solution.py:111
  125.9 15.1 %collective-permute-start.31 = (bf16[16,768]{1,0:T(8,128)(2,1)S(1)}, bf16[16,768]{1,0:T(8,128)(2,1)S(1)}, u32[]{:S(2)}, u32[]{:S(2)}) collective-permute-start(bf16[16,768]{1,0:T(8,128)(2,1)S(1)} %get-tuple-element.155), channel_id=1, source_target_pairs={{0,24},{1,25},{2,26},{3,27},{4,28},{5,29},{6,30},{7,31},{8,16},{9,... | collective-permute-start | bytes 73736 | tf_op jit(solution)/shard_map/ppermute | solution.py:111
  141.0 13.8 %collective-permute-start.37 = (bf16[512,3072]{1,0:T(8,128)(2,1)S(1)}, bf16[512,3072]{1,0:T(8,128)(2,1)S(1)}, u32[]{:S(2)}, u32[]{:S(2)}) collective-permute-start(bf16[512,3072]{1,0:T(8,128)(2,1)S(1)} %get-tuple-element.159.refs_6_), channel_id=1, source_target_pairs={{0,1},{1,0},{2,3},{3,2},{4,5},{5,4},{6,7},{7,6},{8,9},{9,8},{10,11... | collective-permute-start | bytes 9437192 | tf_op jit(solution)/shard_map/ppermute | solution.py:111
  141.1 13.7 %collective-permute-start.38 = (bf16[512,768]{1,0:T(8,128)(2,1)S(1)}, bf16[512,768]{1,0:T(8,128)(2,1)S(1)}, u32[]{:S(2)}, u32[]{:S(2)}) collective-permute-start(bf16[512,768]{1,0:T(8,128)(2,1)S(1)} %get-tuple-element.148.down_ref.refs_4_), channel_id=1, source_target_pairs={{0,1},{1,0},{2,3},{3,2},{4,5},{5,4},{6,7},{7,6},{8,9},{9,8},{10,11... | collective-permute-start | bytes 2359304 | tf_op jit(solution)/shard_map/ppermute | solution.py:111
  141.6 13.2 %collective-permute-start.34 = (bf16[4,16,768]{2,1,0:T(8,128)(2,1)S(1)}, bf16[4,16,768]{2,1,0:T(8,128)(2,1)S(1)}, u32[]{:S(2)}, u32[]{:S(2)}) collective-permute-start(bf16[4,16,768]{2,1,0:T(8,128)(2,1)S(1)} %pad_maximum_fusion.6), channel_id=1, source_target_pairs={{0,2},{1,3},{2,0},{3,1},{4,6},{5,7},{6,4},{7,5},{8,10},{9,11},{10,... | collective-permute-start | bytes 294920 | tf_op jit(solution)/shard_map/ppermute | solution.py:111
  143.8 11.0 %collective-permute-start.35 = (bf16[4,16,768]{2,1,0:T(8,128)(2,1)S(1)}, bf16[4,16,768]{2,1,0:T(8,128)(2,1)S(1)}, u32[]{:S(2)}, u32[]{:S(2)}) collective-permute-start(bf16[4,16,768]{2,1,0:T(8,128)(2,1)S(1)} %pad_maximum_fusion.6), channel_id=1, source_target_pairs={{0,4},{1,5},{2,6},{3,7},{4,0},{5,1},{6,2},{7,3},{8,12},{9,13},{10,... | collective-permute-start | bytes 294920 | tf_op jit(solution)/shard_map/ppermute | solution.py:111
  144.6 10.2 %collective-permute-start.36 = (bf16[4,16,768]{2,1,0:T(8,128)(2,1)S(1)}, bf16[4,16,768]{2,1,0:T(8,128)(2,1)S(1)}, u32[]{:S(2)}, u32[]{:S(2)}) collective-permute-start(bf16[4,16,768]{2,1,0:T(8,128)(2,1)S(1)} %pad_maximum_fusion.6), channel_id=1, source_target_pairs={{0,6},{1,7},{2,4},{3,5},{4,2},{5,3},{6,0},{7,1},{8,14},{9,15},{10,... | collective-permute-start | bytes 294920 | tf_op jit(solution)/shard_map/ppermute | solution.py:111
  156.7 10.0 %collective-permute-start.40 = (bf16[512,3072]{1,0:T(8,128)(2,1)S(1)}, bf16[512,3072]{1,0:T(8,128)(2,1)S(1)}, u32[]{:S(2)}, u32[]{:S(2)}) collective-permute-start(bf16[512,3072]{1,0:T(8,128)(2,1)S(1)} %get-tuple-element.165.refs_2_), channel_id=1, source_target_pairs={{0,1},{1,0},{2,3},{3,2},{4,5},{5,4},{6,7},{7,6},{8,9},{9,8},{10,11... | collective-permute-start | bytes 9437192 | tf_op jit(solution)/shard_map/ppermute | solution.py:111
  156.8 9.8 %collective-permute-start.33 = (bf16[512,768]{1,0:T(8,128)(2,1)S(1)}, bf16[512,768]{1,0:T(8,128)(2,1)S(1)}, u32[]{:S(2)}, u32[]{:S(2)}) collective-permute-start(bf16[512,768]{1,0:T(8,128)(2,1)S(1)} %copy-done.2), channel_id=1, source_target_pairs={{0,1},{1,0},{2,3},{3,2},{4,5},{5,4},{6,7},{7,6},{8,9},{9,8},{10,11... | collective-permute-start | bytes 2359304 | tf_op jit(solution)/shard_map/ppermute | solution.py:111
  157.2 9.5 %collective-permute-start.41 = (f32[8,768]{1,0:T(8,128)S(1)}, f32[8,768]{1,0:T(8,128)S(1)}, u32[]{:S(2)}, u32[]{:S(2)}) collective-permute-start(f32[8,768]{1,0:T(8,128)S(1)} %get-tuple-element.173.refs_11_), channel_id=1, source_target_pairs={{0,1},{1,0},{2,3},{3,2},{4,5},{5,4},{6,7},{7,6},{8,9},{9,8},{10,11... | collective-permute-start | bytes 73736 | tf_op jit(solution)/shard_map/ppermute | solution.py:111
  180.5 19.0 %collective-permute-start.42 = (bf16[2,1312,128]{2,1,0:T(8,128)(2,1)}, bf16[2,1312,128]{2,1,0:T(8,128)(2,1)}, u32[]{:S(2)}, u32[]{:S(2)}) collective-permute-start(bf16[2,1312,128]{2,1,0:T(8,128)(2,1)} %get-tuple-element.192), channel_id=1, source_target_pairs={{0,2},{1,3},{2,0},{3,1},{4,6},{5,7},{6,4},{7,5},{8,10},{9,11},{10,... | collective-permute-start | bytes 2015240 | tf_op jit(solution)/shard_map/ppermute | solution.py:111
  182.6 18.1 %collective-permute-start.43 = (bf16[2,1312,128]{2,1,0:T(8,128)(2,1)}, bf16[2,1312,128]{2,1,0:T(8,128)(2,1)S(1)}, u32[]{:S(2)}, u32[]{:S(2)}) collective-permute-start(bf16[2,1312,128]{2,1,0:T(8,128)(2,1)} %get-tuple-element.193), channel_id=1, source_target_pairs={{0,4},{1,5},{2,6},{3,7},{4,0},{5,1},{6,2},{7,3},{8,12},{9,13},{10,... | collective-permute-start | bytes 2015240 | tf_op jit(solution)/shard_map/ppermute | solution.py:111
  183.3 34.9 %collective-permute-start.45 = (bf16[2,1312,128]{2,1,0:T(8,128)(2,1)}, bf16[2,1312,128]{2,1,0:T(8,128)(2,1)S(1)}, u32[]{:S(2)}, u32[]{:S(2)}) collective-permute-start(bf16[2,1312,128]{2,1,0:T(8,128)(2,1)} %get-tuple-element.220), channel_id=1, source_target_pairs={{0,4},{1,5},{2,6},{3,7},{4,0},{5,1},{6,2},{7,3},{8,12},{9,13},{10,... | collective-permute-start | bytes 2015240 | tf_op jit(solution)/shard_map/ppermute | solution.py:111
  201.8 16.5 %collective-permute-start.44 = (bf16[2,1312,128]{2,1,0:T(8,128)(2,1)}, bf16[2,1312,128]{2,1,0:T(8,128)(2,1)}, u32[]{:S(2)}, u32[]{:S(2)}) collective-permute-start(bf16[2,1312,128]{2,1,0:T(8,128)(2,1)} %add_convert_fusion.2), channel_id=1, source_target_pairs={{0,2},{1,3},{2,0},{3,1},{4,6},{5,7},{6,4},{7,5},{8,10},{9,11},{10,... | collective-permute-start | bytes 2015240 | tf_op jit(solution)/shard_map/ppermute | solution.py:111
  218.2 2.7 collective-permute-start.50
  218.3 4.7 %collective-permute-start.49 = (bf16[2,624,128]{2,1,0:T(8,128)(2,1)}, bf16[2,624,128]{2,1,0:T(8,128)(2,1)S(1)}, u32[]{:S(2)}, u32[]{:S(2)}) collective-permute-start(bf16[2,624,128]{2,1,0:T(8,128)(2,1)} %get-tuple-element.228), channel_id=1, source_target_pairs={{0,1},{1,0},{2,3},{3,2},{4,5},{5,4},{6,7},{7,6},{8,9},{9,8},{10,11... | collective-permute-start | bytes 958472 | tf_op jit(solution)/shard_map/ppermute | solution.py:111
  218.8 5.2 %collective-permute-start.48 = (bf16[4,624,128]{2,1,0:T(8,128)(2,1)}, bf16[4,624,128]{2,1,0:T(8,128)(2,1)S(1)}, u32[]{:S(2)}, u32[]{:S(2)}) collective-permute-start(bf16[4,624,128]{2,1,0:T(8,128)(2,1)} %get-tuple-element.226), channel_id=1, source_target_pairs={{0,1},{1,0},{2,3},{3,2},{4,5},{5,4},{6,7},{7,6},{8,9},{9,8},{10,11... | collective-permute-start | bytes 1916936 | tf_op jit(solution)/shard_map/ppermute | solution.py:111
  218.9 7.4 %collective-permute-start.47 = (bf16[4,624,128]{2,1,0:T(8,128)(2,1)}, bf16[4,624,128]{2,1,0:T(8,128)(2,1)S(1)}, u32[]{:S(2)}, u32[]{:S(2)}) collective-permute-start(bf16[4,624,128]{2,1,0:T(8,128)(2,1)} %get-tuple-element.224), channel_id=1, source_target_pairs={{0,1},{1,0},{2,3},{3,2},{4,5},{5,4},{6,7},{7,6},{8,9},{9,8},{10,11... | collective-permute-start | bytes 1916936 | tf_op jit(solution)/shard_map/ppermute | solution.py:111
  219.3 8.1 %collective-permute-start.46 = (bf16[4,624,128]{2,1,0:T(8,128)(2,1)}, bf16[4,624,128]{2,1,0:T(8,128)(2,1)S(1)}, u32[]{:S(2)}, u32[]{:S(2)}) collective-permute-start(bf16[4,624,128]{2,1,0:T(8,128)(2,1)} %get-tuple-element.222), channel_id=1, source_target_pairs={{0,1},{1,0},{2,3},{3,2},{4,5},{5,4},{6,7},{7,6},{8,9},{9,8},{10,11... | collective-permute-start | bytes 1916936 | tf_op jit(solution)/shard_map/ppermute | solution.py:111
  221.0 17.6 %collective-permute-start.51 = (bf16[2,1312,128]{2,1,0:T(8,128)(2,1)S(1)}, bf16[2,1312,128]{2,1,0:T(8,128)(2,1)S(1)}, u32[]{:S(2)}, u32[]{:S(2)}) collective-permute-start(bf16[2,1312,128]{2,1,0:T(8,128)(2,1)S(1)} %copy-done.50), channel_id=1, source_target_pairs={{0,2},{1,3},{2,0},{3,1},{4,6},{5,7},{6,4},{7,5},{8,10},{9,11},{10,... | collective-permute-start | bytes 2015240 | tf_op jit(solution)/shard_map/ppermute | solution.py:111
  223.1 17.2 %collective-permute-start.52 = (bf16[2,1312,128]{2,1,0:T(8,128)(2,1)S(1)}, bf16[2,1312,128]{2,1,0:T(8,128)(2,1)S(1)}, u32[]{:S(2)}, u32[]{:S(2)}) collective-permute-start(bf16[2,1312,128]{2,1,0:T(8,128)(2,1)S(1)} %add_convert_fusion.3), channel_id=1, source_target_pairs={{0,4},{1,5},{2,6},{3,7},{4,0},{5,1},{6,2},{7,3},{8,12},{9,13},{10,... | collective-permute-start | bytes 2015240 | tf_op jit(solution)/shard_map/ppermute | solution.py:111
  224.0 28.3 %collective-permute-start.61 = (bf16[1312,128]{1,0:T(8,128)(2,1)S(1)}, bf16[1312,128]{1,0:T(8,128)(2,1)S(1)}, u32[]{:S(2)}, u32[]{:S(2)}) collective-permute-start(bf16[1312,128]{1,0:T(8,128)(2,1)S(1)} %get-tuple-element.260), channel_id=1, source_target_pairs={{0,16},{1,17},{2,18},{3,19},{4,20},{5,21},{6,22},{7,23},{8,24},{9,... | collective-permute-start | bytes 1007624 | tf_op jit(solution)/shard_map/ppermute | solution.py:111
  226.3 26.0 %collective-permute-start.62 = (bf16[1312,128]{1,0:T(8,128)(2,1)S(1)}, bf16[1312,128]{1,0:T(8,128)(2,1)S(1)}, u32[]{:S(2)}, u32[]{:S(2)}) collective-permute-start(bf16[1312,128]{1,0:T(8,128)(2,1)S(1)} %get-tuple-element.261), channel_id=1, source_target_pairs={{0,24},{1,25},{2,26},{3,27},{4,28},{5,29},{6,30},{7,31},{8,16},{9,... | collective-permute-start | bytes 1007624 | tf_op jit(solution)/shard_map/ppermute | solution.py:111
  240.3 8.8 %collective-permute-start.53 = (bf16[2,624,128]{2,1,0:T(8,128)(2,1)S(1)}, bf16[2,624,128]{2,1,0:T(8,128)(2,1)S(1)}, u32[]{:S(2)}, u32[]{:S(2)}) collective-permute-start(bf16[2,624,128]{2,1,0:T(8,128)(2,1)S(1)} %add_convert_fusion.10), channel_id=1, source_target_pairs={{0,4},{1,5},{2,6},{3,7},{4,0},{5,1},{6,2},{7,3},{8,12},{9,13},{10,... | collective-permute-start | bytes 958472 | tf_op jit(solution)/shard_map/ppermute | solution.py:111
  241.4 14.9 %collective-permute-start.60 = (bf16[1312,128]{1,0:T(8,128)(2,1)S(1)}, bf16[1312,128]{1,0:T(8,128)(2,1)S(1)}, u32[]{:S(2)}, u32[]{:S(2)}) collective-permute-start(bf16[1312,128]{1,0:T(8,128)(2,1)S(1)} %get-tuple-element.258), channel_id=1, source_target_pairs={{0,8},{1,9},{2,10},{3,11},{4,12},{5,13},{6,14},{7,15},{8,0},{9,1},... | collective-permute-start | bytes 1007624 | tf_op jit(solution)/shard_map/ppermute | solution.py:111
  242.0 8.6 %collective-permute-start.55 = (bf16[2,624,128]{2,1,0:T(8,128)(2,1)S(1)}, bf16[2,624,128]{2,1,0:T(8,128)(2,1)S(1)}, u32[]{:S(2)}, u32[]{:S(2)}) collective-permute-start(bf16[2,624,128]{2,1,0:T(8,128)(2,1)S(1)} %add_convert_fusion.11), channel_id=1, source_target_pairs={{0,2},{1,3},{2,0},{3,1},{4,6},{5,7},{6,4},{7,5},{8,10},{9,11},{10,... | collective-permute-start | bytes 958472 | tf_op jit(solution)/shard_map/ppermute | solution.py:111
  249.2 14.8 %collective-permute-start.54 = (bf16[4,624,128]{2,1,0:T(8,128)(2,1)S(1)}, bf16[4,624,128]{2,1,0:T(8,128)(2,1)S(1)}, u32[]{:S(2)}, u32[]{:S(2)}) collective-permute-start(bf16[4,624,128]{2,1,0:T(8,128)(2,1)S(1)} %pad_maximum_fusion.3), channel_id=1, source_target_pairs={{0,2},{1,3},{2,0},{3,1},{4,6},{5,7},{6,4},{7,5},{8,10},{9,11},{10,... | collective-permute-start | bytes 1916936 | tf_op jit(solution)/shard_map/ppermute | solution.py:111
  250.8 14.8 %collective-permute-start.56 = (bf16[4,624,128]{2,1,0:T(8,128)(2,1)S(1)}, bf16[4,624,128]{2,1,0:T(8,128)(2,1)S(1)}, u32[]{:S(2)}, u32[]{:S(2)}) collective-permute-start(bf16[4,624,128]{2,1,0:T(8,128)(2,1)S(1)} %pad_maximum_fusion.4), channel_id=1, source_target_pairs={{0,4},{1,5},{2,6},{3,7},{4,0},{5,1},{6,2},{7,3},{8,12},{9,13},{10,... | collective-permute-start | bytes 1916936 | tf_op jit(solution)/shard_map/ppermute | solution.py:111
  266.0 6.9 %collective-permute-start.57 = (bf16[624,128]{1,0:T(8,128)(2,1)S(1)}, bf16[624,128]{1,0:T(8,128)(2,1)S(1)}, u32[]{:S(2)}, u32[]{:S(2)}) collective-permute-start(bf16[624,128]{1,0:T(8,128)(2,1)S(1)} %get-tuple-element.262), channel_id=1, source_target_pairs={{0,8},{1,9},{2,10},{3,11},{4,12},{5,13},{6,14},{7,15},{8,0},{9,1},... | collective-permute-start | bytes 479240 | tf_op jit(solution)/shard_map/ppermute | solution.py:111
  266.6 12.9 %collective-permute-start.58 = (bf16[624,128]{1,0:T(8,128)(2,1)S(1)}, bf16[624,128]{1,0:T(8,128)(2,1)S(1)}, u32[]{:S(2)}, u32[]{:S(2)}) collective-permute-start(bf16[624,128]{1,0:T(8,128)(2,1)S(1)} %get-tuple-element.264), channel_id=1, source_target_pairs={{0,16},{1,17},{2,18},{3,19},{4,20},{5,21},{6,22},{7,23},{8,24},{9,... | collective-permute-start | bytes 479240 | tf_op jit(solution)/shard_map/ppermute | solution.py:111
  269.0 10.5 %collective-permute-start.59 = (bf16[624,128]{1,0:T(8,128)(2,1)S(1)}, bf16[624,128]{1,0:T(8,128)(2,1)S(1)}, u32[]{:S(2)}, u32[]{:S(2)}) collective-permute-start(bf16[624,128]{1,0:T(8,128)(2,1)S(1)} %get-tuple-element.263), channel_id=1, source_target_pairs={{0,24},{1,25},{2,26},{3,27},{4,28},{5,29},{6,30},{7,31},{8,16},{9,... | collective-permute-start | bytes 479240 | tf_op jit(solution)/shard_map/ppermute | solution.py:111
  283.6 3.7 %collective-permute-start.64 = (f32[]{:T(128)}, f32[]{:T(128)}, u32[]{:S(2)}, u32[]{:S(2)}) collective-permute-start(f32[]{:T(128)} %add.205), channel_id=1, source_target_pairs={{0,2},{1,3},{2,0},{3,1},{4,6},{5,7},{6,4},{7,5},{8,10},{9,11},{10,... | collective-permute-start | bytes 20 | tf_op jit(solution)/shard_map/ppermute | solution.py:111
  287.9 3.7 %collective-permute-start.65 = (f32[]{:T(128)}, f32[]{:T(128)}, u32[]{:S(2)}, u32[]{:S(2)}) collective-permute-start(f32[]{:T(128)} %add.206), channel_id=1, source_target_pairs={{0,4},{1,5},{2,6},{3,7},{4,0},{5,1},{6,2},{7,3},{8,12},{9,13},{10,... | collective-permute-start | bytes 20 | tf_op jit(solution)/shard_map/ppermute | solution.py:111
  292.1 4.0 %collective-permute-start.66 = (f32[]{:T(128)}, f32[]{:T(128)}, u32[]{:S(2)}, u32[]{:S(2)}) collective-permute-start(f32[]{:T(128)} %add.207), channel_id=1, source_target_pairs={{0,8},{1,9},{2,10},{3,11},{4,12},{5,13},{6,14},{7,15},{8,0},{9,1},... | collective-permute-start | bytes 20 | tf_op jit(solution)/shard_map/ppermute | solution.py:111
  296.7 4.8 %collective-permute-start.67 = (f32[]{:T(128)}, f32[]{:T(128)}, u32[]{:S(2)}, u32[]{:S(2)}) collective-permute-start(f32[]{:T(128)} %add.208), channel_id=1, source_target_pairs={{0,16},{1,17},{2,18},{3,19},{4,20},{5,21},{6,22},{7,23},{8,24},{9,... | collective-permute-start | bytes 20 | tf_op jit(solution)/shard_map/ppermute | solution.py:111
  (58 other events, 737.9 us)

commit v2 on v1

--- a/solution.py
+++ b/solution.py
@@ -249,17 +249,29 @@
 
 def place_blocks(shard, layout, pieces, me, stage, flat, sems):
     count, rows = stage.shape[0], stage.shape[1]
+    inner = shard // (8 * LANES) * 8
     for piece, slots in zip(pieces, piece_slots(me, layout)):
         for k, slot in enumerate(slots):
             pltpu.make_async_copy(piece.at[k], stage.at[slot], sems.at[slot]).start()
-    flat[pl.ds(0, 8), :] = jnp.zeros((8, LANES), jnp.float32)
-
-    def place(device, carry):
+
+    def start_of(device):
+        return pl.multiple_of(device * shard // LANES // 8 * 8, 8)
+
+    def clear(device, carry):
+        at = start_of(device)
+        flat[pl.ds(at, 8), :] = jnp.zeros((8, LANES), jnp.float32)
+        flat[pl.ds(at + inner, 16), :] = jnp.zeros((16, LANES), jnp.float32)
+        return carry
+
+    lax.fori_loop(0, count, clear, 0)
+
+    def place(index, carry):
+        device = me ^ ((index >> 4) + 2 * ((index >> 2) & 3) + 8 * (index & 3))
         pltpu.make_async_copy(pieces[0].at[0], stage.at[device], sems.at[device]).wait()
-        at = pl.multiple_of(device * shard // LANES // 8 * 8, 8)
-        before = flat[pl.ds(at, 8), :]
-        flat[pl.ds(at, rows), :] = stage[device].astype(jnp.float32)
-        flat[pl.ds(at, 8), :] += before
+        at = start_of(device)
+        flat[pl.ds(at, 8), :] += stage[device, :16].astype(jnp.float32)[:8]
+        flat[pl.ds(at + 8, inner - 8), :] = stage[device].astype(jnp.float32)[8:inner]
+        flat[pl.ds(at + inner, 16), :] += stage[device].astype(jnp.float32)[inner : inner + 16]
         return carry
 
     lax.fori_loop(0, count, place, 0)
@@ -703,15 +715,11 @@
     stage, flat, first_all, picked, mask, sems, in_sems = refs[22:]
     cols = w_ref.shape[1] // LANES
     tokens = mask.shape[1]
-    loads = [pltpu.make_async_copy(first_hbm, first_all, in_sems.at[2])]
-    for view in range(2):
-        loads.append(pltpu.make_async_copy(mask_hbm.at[view, 2], mask.at[view], in_sems.at[view]))
-    for load in loads:
-        load.start()
     place_blocks(shard, HALVES, pieces, me_ref[0], stage, flat, sems)
+    loads = [(first_hbm, first_all)] + [(mask_hbm.at[view, 2], mask.at[view]) for view in range(2)]
+    loads = bring(loads, in_sems)
     gather_matrix(flat, w_ref)
-    for load in loads:
-        load.wait()
+    await_all(loads)
     n = unit_ref.shape[0] // 2
     for view in range(2):
         for slot in range(n):
@@ -1027,18 +1035,17 @@
         for side in range(2):
             pairs.append((mains[2 * k + side], whole.at[pl.ds(side * many, many)]))
     loads = bring(pairs + [(part_in, part), (part_sib_in, part_sib)], in_sems)
-    for load in loads[:6]:
-        load.wait()
     top_row = lax.broadcasted_iota(jnp.int32, (16, 1), 0) == 0
-    for side in range(2):
-        first_at = place if side == 0 else n - place
-        for view in range(2):
-            for slot in range(half):
-                at = pl.multiple_of(side * many + view * (many // 2) + pick_ref[side, slot], 16)
-                source = pl.ds(first_at + view * half + slot, 1)
-                for whole, cols in ((up, pl.ds(D, 4 * D)), (down, pl.ds(0, D))):
-                    more = jnp.where(top_row, cls[source, cols], 0.0)
+
+    def join(whole, cols):
+        for side in range(2):
+            first_at = place if side == 0 else n - place
+            for view in range(2):
+                for slot in range(half):
+                    at = pl.multiple_of(side * many + view * (many // 2) + pick_ref[side, slot], 16)
+                    more = jnp.where(top_row, cls[pl.ds(first_at + view * half + slot, 1), cols], 0.0)
                     whole[pl.ds(at, 16), :] = (whole[pl.ds(at, 16), :] + more).astype(jnp.bfloat16)
+
     blocks, rows = stage.shape[0], stage.shape[1]
     cols = 9 * D // LANES
     pick = pick_columns(core, blocks)
@@ -1057,11 +1064,13 @@
         for k in range(right.shape[1] // chunk):
             spread(plain_rows(left, right[:, pl.ds(k * chunk, chunk)], NN), first_col + k * chunk // LANES)
 
+    await_all(loads[:4])
+    join(up, pl.ds(D, 4 * D))
     fill(plain_rows(pick, first[...], NT).astype(jnp.bfloat16), up, 0)
     few = plain_rows(pick, cls_low[:, :D], NT).astype(jnp.bfloat16)
     spread(plain_rows(few, cls_low[:, D:], NN), 8 * D // LANES)
-    for load in loads[6:]:
-        load.wait()
+    await_all(loads[4:])
+    join(down, pl.ds(0, D))
     fill(plain_rows(pick, down[...], NT).astype(jnp.bfloat16), act, 4 * D // LANES)
 
     @pl.when(core == 1)

time: 313 us -> 310 us (level)
  no operation moved by 1% of the time
where the time goes in v2:
time: 310 us; the launch traced here: 307 us
  Pallas kernels  103 us (33%)
  waiting for transfers between devices  91.5 us (30%)
  starting transfers between devices  74.4 us (24%)
  other arithmetic  18 us (6%)
  between operations  13.7 us (4%)
  local copies, waits for them, and re-layouts  6.23 us (2%)
    ppermute x68, waiting for transfers between devices, swap(): return lax.ppermute(value, 'sent', [(i, i ^ bit) for i in range(count)])  91.5 us
    ppermute x68, starting transfers between devices, swap(): return lax.ppermute(value, 'sent', [(i, i ^ bit) for i in range(count)])  74.4 us
    pallas_call x1, Pallas kernels, attn_forward(): pl.pallas_call(functools.partial(attn_kernel, shard), out_shape=tuple((ja...  20.2 us
    pallas_call x1, Pallas kernels, head_grads(): pl.pallas_call(functools.partial(head_grad_kernel, shard), out_shape=tupl...  14.3 us
    pallas_call x1, Pallas kernels, attn_grads(): pl.pallas_call(functools.partial(attn_grad_kernel, shard), out_shape=(jax...  12.8 us
    pallas_call x1, Pallas kernels, head_forward(): pl.pallas_call(forward_kernel, out_shape=(result((both, 4 * D), low, True...  12.4 us
    pallas_call x1, Pallas kernels, make_head(): pl.pallas_call(functools.partial(head_kernel, shard), out_shape=(result((...  9.91 us
    pallas_call x1, Pallas kernels, head_backward(): pl.pallas_call(backward_kernel, out_shape=(result((both, 4 * D), low, Tru...  9.4 us
  transfers between devices with their start and end apart: 68, of which 29 were waited for; matrix products, arithmetic and copies ran while one was open for 5% of the time, Pallas kernels for 26%

profile of v2, /device:TPU:0, one launch (start us, length us, event | category | flops | bytes accessed | tf_op | source)
XLA Modules:
  0.0 307.0 jit_solution(9694871354466634652)
XLA Ops:
  0.7 1.2 select_bitcast_fusion.1
  2.0 3.1 %collective-permute-start = (bf16[624,128]{1,0:T(8,128)(2,1)S(1)}, bf16[624,128]{1,0:T(8,128)(2,1)S(1)}, u32[]{:S(2)}, u32[]{:S(2)}) collective-permute-start(bf16[624,128]{1,0:T(8,128)(2,1)S(1)} %fusion.5), channel_id=1, source_target_pairs={{0,8},{1,9},{2,10},{3,11},{4,12},{5,13},{6,14},{7,15},{8,0},{9,1},... | collective-permute-start | bytes 479240 | tf_op jit(solution)/shard_map/ppermute | solution.py:111
  5.1 2.6 collective-permute-start.1
  7.7 3.8 %collective-permute-done = bf16[624,128]{1,0:T(8,128)(2,1)S(1)} collective-permute-done((bf16[624,128]{1,0:T(8,128)(2,1)S(1)}, bf16[624,128]{1,0:T(8,128)(2,1)S(1)}, u32[]{:S(2)}, u32[]{:S(2)}) %collective-permute-start) | collective-permute-done | bytes 159776 | tf_op jit(solution)/shard_map/ppermute | solution.py:111
  11.6 8.3 %collective-permute-done.1 = bf16[624,128]{1,0:T(8,128)(2,1)S(1)} collective-permute-done((bf16[624,128]{1,0:T(8,128)(2,1)S(1)}, bf16[624,128]{1,0:T(8,128)(2,1)S(1)}, u32[]{:S(2)}, u32[]{:S(2)}) %collective-permute-start.1) | collective-permute-done | bytes 159776 | tf_op jit(solution)/shard_map/ppermute | solution.py:111
  20.0 1.6 collective-permute-start.4
  21.6 1.5 collective-permute-start.3
  23.3 2.6 collective-permute-start.12
  26.0 1.1 collective-permute-start.13
  27.1 1.4 collective-permute-start.14
  28.4 5.2 %collective-permute-done.4.refs_2_ = bf16[4,624,128]{2,1,0:T(8,128)(2,1)S(1)} collective-permute-done((bf16[4,624,128]{2,1,0:T(8,128)(2,1)S(1)}, bf16[4,624,128]{2,1,0:T(8,128)(2,1)S(1)}, u32[]{:S(2)}, u32[]{:S(2)}) %collective-permute-start.4) | collective-permute-done | bytes 639008 | tf_op jit(solution)/shard_map/ppermute | solution.py:111
  34.5 1.5 collective-permute-start.5
  36.9 1.4 collective-permute-start.6
  43.0 9.1 %collective-permute-done.13 = bf16[1312,128]{1,0:T(8,128)(2,1)S(1)} collective-permute-done((bf16[1312,128]{1,0:T(8,128)(2,1)S(1)}, bf16[1312,128]{1,0:T(8,128)(2,1)S(1)}, u32[]{:S(2)}, u32[]{:S(2)}) %collective-permute-start.13) | collective-permute-done | bytes 335904 | tf_op jit(solution)/shard_map/ppermute | solution.py:111
  56.6 1.6 collective-permute-start.15
  58.2 1.5 collective-permute-start.17
  64.1 20.2 %shard_map.220 = (bf16[768,3072]{1,0:T(8,128)(2,1)}, f32[8,768]{1,0:T(8,128)}, f32[256,768]{1,0:T(8,128)}, bf16[512,768]{1,0:T(8,128)(2,1)}, bf16[512,2304]{1,0:...) custom-call(s32[1]{0:T(128)} %bitcast.me_ref, ...), custom_call_target="tpu_custom_call" | custom-call | tf_op jit(solution)/shard_map/pallas_call | solution.py:466
  84.6 1.5 collective-permute-done.15.refs_2_
  86.3 1.5 collective-permute-start.19
  89.0 13.6 %collective-permute-done.19.refs_6_ = bf16[2,1312,128]{2,1,0:T(8,128)(2,1)S(1)} collective-permute-done((bf16[2,1312,128]{2,1,0:T(8,128)(2,1)}, bf16[2,1312,128]{2,1,0:T(8,128)(2,1)S(1)}, u32[]{:S(2)}, u32[]{:S(2)}) %collective-permute-start.19) | collective-permute-done | bytes 671776 | tf_op jit(solution)/shard_map/ppermute | solution.py:111
  102.6 1.1 collective-permute-done.20.refs_7_
  106.9 9.9 %shard_map.221 = (bf16[768,6912]{1,0:T(8,128)(2,1)S(1)}, f32[8,768]{1,0:T(8,128)S(1)}, bf16[16,768]{1,0:T(8,128)(2,1)S(1)}, f32[16,5376]{1,0:T(8,128)S(1)}) custom-call(s32[1]{0:T(128)} %bitcast.me_ref, s32[9]{0:T(128)S(1)} %pad_add_fusion.1.pick_ref, bf16[2,1312,128]{2,1,0:T(8,128)(2,1)} %copy-done.14, bf16[2,1312,128]{2,1,0:T(8,128)(2,1)} %copy-done.13, ...), custom_call_target="tpu_custom_call" | custom-call | tf_op jit(solution)/shard_map/pallas_call | solution.py:752
  117.1 5.1 %collective-permute-start.29 = (bf16[16,768]{1,0:T(8,128)(2,1)S(1)}, bf16[16,768]{1,0:T(8,128)(2,1)S(1)}, u32[]{:S(2)}, u32[]{:S(2)}) collective-permute-start(bf16[16,768]{1,0:T(8,128)(2,1)S(1)} %get-tuple-element.155), channel_id=1, source_target_pairs={{0,8},{1,9},{2,10},{3,11},{4,12},{5,13},{6,14},{7,15},{8,0},{9,1},... | collective-permute-start | bytes 73736 | tf_op jit(solution)/shard_map/ppermute | solution.py:111
  122.1 1.2 collective-permute-start.30
  123.3 1.5 collective-permute-start.31
  124.8 1.1 copy-done.8
  126.0 12.4 %shard_map.222 = (bf16[512,3072]{1,0:T(8,128)(2,1)S(1)}, bf16[512,3072]{1,0:T(8,128)(2,1)S(1)}, bf16[2,256,768]{2,1,0:T(8,128)(2,1)}, f32[512,768]{1,0:T(8,128)S...) custom-call(bf16[512,768]{1,0:T(8,128)(2,1)S(1)} %copy-done.2, f32[512,768]{1,0:T(8,128)S(1)} %copy-done.1, ...), custom_call_target="tpu_custom_call" | custom-call | tf_op jit(solution)/shard_map/pallas_call | solution.py:851
  139.0 2.1 collective-permute-start.34
  142.7 9.4 %shard_map.223 = (bf16[512,3072]{1,0:T(8,128)(2,1)S(1)}, f32[512,768]{1,0:T(8,128)}, f32[8,768]{1,0:T(8,128)S(1)}) custom-call(bf16[512,768]{1,0:T(8,128)(2,1)S(1)} %get-tuple-element.148.down_ref.refs_4_, bf16[512,3072]{1,0:T(8,128)(2,1)S(1)} %get-tuple-element.149.slope_ref, f32[512,768]{1,0:T(8,128)S(1)} %get-tuple-element.150.d_res_ref, ...), custom_call_target="tpu_custom_call" | custom-call | tf_op jit(solution)/shard_map/pallas_call | solution.py:898
  152.3 1.7 collective-permute-done.39.sib_ref
  154.7 9.2 %shard_map.224 = (f32[1,1]{1,0:T(1,128)}, f32[16,768]{1,0:T(8,128)}, f32[32,3840]{1,0:T(8,128)S(1)}, bf16[32,1536]{1,0:T(8,128)(2,1)S(1)}, f32[8,768]{1,0:T(8,128)S(1)}) custom-call(s32[1]{0:T(128)} %bitcast.me_ref, bf16[4,4,16,768]{3,2,1,0:T(8,128)(2,1)} %copy-done.18, bf16[4,4,16,768]{3,2,1,0:T(8,128)(2,1)} %copy-done.39, bf16[768,6912]{1,0:T(8,128)(2,1)} %copy-done, ...), custom_call_target="tpu_custom_call" | custom-call | tf_op jit(solution)/shard_map/pallas_call | solution.py:997
  164.0 14.3 %shard_map.225 = (bf16[2,1312,128]{2,1,0:T(8,128)(2,1)}, bf16[2,1312,128]{2,1,0:T(8,128)(2,1)}, bf16[2,1312,128]{2,1,0:T(8,128)(2,1)}, bf16[2,1312,128]{2,1,0:T(...) custom-call(s32[1]{0:T(128)} %bitcast.me_ref, ...), custom_call_target="tpu_custom_call" | custom-call | tf_op jit(solution)/shard_map/pallas_call | solution.py:1099
  178.3 2.0 collective-permute-start.42
  180.8 1.6 collective-permute-start.45
  182.3 6.1 %shard_map.226 = (f32[512,768]{1,0:T(8,128)S(1)}, bf16[768,768]{1,0:T(8,128)(2,1)S(1)}, bf16[512,768]{1,0:T(8,128)(2,1)S(1)}, f32[8,768]{1,0:T(8,128)S(1)}) custom-call(s32[9]{0:T(128)S(1)} %pad_add_fusion.1.pick_ref, f32[512,768]{1,0:T(8,128)} %get-tuple-element.182.d_first, f32[16,768]{1,0:T(8,128)} %get-tuple-element.183.d_cls_in, ...), custom_call_target="tpu_custom_call" | custom-call | tf_op jit(solution)/shard_map/pallas_call | solution.py:541
  188.5 8.8 %shard_map.227 = (bf16[512,2304]{1,0:T(8,128)(2,1)S(1)}, f32[8,768]{1,0:T(8,128)}) custom-call(bf16[512,768]{1,0:T(8,128)(2,1)S(1)} %get-tuple-element.188.d_mixed, bf16[512,2304]{1,0:T(8,128)(2,1)S(1)} %copy-done.5, f32[4,6,256,128]{3,2,1,0:T(8,128)S(1)} %copy-done.4), custom_call_target="tpu_custom_call" | custom-call | tf_op jit(solution)/shard_map/pallas_call | solution.py:596
  197.3 1.1 collective-permute-done.43
  198.4 1.1 add_convert_fusion.2
  201.6 1.5 add_convert_fusion.3
  203.1 12.8 %shard_map.228 = (f32[256,768]{1,0:T(8,128)}, bf16[4,624,128]{2,1,0:T(8,128)(2,1)}, bf16[4,624,128]{2,1,0:T(8,128)(2,1)}, bf16[4,624,128]{2,1,0:T(8,128)(2,1)}, ...) custom-call(s32[1]{0:T(128)} %bitcast.me_ref, ...), custom_call_target="tpu_custom_call" | custom-call | tf_op jit(solution)/shard_map/pallas_call | solution.py:679
  217.1 1.5 add_convert_fusion
  218.7 2.0 collective-permute-start.51
  221.4 2.1 collective-permute-start.61
  223.8 1.2 collective-permute-start.62
  225.4 11.0 %collective-permute-done.51 = bf16[2,1312,128]{2,1,0:T(8,128)(2,1)S(1)} collective-permute-done((bf16[2,1312,128]{2,1,0:T(8,128)(2,1)S(1)}, bf16[2,1312,128]{2,1,0:T(8,128)(2,1)S(1)}, u32[]{:S(2)}, u32[]{:S(2)}) %collective-permute-start.51) | collective-permute-done | bytes 671776 | tf_op jit(solution)/shard_map/ppermute | solution.py:111
  236.4 1.7 collective-permute-done.52
  239.8 1.1 collective-permute-start.55
  240.9 5.9 %collective-permute-done.53 = bf16[2,624,128]{2,1,0:T(8,128)(2,1)S(1)} collective-permute-done((bf16[2,624,128]{2,1,0:T(8,128)(2,1)S(1)}, bf16[2,624,128]{2,1,0:T(8,128)(2,1)S(1)}, u32[]{:S(2)}, u32[]{:S(2)}) %collective-permute-start.53) | collective-permute-done | bytes 319520 | tf_op jit(solution)/shard_map/ppermute | solution.py:111
  247.0 1.5 collective-permute-start.54
  248.6 2.2 collective-permute-start.56
  250.8 2.9 collective-permute-done.60
  254.0 7.7 %collective-permute-done.54 = bf16[4,624,128]{2,1,0:T(8,128)(2,1)S(1)} collective-permute-done((bf16[4,624,128]{2,1,0:T(8,128)(2,1)S(1)}, bf16[4,624,128]{2,1,0:T(8,128)(2,1)S(1)}, u32[]{:S(2)}, u32[]{:S(2)}) %collective-permute-start.54) | collective-permute-done | bytes 639008 | tf_op jit(solution)/shard_map/ppermute | solution.py:111
  261.7 1.7 collective-permute-done.56
  264.6 2.1 collective-permute-start.58
  266.7 1.5 collective-permute-start.59
  269.0 1.1 collective-permute-done.57
  270.1 6.8 %collective-permute-done.58 = bf16[624,128]{1,0:T(8,128)(2,1)S(1)} collective-permute-done((bf16[624,128]{1,0:T(8,128)(2,1)S(1)}, bf16[624,128]{1,0:T(8,128)(2,1)S(1)}, u32[]{:S(2)}, u32[]{:S(2)}) %collective-permute-start.58) | collective-permute-done | bytes 159776 | tf_op jit(solution)/shard_map/ppermute | solution.py:111
  281.0 2.2 collective-permute-start.64
  283.2 1.5 collective-permute-done.64
  285.3 3.1 %collective-permute-start.65 = (f32[]{:T(128)}, f32[]{:T(128)}, u32[]{:S(2)}, u32[]{:S(2)}) collective-permute-start(f32[]{:T(128)} %add.206), channel_id=1, source_target_pairs={{0,4},{1,5},{2,6},{3,7},{4,0},{5,1},{6,2},{7,3},{8,12},{9,13},{10,... | collective-permute-start | bytes 20 | tf_op jit(solution)/shard_map/ppermute | solution.py:111
  289.6 3.6 %collective-permute-start.66 = (f32[]{:T(128)}, f32[]{:T(128)}, u32[]{:S(2)}, u32[]{:S(2)}) collective-permute-start(f32[]{:T(128)} %add.207), channel_id=1, source_target_pairs={{0,8},{1,9},{2,10},{3,11},{4,12},{5,13},{6,14},{7,15},{8,0},{9,1},... | collective-permute-start | bytes 20 | tf_op jit(solution)/shard_map/ppermute | solution.py:111
  294.1 4.7 %collective-permute-start.67 = (f32[]{:T(128)}, f32[]{:T(128)}, u32[]{:S(2)}, u32[]{:S(2)}) collective-permute-start(f32[]{:T(128)} %add.208), channel_id=1, source_target_pairs={{0,16},{1,17},{2,18},{3,19},{4,20},{5,21},{6,22},{7,23},{8,24},{9,... | collective-permute-start | bytes 20 | tf_op jit(solution)/shard_map/ppermute | solution.py:111
  299.9 3.1 %multiply_add_fusion.1 = (f32[166080]{0:T(1024)}, f32[166080]{0:T(1024)}, f32[166080]{0:T(1024)}, f32[166080]{0:T(1024)}) fusion(f32[166080]{0:T(1024)S(1)} %copy-done.34, f32[166080]{0:T(1024)S(1)} %copy-done.16, f32[166080]{0:T(1024)S(1)} %get-tuple-element.253, f32[]{:T(128)S(6)} %min_shard_map.3, f32[166080]{0:T(1024)S(1)} %copy-done.35, f32[166080]{0:T(1024)} %param.23), kind=kLoop, calls=%fused_computation.21 | loop fusion | flops 2989440 | bytes 5978884 | tf_op jit(solution)/shard_map/add | solution.py:75
  303.0 1.2 multiply_add_fusion.3
  (239 shorter events, 31.6 us)
Async XLA Ops:
  2.0 9.6 %collective-permute-start = (bf16[624,128]{1,0:T(8,128)(2,1)S(1)}, bf16[624,128]{1,0:T(8,128)(2,1)S(1)}, u32[]{:S(2)}, u32[]{:S(2)}) collective-permute-start(bf16[624,128]{1,0:T(8,128)(2,1)S(1)} %fusion.5), channel_id=1, source_target_pairs={{0,8},{1,9},{2,10},{3,11},{4,12},{5,13},{6,14},{7,15},{8,0},{9,1},... | collective-permute-start | bytes 479240 | tf_op jit(solution)/shard_map/ppermute | solution.py:111
  5.1 14.8 %collective-permute-start.1 = (bf16[624,128]{1,0:T(8,128)(2,1)S(1)}, bf16[624,128]{1,0:T(8,128)(2,1)S(1)}, u32[]{:S(2)}, u32[]{:S(2)}) collective-permute-start(bf16[624,128]{1,0:T(8,128)(2,1)S(1)} %fusion.5), channel_id=1, source_target_pairs={{0,16},{1,17},{2,18},{3,19},{4,20},{5,21},{6,22},{7,23},{8,24},{9,... | collective-permute-start | bytes 479240 | tf_op jit(solution)/shard_map/ppermute | solution.py:111
  7.7 12.2 %collective-permute-start.2 = (bf16[624,128]{1,0:T(8,128)(2,1)S(1)}, bf16[624,128]{1,0:T(8,128)(2,1)S(1)}, u32[]{:S(2)}, u32[]{:S(2)}) collective-permute-start(bf16[624,128]{1,0:T(8,128)(2,1)S(1)} %fusion.5), channel_id=1, source_target_pairs={{0,24},{1,25},{2,26},{3,27},{4,28},{5,29},{6,30},{7,31},{8,16},{9,... | collective-permute-start | bytes 479240 | tf_op jit(solution)/shard_map/ppermute | solution.py:111
  20.0 13.7 %collective-permute-start.4 = (bf16[4,624,128]{2,1,0:T(8,128)(2,1)S(1)}, bf16[4,624,128]{2,1,0:T(8,128)(2,1)S(1)}, u32[]{:S(2)}, u32[]{:S(2)}) collective-permute-start(bf16[4,624,128]{2,1,0:T(8,128)(2,1)S(1)} %pad_maximum_fusion.2.refs_0_), channel_id=1, source_target_pairs={{0,4},{1,5},{2,6},{3,7},{4,0},{5,1},{6,2},{7,3},{8,12},{9,13},{10,... | collective-permute-start | bytes 1916936 | tf_op jit(solution)/shard_map/ppermute | solution.py:111
  21.6 14.5 %collective-permute-start.3 = (bf16[4,624,128]{2,1,0:T(8,128)(2,1)S(1)}, bf16[4,624,128]{2,1,0:T(8,128)(2,1)S(1)}, u32[]{:S(2)}, u32[]{:S(2)}) collective-permute-start(bf16[4,624,128]{2,1,0:T(8,128)(2,1)S(1)} %pad_maximum_fusion.2.refs_0_), channel_id=1, source_target_pairs={{0,2},{1,3},{2,0},{3,1},{4,6},{5,7},{6,4},{7,5},{8,10},{9,11},{10,... | collective-permute-start | bytes 1916936 | tf_op jit(solution)/shard_map/ppermute | solution.py:111
  23.3 19.6 %collective-permute-start.12 = (bf16[1312,128]{1,0:T(8,128)(2,1)S(1)}, bf16[1312,128]{1,0:T(8,128)(2,1)S(1)}, u32[]{:S(2)}, u32[]{:S(2)}) collective-permute-start(bf16[1312,128]{1,0:T(8,128)(2,1)S(1)} %fusion), channel_id=1, source_target_pairs={{0,8},{1,9},{2,10},{3,11},{4,12},{5,13},{6,14},{7,15},{8,0},{9,1},... | collective-permute-start | bytes 1007624 | tf_op jit(solution)/shard_map/ppermute | solution.py:111
  26.0 26.1 %collective-permute-start.13 = (bf16[1312,128]{1,0:T(8,128)(2,1)S(1)}, bf16[1312,128]{1,0:T(8,128)(2,1)S(1)}, u32[]{:S(2)}, u32[]{:S(2)}) collective-permute-start(bf16[1312,128]{1,0:T(8,128)(2,1)S(1)} %fusion), channel_id=1, source_target_pairs={{0,16},{1,17},{2,18},{3,19},{4,20},{5,21},{6,22},{7,23},{8,24},{9,... | collective-permute-start | bytes 1007624 | tf_op jit(solution)/shard_map/ppermute | solution.py:111
  27.1 25.0 %collective-permute-start.14 = (bf16[1312,128]{1,0:T(8,128)(2,1)S(1)}, bf16[1312,128]{1,0:T(8,128)(2,1)S(1)}, u32[]{:S(2)}, u32[]{:S(2)}) collective-permute-start(bf16[1312,128]{1,0:T(8,128)(2,1)S(1)} %fusion), channel_id=1, source_target_pairs={{0,24},{1,25},{2,26},{3,27},{4,28},{5,29},{6,30},{7,31},{8,16},{9,... | collective-permute-start | bytes 1007624 | tf_op jit(solution)/shard_map/ppermute | solution.py:111
  34.5 18.9 %collective-permute-start.5 = (bf16[2,624,128]{2,1,0:T(8,128)(2,1)}, bf16[2,624,128]{2,1,0:T(8,128)(2,1)}, u32[]{:S(2)}, u32[]{:S(2)}) collective-permute-start(bf16[2,624,128]{2,1,0:T(8,128)(2,1)} %slice.74), channel_id=1, source_target_pairs={{0,2},{1,3},{2,0},{3,1},{4,6},{5,7},{6,4},{7,5},{8,10},{9,11},{10,... | collective-permute-start | bytes 958472 | tf_op jit(solution)/shard_map/ppermute | solution.py:111
  36.9 16.5 %collective-permute-start.6 = (bf16[2,624,128]{2,1,0:T(8,128)(2,1)}, bf16[2,624,128]{2,1,0:T(8,128)(2,1)}, u32[]{:S(2)}, u32[]{:S(2)}) collective-permute-start(bf16[2,624,128]{2,1,0:T(8,128)(2,1)} %slice.75), channel_id=1, source_target_pairs={{0,4},{1,5},{2,6},{3,7},{4,0},{5,1},{6,2},{7,3},{8,12},{9,13},{10,... | collective-permute-start | bytes 958472 | tf_op jit(solution)/shard_map/ppermute | solution.py:111
  43.0 13.7 %collective-permute-start.7 = (bf16[4,624,128]{2,1,0:T(8,128)(2,1)S(1)}, bf16[4,624,128]{2,1,0:T(8,128)(2,1)}, u32[]{:S(2)}, u32[]{:S(2)}) collective-permute-start(bf16[4,624,128]{2,1,0:T(8,128)(2,1)S(1)} %pad_maximum_fusion.2.refs_0_), channel_id=1, source_target_pairs={{0,1},{1,0},{2,3},{3,2},{4,5},{5,4},{6,7},{7,6},{8,9},{9,8},{10,11... | collective-permute-start | bytes 1916936 | tf_op jit(solution)/shard_map/ppermute | solution.py:111
  52.1 6.1 %collective-permute-start.8 = (bf16[4,624,128]{2,1,0:T(8,128)(2,1)S(1)}, bf16[4,624,128]{2,1,0:T(8,128)(2,1)}, u32[]{:S(2)}, u32[]{:S(2)}) collective-permute-start(bf16[4,624,128]{2,1,0:T(8,128)(2,1)S(1)} %collective-permute-done.3.refs_1_), channel_id=1, source_target_pairs={{0,1},{1,0},{2,3},{3,2},{4,5},{5,4},{6,7},{7,6},{8,9},{9,8},{10,11... | collective-permute-start | bytes 1916936 | tf_op jit(solution)/shard_map/ppermute | solution.py:111
  52.1 7.6 %collective-permute-start.9 = (bf16[4,624,128]{2,1,0:T(8,128)(2,1)S(1)}, bf16[4,624,128]{2,1,0:T(8,128)(2,1)}, u32[]{:S(2)}, u32[]{:S(2)}) collective-permute-start(bf16[4,624,128]{2,1,0:T(8,128)(2,1)S(1)} %collective-permute-done.4.refs_2_), channel_id=1, source_target_pairs={{0,1},{1,0},{2,3},{3,2},{4,5},{5,4},{6,7},{7,6},{8,9},{9,8},{10,11... | collective-permute-start | bytes 1916936 | tf_op jit(solution)/shard_map/ppermute | solution.py:111
  54.5 29.9 %collective-permute-start.16 = (bf16[2,1312,128]{2,1,0:T(8,128)(2,1)S(1)}, bf16[2,1312,128]{2,1,0:T(8,128)(2,1)}, u32[]{:S(2)}, u32[]{:S(2)}) collective-permute-start(bf16[2,1312,128]{2,1,0:T(8,128)(2,1)S(1)} %pad_maximum_fusion.1.refs_1_), channel_id=1, source_target_pairs={{0,2},{1,3},{2,0},{3,1},{4,6},{5,7},{6,4},{7,5},{8,10},{9,11},{10,... | collective-permute-start | bytes 2015240 | tf_op jit(solution)/shard_map/ppermute | solution.py:111
  55.1 29.6 %collective-permute-start.18 = (bf16[2,1312,128]{2,1,0:T(8,128)(2,1)S(1)}, bf16[2,1312,128]{2,1,0:T(8,128)(2,1)}, u32[]{:S(2)}, u32[]{:S(2)}) collective-permute-start(bf16[2,1312,128]{2,1,0:T(8,128)(2,1)S(1)} %pad_maximum_fusion.1.refs_1_), channel_id=1, source_target_pairs={{0,4},{1,5},{2,6},{3,7},{4,0},{5,1},{6,2},{7,3},{8,12},{9,13},{10,... | collective-permute-start | bytes 2015240 | tf_op jit(solution)/shard_map/ppermute | solution.py:111
  56.6 29.4 %collective-permute-start.15 = (bf16[2,1312,128]{2,1,0:T(8,128)(2,1)S(1)}, bf16[2,1312,128]{2,1,0:T(8,128)(2,1)}, u32[]{:S(2)}, u32[]{:S(2)}) collective-permute-start(bf16[2,1312,128]{2,1,0:T(8,128)(2,1)S(1)} %pad_maximum_fusion.refs_0_), channel_id=1, source_target_pairs={{0,2},{1,3},{2,0},{3,1},{4,6},{5,7},{6,4},{7,5},{8,10},{9,11},{10,... | collective-permute-start | bytes 2015240 | tf_op jit(solution)/shard_map/ppermute | solution.py:111
  58.2 28.1 %collective-permute-start.17 = (bf16[2,1312,128]{2,1,0:T(8,128)(2,1)S(1)}, bf16[2,1312,128]{2,1,0:T(8,128)(2,1)}, u32[]{:S(2)}, u32[]{:S(2)}) collective-permute-start(bf16[2,1312,128]{2,1,0:T(8,128)(2,1)S(1)} %pad_maximum_fusion.refs_0_), channel_id=1, source_target_pairs={{0,4},{1,5},{2,6},{3,7},{4,0},{5,1},{6,2},{7,3},{8,12},{9,13},{10,... | collective-permute-start | bytes 2015240 | tf_op jit(solution)/shard_map/ppermute | solution.py:111
  63.4 25.0 %collective-permute-start.22 = (bf16[2,1312,128]{2,1,0:T(8,128)(2,1)S(1)}, bf16[2,1312,128]{2,1,0:T(8,128)(2,1)S(1)}, u32[]{:S(2)}, u32[]{:S(2)}) collective-permute-start(bf16[2,1312,128]{2,1,0:T(8,128)(2,1)S(1)} %pad_maximum_fusion.1.refs_1_), channel_id=1, source_target_pairs={{0,1},{1,0},{2,3},{3,2},{4,5},{5,4},{6,7},{7,6},{8,9},{9,8},{10,11... | collective-permute-start | bytes 2015240 | tf_op jit(solution)/shard_map/ppermute | solution.py:111
  84.4 4.4 %collective-permute-start.21 = (bf16[2,1312,128]{2,1,0:T(8,128)(2,1)S(1)}, bf16[2,1312,128]{2,1,0:T(8,128)(2,1)S(1)}, u32[]{:S(2)}, u32[]{:S(2)}) collective-permute-start(bf16[2,1312,128]{2,1,0:T(8,128)(2,1)S(1)} %pad_maximum_fusion.refs_0_), channel_id=1, source_target_pairs={{0,1},{1,0},{2,3},{3,2},{4,5},{5,4},{6,7},{7,6},{8,9},{9,8},{10,11... | collective-permute-start | bytes 2015240 | tf_op jit(solution)/shard_map/ppermute | solution.py:111
  86.3 16.2 %collective-permute-start.19 = (bf16[2,1312,128]{2,1,0:T(8,128)(2,1)}, bf16[2,1312,128]{2,1,0:T(8,128)(2,1)S(1)}, u32[]{:S(2)}, u32[]{:S(2)}) collective-permute-start(bf16[2,1312,128]{2,1,0:T(8,128)(2,1)} %collective-permute-done.17.refs_4_), channel_id=1, source_target_pairs={{0,2},{1,3},{2,0},{3,1},{4,6},{5,7},{6,4},{7,5},{8,10},{9,11},{10,... | collective-permute-start | bytes 2015240 | tf_op jit(solution)/shard_map/ppermute | solution.py:111
  87.8 15.8 %collective-permute-start.20 = (bf16[2,1312,128]{2,1,0:T(8,128)(2,1)}, bf16[2,1312,128]{2,1,0:T(8,128)(2,1)S(1)}, u32[]{:S(2)}, u32[]{:S(2)}) collective-permute-start(bf16[2,1312,128]{2,1,0:T(8,128)(2,1)} %collective-permute-done.16.refs_3_), channel_id=1, source_target_pairs={{0,4},{1,5},{2,6},{3,7},{4,0},{5,1},{6,2},{7,3},{8,12},{9,13},{10,... | collective-permute-start | bytes 2015240 | tf_op jit(solution)/shard_map/ppermute | solution.py:111
  88.3 15.3 %collective-permute-start.23 = (bf16[2,1312,128]{2,1,0:T(8,128)(2,1)}, bf16[2,1312,128]{2,1,0:T(8,128)(2,1)S(1)}, u32[]{:S(2)}, u32[]{:S(2)}) collective-permute-start(bf16[2,1312,128]{2,1,0:T(8,128)(2,1)} %collective-permute-done.15.refs_2_), channel_id=1, source_target_pairs={{0,1},{1,0},{2,3},{3,2},{4,5},{5,4},{6,7},{7,6},{8,9},{9,8},{10,11... | collective-permute-start | bytes 2015240 | tf_op jit(solution)/shard_map/ppermute | solution.py:111
  88.4 15.8 %collective-permute-start.24 = (bf16[2,1312,128]{2,1,0:T(8,128)(2,1)}, bf16[2,1312,128]{2,1,0:T(8,128)(2,1)S(1)}, u32[]{:S(2)}, u32[]{:S(2)}) collective-permute-start(bf16[2,1312,128]{2,1,0:T(8,128)(2,1)} %collective-permute-done.16.refs_3_), channel_id=1, source_target_pairs={{0,1},{1,0},{2,3},{3,2},{4,5},{5,4},{6,7},{7,6},{8,9},{9,8},{10,11... | collective-permute-start | bytes 2015240 | tf_op jit(solution)/shard_map/ppermute | solution.py:111
  88.9 15.3 %collective-permute-start.25 = (bf16[2,1312,128]{2,1,0:T(8,128)(2,1)}, bf16[2,1312,128]{2,1,0:T(8,128)(2,1)S(1)}, u32[]{:S(2)}, u32[]{:S(2)}) collective-permute-start(bf16[2,1312,128]{2,1,0:T(8,128)(2,1)} %collective-permute-done.17.refs_4_), channel_id=1, source_target_pairs={{0,1},{1,0},{2,3},{3,2},{4,5},{5,4},{6,7},{7,6},{8,9},{9,8},{10,11... | collective-permute-start | bytes 2015240 | tf_op jit(solution)/shard_map/ppermute | solution.py:111
  102.6 2.3 collective-permute-start.26
  103.7 2.2 collective-permute-start.27
  103.7 3.2 %collective-permute-start.28 = (bf16[2,1312,128]{2,1,0:T(8,128)(2,1)S(1)}, bf16[2,1312,128]{2,1,0:T(8,128)(2,1)}, u32[]{:S(2)}, u32[]{:S(2)}) collective-permute-start(bf16[2,1312,128]{2,1,0:T(8,128)(2,1)S(1)} %collective-permute-done.20.refs_7_), channel_id=1, source_target_pairs={{0,1},{1,0},{2,3},{3,2},{4,5},{5,4},{6,7},{7,6},{8,9},{9,8},{10,11... | collective-permute-start | bytes 2015240 | tf_op jit(solution)/shard_map/ppermute | solution.py:111
  116.9 21.6 %collective-permute-start.32 = (f32[16,5376]{1,0:T(8,128)S(1)}, f32[16,5376]{1,0:T(8,128)S(1)}, u32[]{:S(2)}, u32[]{:S(2)}) collective-permute-start(f32[16,5376]{1,0:T(8,128)S(1)} %get-tuple-element.147.cls_own), channel_id=1, source_target_pairs={{0,1},{1,0},{2,3},{3,2},{4,5},{5,4},{6,7},{7,6},{8,9},{9,8},{10,11... | collective-permute-start | bytes 1032200 | tf_op jit(solution)/shard_map/ppermute | solution.py:111
  117.1 21.3 %collective-permute-start.29 = (bf16[16,768]{1,0:T(8,128)(2,1)S(1)}, bf16[16,768]{1,0:T(8,128)(2,1)S(1)}, u32[]{:S(2)}, u32[]{:S(2)}) collective-permute-start(bf16[16,768]{1,0:T(8,128)(2,1)S(1)} %get-tuple-element.155), channel_id=1, source_target_pairs={{0,8},{1,9},{2,10},{3,11},{4,12},{5,13},{6,14},{7,15},{8,0},{9,1},... | collective-permute-start | bytes 73736 | tf_op jit(solution)/shard_map/ppermute | solution.py:111
  122.1 16.3 %collective-permute-start.30 = (bf16[16,768]{1,0:T(8,128)(2,1)S(1)}, bf16[16,768]{1,0:T(8,128)(2,1)S(1)}, u32[]{:S(2)}, u32[]{:S(2)}) collective-permute-start(bf16[16,768]{1,0:T(8,128)(2,1)S(1)} %get-tuple-element.155), channel_id=1, source_target_pairs={{0,16},{1,17},{2,18},{3,19},{4,20},{5,21},{6,22},{7,23},{8,24},{9,... | collective-permute-start | bytes 73736 | tf_op jit(solution)/shard_map/ppermute | solution.py:111
  123.3 15.1 %collective-permute-start.31 = (bf16[16,768]{1,0:T(8,128)(2,1)S(1)}, bf16[16,768]{1,0:T(8,128)(2,1)S(1)}, u32[]{:S(2)}, u32[]{:S(2)}) collective-permute-start(bf16[16,768]{1,0:T(8,128)(2,1)S(1)} %get-tuple-element.155), channel_id=1, source_target_pairs={{0,24},{1,25},{2,26},{3,27},{4,28},{5,29},{6,30},{7,31},{8,16},{9,... | collective-permute-start | bytes 73736 | tf_op jit(solution)/shard_map/ppermute | solution.py:111
  138.4 13.7 %collective-permute-start.37 = (bf16[512,3072]{1,0:T(8,128)(2,1)S(1)}, bf16[512,3072]{1,0:T(8,128)(2,1)S(1)}, u32[]{:S(2)}, u32[]{:S(2)}) collective-permute-start(bf16[512,3072]{1,0:T(8,128)(2,1)S(1)} %get-tuple-element.159.refs_6_), channel_id=1, source_target_pairs={{0,1},{1,0},{2,3},{3,2},{4,5},{5,4},{6,7},{7,6},{8,9},{9,8},{10,11... | collective-permute-start | bytes 9437192 | tf_op jit(solution)/shard_map/ppermute | solution.py:111
  138.5 13.6 %collective-permute-start.38 = (bf16[512,768]{1,0:T(8,128)(2,1)S(1)}, bf16[512,768]{1,0:T(8,128)(2,1)S(1)}, u32[]{:S(2)}, u32[]{:S(2)}) collective-permute-start(bf16[512,768]{1,0:T(8,128)(2,1)S(1)} %get-tuple-element.148.down_ref.refs_4_), channel_id=1, source_target_pairs={{0,1},{1,0},{2,3},{3,2},{4,5},{5,4},{6,7},{7,6},{8,9},{9,8},{10,11... | collective-permute-start | bytes 2359304 | tf_op jit(solution)/shard_map/ppermute | solution.py:111
  139.0 13.0 %collective-permute-start.34 = (bf16[4,16,768]{2,1,0:T(8,128)(2,1)S(1)}, bf16[4,16,768]{2,1,0:T(8,128)(2,1)S(1)}, u32[]{:S(2)}, u32[]{:S(2)}) collective-permute-start(bf16[4,16,768]{2,1,0:T(8,128)(2,1)S(1)} %pad_maximum_fusion.6), channel_id=1, source_target_pairs={{0,2},{1,3},{2,0},{3,1},{4,6},{5,7},{6,4},{7,5},{8,10},{9,11},{10,... | collective-permute-start | bytes 294920 | tf_op jit(solution)/shard_map/ppermute | solution.py:111
  141.1 11.0 %collective-permute-start.35 = (bf16[4,16,768]{2,1,0:T(8,128)(2,1)S(1)}, bf16[4,16,768]{2,1,0:T(8,128)(2,1)S(1)}, u32[]{:S(2)}, u32[]{:S(2)}) collective-permute-start(bf16[4,16,768]{2,1,0:T(8,128)(2,1)S(1)} %pad_maximum_fusion.6), channel_id=1, source_target_pairs={{0,4},{1,5},{2,6},{3,7},{4,0},{5,1},{6,2},{7,3},{8,12},{9,13},{10,... | collective-permute-start | bytes 294920 | tf_op jit(solution)/shard_map/ppermute | solution.py:111
  141.6 10.5 %collective-permute-start.36 = (bf16[4,16,768]{2,1,0:T(8,128)(2,1)S(1)}, bf16[4,16,768]{2,1,0:T(8,128)(2,1)S(1)}, u32[]{:S(2)}, u32[]{:S(2)}) collective-permute-start(bf16[4,16,768]{2,1,0:T(8,128)(2,1)S(1)} %pad_maximum_fusion.6), channel_id=1, source_target_pairs={{0,6},{1,7},{2,4},{3,5},{4,2},{5,3},{6,0},{7,1},{8,14},{9,15},{10,... | collective-permute-start | bytes 294920 | tf_op jit(solution)/shard_map/ppermute | solution.py:111
  154.0 10.0 %collective-permute-start.40 = (bf16[512,3072]{1,0:T(8,128)(2,1)S(1)}, bf16[512,3072]{1,0:T(8,128)(2,1)S(1)}, u32[]{:S(2)}, u32[]{:S(2)}) collective-permute-start(bf16[512,3072]{1,0:T(8,128)(2,1)S(1)} %get-tuple-element.165.refs_2_), channel_id=1, source_target_pairs={{0,1},{1,0},{2,3},{3,2},{4,5},{5,4},{6,7},{7,6},{8,9},{9,8},{10,11... | collective-permute-start | bytes 9437192 | tf_op jit(solution)/shard_map/ppermute | solution.py:111
  154.1 9.8 %collective-permute-start.33 = (bf16[512,768]{1,0:T(8,128)(2,1)S(1)}, bf16[512,768]{1,0:T(8,128)(2,1)S(1)}, u32[]{:S(2)}, u32[]{:S(2)}) collective-permute-start(bf16[512,768]{1,0:T(8,128)(2,1)S(1)} %copy-done.2), channel_id=1, source_target_pairs={{0,1},{1,0},{2,3},{3,2},{4,5},{5,4},{6,7},{7,6},{8,9},{9,8},{10,11... | collective-permute-start | bytes 2359304 | tf_op jit(solution)/shard_map/ppermute | solution.py:111
  154.5 9.5 %collective-permute-start.41 = (f32[8,768]{1,0:T(8,128)S(1)}, f32[8,768]{1,0:T(8,128)S(1)}, u32[]{:S(2)}, u32[]{:S(2)}) collective-permute-start(f32[8,768]{1,0:T(8,128)S(1)} %get-tuple-element.173.refs_11_), channel_id=1, source_target_pairs={{0,1},{1,0},{2,3},{3,2},{4,5},{5,4},{6,7},{7,6},{8,9},{9,8},{10,11... | collective-permute-start | bytes 73736 | tf_op jit(solution)/shard_map/ppermute | solution.py:111
  178.3 19.0 %collective-permute-start.42 = (bf16[2,1312,128]{2,1,0:T(8,128)(2,1)}, bf16[2,1312,128]{2,1,0:T(8,128)(2,1)}, u32[]{:S(2)}, u32[]{:S(2)}) collective-permute-start(bf16[2,1312,128]{2,1,0:T(8,128)(2,1)} %get-tuple-element.192), channel_id=1, source_target_pairs={{0,2},{1,3},{2,0},{3,1},{4,6},{5,7},{6,4},{7,5},{8,10},{9,11},{10,... | collective-permute-start | bytes 2015240 | tf_op jit(solution)/shard_map/ppermute | solution.py:111
  180.3 18.1 %collective-permute-start.43 = (bf16[2,1312,128]{2,1,0:T(8,128)(2,1)}, bf16[2,1312,128]{2,1,0:T(8,128)(2,1)S(1)}, u32[]{:S(2)}, u32[]{:S(2)}) collective-permute-start(bf16[2,1312,128]{2,1,0:T(8,128)(2,1)} %get-tuple-element.193), channel_id=1, source_target_pairs={{0,4},{1,5},{2,6},{3,7},{4,0},{5,1},{6,2},{7,3},{8,12},{9,13},{10,... | collective-permute-start | bytes 2015240 | tf_op jit(solution)/shard_map/ppermute | solution.py:111
  180.8 35.2 %collective-permute-start.45 = (bf16[2,1312,128]{2,1,0:T(8,128)(2,1)}, bf16[2,1312,128]{2,1,0:T(8,128)(2,1)S(1)}, u32[]{:S(2)}, u32[]{:S(2)}) collective-permute-start(bf16[2,1312,128]{2,1,0:T(8,128)(2,1)} %get-tuple-element.220), channel_id=1, source_target_pairs={{0,4},{1,5},{2,6},{3,7},{4,0},{5,1},{6,2},{7,3},{8,12},{9,13},{10,... | collective-permute-start | bytes 2015240 | tf_op jit(solution)/shard_map/ppermute | solution.py:111
  199.5 16.5 %collective-permute-start.44 = (bf16[2,1312,128]{2,1,0:T(8,128)(2,1)}, bf16[2,1312,128]{2,1,0:T(8,128)(2,1)}, u32[]{:S(2)}, u32[]{:S(2)}) collective-permute-start(bf16[2,1312,128]{2,1,0:T(8,128)(2,1)} %add_convert_fusion.2), channel_id=1, source_target_pairs={{0,2},{1,3},{2,0},{3,1},{4,6},{5,7},{6,4},{7,5},{8,10},{9,11},{10,... | collective-permute-start | bytes 2015240 | tf_op jit(solution)/shard_map/ppermute | solution.py:111
  216.0 2.7 collective-permute-start.50
  216.0 4.7 %collective-permute-start.49 = (bf16[2,624,128]{2,1,0:T(8,128)(2,1)}, bf16[2,624,128]{2,1,0:T(8,128)(2,1)S(1)}, u32[]{:S(2)}, u32[]{:S(2)}) collective-permute-start(bf16[2,624,128]{2,1,0:T(8,128)(2,1)} %get-tuple-element.228), channel_id=1, source_target_pairs={{0,1},{1,0},{2,3},{3,2},{4,5},{5,4},{6,7},{7,6},{8,9},{9,8},{10,11... | collective-permute-start | bytes 958472 | tf_op jit(solution)/shard_map/ppermute | solution.py:111
  216.5 4.9 %collective-permute-start.48 = (bf16[4,624,128]{2,1,0:T(8,128)(2,1)}, bf16[4,624,128]{2,1,0:T(8,128)(2,1)S(1)}, u32[]{:S(2)}, u32[]{:S(2)}) collective-permute-start(bf16[4,624,128]{2,1,0:T(8,128)(2,1)} %get-tuple-element.226), channel_id=1, source_target_pairs={{0,1},{1,0},{2,3},{3,2},{4,5},{5,4},{6,7},{7,6},{8,9},{9,8},{10,11... | collective-permute-start | bytes 1916936 | tf_op jit(solution)/shard_map/ppermute | solution.py:111
  216.6 7.1 %collective-permute-start.47 = (bf16[4,624,128]{2,1,0:T(8,128)(2,1)}, bf16[4,624,128]{2,1,0:T(8,128)(2,1)S(1)}, u32[]{:S(2)}, u32[]{:S(2)}) collective-permute-start(bf16[4,624,128]{2,1,0:T(8,128)(2,1)} %get-tuple-element.224), channel_id=1, source_target_pairs={{0,1},{1,0},{2,3},{3,2},{4,5},{5,4},{6,7},{7,6},{8,9},{9,8},{10,11... | collective-permute-start | bytes 1916936 | tf_op jit(solution)/shard_map/ppermute | solution.py:111
  217.1 8.1 %collective-permute-start.46 = (bf16[4,624,128]{2,1,0:T(8,128)(2,1)}, bf16[4,624,128]{2,1,0:T(8,128)(2,1)S(1)}, u32[]{:S(2)}, u32[]{:S(2)}) collective-permute-start(bf16[4,624,128]{2,1,0:T(8,128)(2,1)} %get-tuple-element.222), channel_id=1, source_target_pairs={{0,1},{1,0},{2,3},{3,2},{4,5},{5,4},{6,7},{7,6},{8,9},{9,8},{10,11... | collective-permute-start | bytes 1916936 | tf_op jit(solution)/shard_map/ppermute | solution.py:111
  218.7 17.7 %collective-permute-start.51 = (bf16[2,1312,128]{2,1,0:T(8,128)(2,1)S(1)}, bf16[2,1312,128]{2,1,0:T(8,128)(2,1)S(1)}, u32[]{:S(2)}, u32[]{:S(2)}) collective-permute-start(bf16[2,1312,128]{2,1,0:T(8,128)(2,1)S(1)} %copy-done.50), channel_id=1, source_target_pairs={{0,2},{1,3},{2,0},{3,1},{4,6},{5,7},{6,4},{7,5},{8,10},{9,11},{10,... | collective-permute-start | bytes 2015240 | tf_op jit(solution)/shard_map/ppermute | solution.py:111
  220.8 17.2 %collective-permute-start.52 = (bf16[2,1312,128]{2,1,0:T(8,128)(2,1)S(1)}, bf16[2,1312,128]{2,1,0:T(8,128)(2,1)S(1)}, u32[]{:S(2)}, u32[]{:S(2)}) collective-permute-start(bf16[2,1312,128]{2,1,0:T(8,128)(2,1)S(1)} %add_convert_fusion.3), channel_id=1, source_target_pairs={{0,4},{1,5},{2,6},{3,7},{4,0},{5,1},{6,2},{7,3},{8,12},{9,13},{10,... | collective-permute-start | bytes 2015240 | tf_op jit(solution)/shard_map/ppermute | solution.py:111
  221.4 29.3 %collective-permute-start.61 = (bf16[1312,128]{1,0:T(8,128)(2,1)S(1)}, bf16[1312,128]{1,0:T(8,128)(2,1)S(1)}, u32[]{:S(2)}, u32[]{:S(2)}) collective-permute-start(bf16[1312,128]{1,0:T(8,128)(2,1)S(1)} %get-tuple-element.260), channel_id=1, source_target_pairs={{0,16},{1,17},{2,18},{3,19},{4,20},{5,21},{6,22},{7,23},{8,24},{9,... | collective-permute-start | bytes 1007624 | tf_op jit(solution)/shard_map/ppermute | solution.py:111
  223.8 27.0 %collective-permute-start.62 = (bf16[1312,128]{1,0:T(8,128)(2,1)S(1)}, bf16[1312,128]{1,0:T(8,128)(2,1)S(1)}, u32[]{:S(2)}, u32[]{:S(2)}) collective-permute-start(bf16[1312,128]{1,0:T(8,128)(2,1)S(1)} %get-tuple-element.261), channel_id=1, source_target_pairs={{0,24},{1,25},{2,26},{3,27},{4,28},{5,29},{6,30},{7,31},{8,16},{9,... | collective-permute-start | bytes 1007624 | tf_op jit(solution)/shard_map/ppermute | solution.py:111
  238.0 8.8 %collective-permute-start.53 = (bf16[2,624,128]{2,1,0:T(8,128)(2,1)S(1)}, bf16[2,624,128]{2,1,0:T(8,128)(2,1)S(1)}, u32[]{:S(2)}, u32[]{:S(2)}) collective-permute-start(bf16[2,624,128]{2,1,0:T(8,128)(2,1)S(1)} %add_convert_fusion.10), channel_id=1, source_target_pairs={{0,4},{1,5},{2,6},{3,7},{4,0},{5,1},{6,2},{7,3},{8,12},{9,13},{10,... | collective-permute-start | bytes 958472 | tf_op jit(solution)/shard_map/ppermute | solution.py:111
  238.8 14.9 %collective-permute-start.60 = (bf16[1312,128]{1,0:T(8,128)(2,1)S(1)}, bf16[1312,128]{1,0:T(8,128)(2,1)S(1)}, u32[]{:S(2)}, u32[]{:S(2)}) collective-permute-start(bf16[1312,128]{1,0:T(8,128)(2,1)S(1)} %get-tuple-element.258), channel_id=1, source_target_pairs={{0,8},{1,9},{2,10},{3,11},{4,12},{5,13},{6,14},{7,15},{8,0},{9,1},... | collective-permute-start | bytes 1007624 | tf_op jit(solution)/shard_map/ppermute | solution.py:111
  239.8 8.7 %collective-permute-start.55 = (bf16[2,624,128]{2,1,0:T(8,128)(2,1)S(1)}, bf16[2,624,128]{2,1,0:T(8,128)(2,1)S(1)}, u32[]{:S(2)}, u32[]{:S(2)}) collective-permute-start(bf16[2,624,128]{2,1,0:T(8,128)(2,1)S(1)} %add_convert_fusion.11), channel_id=1, source_target_pairs={{0,2},{1,3},{2,0},{3,1},{4,6},{5,7},{6,4},{7,5},{8,10},{9,11},{10,... | collective-permute-start | bytes 958472 | tf_op jit(solution)/shard_map/ppermute | solution.py:111
  247.0 14.8 %collective-permute-start.54 = (bf16[4,624,128]{2,1,0:T(8,128)(2,1)S(1)}, bf16[4,624,128]{2,1,0:T(8,128)(2,1)S(1)}, u32[]{:S(2)}, u32[]{:S(2)}) collective-permute-start(bf16[4,624,128]{2,1,0:T(8,128)(2,1)S(1)} %pad_maximum_fusion.3), channel_id=1, source_target_pairs={{0,2},{1,3},{2,0},{3,1},{4,6},{5,7},{6,4},{7,5},{8,10},{9,11},{10,... | collective-permute-start | bytes 1916936 | tf_op jit(solution)/shard_map/ppermute | solution.py:111
  248.6 14.8 %collective-permute-start.56 = (bf16[4,624,128]{2,1,0:T(8,128)(2,1)S(1)}, bf16[4,624,128]{2,1,0:T(8,128)(2,1)S(1)}, u32[]{:S(2)}, u32[]{:S(2)}) collective-permute-start(bf16[4,624,128]{2,1,0:T(8,128)(2,1)S(1)} %pad_maximum_fusion.4), channel_id=1, source_target_pairs={{0,4},{1,5},{2,6},{3,7},{4,0},{5,1},{6,2},{7,3},{8,12},{9,13},{10,... | collective-permute-start | bytes 1916936 | tf_op jit(solution)/shard_map/ppermute | solution.py:111
  263.7 6.4 %collective-permute-start.57 = (bf16[624,128]{1,0:T(8,128)(2,1)S(1)}, bf16[624,128]{1,0:T(8,128)(2,1)S(1)}, u32[]{:S(2)}, u32[]{:S(2)}) collective-permute-start(bf16[624,128]{1,0:T(8,128)(2,1)S(1)} %get-tuple-element.262), channel_id=1, source_target_pairs={{0,8},{1,9},{2,10},{3,11},{4,12},{5,13},{6,14},{7,15},{8,0},{9,1},... | collective-permute-start | bytes 479240 | tf_op jit(solution)/shard_map/ppermute | solution.py:111
  264.6 12.3 %collective-permute-start.58 = (bf16[624,128]{1,0:T(8,128)(2,1)S(1)}, bf16[624,128]{1,0:T(8,128)(2,1)S(1)}, u32[]{:S(2)}, u32[]{:S(2)}) collective-permute-start(bf16[624,128]{1,0:T(8,128)(2,1)S(1)} %get-tuple-element.264), channel_id=1, source_target_pairs={{0,16},{1,17},{2,18},{3,19},{4,20},{5,21},{6,22},{7,23},{8,24},{9,... | collective-permute-start | bytes 479240 | tf_op jit(solution)/shard_map/ppermute | solution.py:111
  266.7 10.2 %collective-permute-start.59 = (bf16[624,128]{1,0:T(8,128)(2,1)S(1)}, bf16[624,128]{1,0:T(8,128)(2,1)S(1)}, u32[]{:S(2)}, u32[]{:S(2)}) collective-permute-start(bf16[624,128]{1,0:T(8,128)(2,1)S(1)} %get-tuple-element.263), channel_id=1, source_target_pairs={{0,24},{1,25},{2,26},{3,27},{4,28},{5,29},{6,30},{7,31},{8,16},{9,... | collective-permute-start | bytes 479240 | tf_op jit(solution)/shard_map/ppermute | solution.py:111
  281.0 3.7 %collective-permute-start.64 = (f32[]{:T(128)}, f32[]{:T(128)}, u32[]{:S(2)}, u32[]{:S(2)}) collective-permute-start(f32[]{:T(128)} %add.205), channel_id=1, source_target_pairs={{0,2},{1,3},{2,0},{3,1},{4,6},{5,7},{6,4},{7,5},{8,10},{9,11},{10,... | collective-permute-start | bytes 20 | tf_op jit(solution)/shard_map/ppermute | solution.py:111
  285.3 3.7 %collective-permute-start.65 = (f32[]{:T(128)}, f32[]{:T(128)}, u32[]{:S(2)}, u32[]{:S(2)}) collective-permute-start(f32[]{:T(128)} %add.206), channel_id=1, source_target_pairs={{0,4},{1,5},{2,6},{3,7},{4,0},{5,1},{6,2},{7,3},{8,12},{9,13},{10,... | collective-permute-start | bytes 20 | tf_op jit(solution)/shard_map/ppermute | solution.py:111
  289.6 4.0 %collective-permute-start.66 = (f32[]{:T(128)}, f32[]{:T(128)}, u32[]{:S(2)}, u32[]{:S(2)}) collective-permute-start(f32[]{:T(128)} %add.207), channel_id=1, source_target_pairs={{0,8},{1,9},{2,10},{3,11},{4,12},{5,13},{6,14},{7,15},{8,0},{9,1},... | collective-permute-start | bytes 20 | tf_op jit(solution)/shard_map/ppermute | solution.py:111
  294.1 5.0 %collective-permute-start.67 = (f32[]{:T(128)}, f32[]{:T(128)}, u32[]{:S(2)}, u32[]{:S(2)}) collective-permute-start(f32[]{:T(128)} %add.208), channel_id=1, source_target_pairs={{0,16},{1,17},{2,18},{3,19},{4,20},{5,21},{6,22},{7,23},{8,24},{9,... | collective-permute-start | bytes 20 | tf_op jit(solution)/shard_map/ppermute | solution.py:111
  (58 other events, 723.1 us)

commit v3 on v2

--- a/solution.py
+++ b/solution.py
@@ -954,7 +954,8 @@
     positive = jnp.sum(jnp.where(diagonal, table, 0.0), axis=-1, keepdims=True)
     row_one = lax.broadcasted_iota(jnp.int32, (total, 1), 0)
     anchors = ((row_one & (n - 1)) < half) & (positive > 0.5 * masked_scores)
-    loss_ref[0, 0] = jnp.sum(jnp.where(anchors, row_lse - positive, 0.0))
+    count = 0.5 * jnp.sum(valid_ref[...])
+    loss_ref[0, 0] = jnp.sum(jnp.where(anchors, row_lse - positive, 0.0)) / count
     slope = (jnp.exp(table - row_lse) - jnp.where(diagonal, 1.0, 0.0)) * (1.0 / logit_divisor)
     sims[...] = jnp.where(anchors, slope, 0.0).astype(jnp.bfloat16)
     back[...] = plain_rows(sims[...], everyone, TN)
@@ -1219,7 +1220,7 @@
     units = jnp.stack(unit_lines)
     units_sib = swap(units, CORE)
     up_sib, parts_sib = swap(after(up_low, units_sib), CORE), swap(parts, CORE)
-    loss_sum, d_first_cls, cls_grads, cls_low, cls_part = pooled_backward(
+    loss, d_first_cls, cls_grads, cls_low, cls_part = pooled_backward(
         device, (units, units_sib), head_mats, (cls, cls_sib), valid_row, head_vecs
     )
     head_pieces = head_grads(
@@ -1232,7 +1233,7 @@
         cls_part,
         (parts, parts_sib),
     )
-    loss_sum = loss_sum[0, 0]
+    loss = loss[0, 0]
     d_first, head_pieces = lax.optimization_barrier((d_first, head_pieces))
     line_low, line_high, x_low, x_high, y_low, y_high, d_low, d_high = head_pieces
     d_low, d_high = swap(d_low, XBIT), swap(d_high, YBIT)
@@ -1272,7 +1273,6 @@
     attn_share = unpack_shard(scatter_attn(attn_sums), device, shards[0])
     squares = jnp.sum(attn_share * attn_share) + jnp.sum(head_share * head_share)
     total_squares = sum_small(squares)
-    loss = loss_sum / jnp.sum(valid_everything)
     grad_norm = jnp.sqrt(total_squares)
     clip_scale = jnp.minimum(1.0, clip_bound / grad_norm)
     attn_new = adam_step(attn_share * clip_scale, attn_params, attn_moment, attn_second, attn_ema)

time: 310 us -> 308 us (level)
  transfers between devices with their start and end apart: 68 -> 68, of which waited for: 29 -> 31; matrix products, arithmetic and copies ran while one was open for 5% -> 4% of each run, Pallas kernels for 26% -> 26%
where the time goes in v3:
time: 308 us; the launch traced here: 304 us
  Pallas kernels  103 us (33%)
  waiting for transfers between devices  93 us (30%)
  starting transfers between devices  72.5 us (24%)
  other arithmetic  17.3 us (6%)
  between operations  11.7 us (4%)
  local copies, waits for them, and re-layouts  6.45 us (2%)
    ppermute x68, waiting for transfers between devices, swap(): return lax.ppermute(value, 'sent', [(i, i ^ bit) for i in range(count)])  93 us
    ppermute x68, starting transfers between devices, swap(): return lax.ppermute(value, 'sent', [(i, i ^ bit) for i in range(count)])  72.5 us
    pallas_call x1, Pallas kernels, attn_forward(): pl.pallas_call(functools.partial(attn_kernel, shard), out_shape=tuple((ja...  20.3 us
    pallas_call x1, Pallas kernels, head_grads(): pl.pallas_call(functools.partial(head_grad_kernel, shard), out_shape=tupl...  14.3 us
    pallas_call x1, Pallas kernels, attn_grads(): pl.pallas_call(functools.partial(attn_grad_kernel, shard), out_shape=(jax...  12.9 us
    pallas_call x1, Pallas kernels, head_forward(): pl.pallas_call(forward_kernel, out_shape=(result((both, 4 * D), low, True...  12.4 us
    pallas_call x1, Pallas kernels, make_head(): pl.pallas_call(functools.partial(head_kernel, shard), out_shape=(result((...  9.96 us
    pallas_call x1, Pallas kernels, head_backward(): pl.pallas_call(backward_kernel, out_shape=(result((both, 4 * D), low, Tru...  9.42 us
  transfers between devices with their start and end apart: 68, of which 31 were waited for; matrix products, arithmetic and copies ran while one was open for 4% of the time, Pallas kernels for 26%

profile of v3, /device:TPU:0, one launch (start us, length us, event | category | flops | bytes accessed | tf_op | source)
XLA Modules:
  0.0 304.3 jit_solution(3877766789531672514)
XLA Ops:
  0.7 1.2 select_bitcast_fusion.1
  2.0 3.1 %collective-permute-start = (bf16[624,128]{1,0:T(8,128)(2,1)S(1)}, bf16[624,128]{1,0:T(8,128)(2,1)S(1)}, u32[]{:S(2)}, u32[]{:S(2)}) collective-permute-start(bf16[624,128]{1,0:T(8,128)(2,1)S(1)} %fusion.5), channel_id=1, source_target_pairs={{0,8},{1,9},{2,10},{3,11},{4,12},{5,13},{6,14},{7,15},{8,0},{9,1},... | collective-permute-start | bytes 479240 | tf_op jit(solution)/shard_map/ppermute | solution.py:111
  5.1 2.6 collective-permute-start.1
  7.7 3.8 %collective-permute-done = bf16[624,128]{1,0:T(8,128)(2,1)S(1)} collective-permute-done((bf16[624,128]{1,0:T(8,128)(2,1)S(1)}, bf16[624,128]{1,0:T(8,128)(2,1)S(1)}, u32[]{:S(2)}, u32[]{:S(2)}) %collective-permute-start) | collective-permute-done | bytes 159776 | tf_op jit(solution)/shard_map/ppermute | solution.py:111
  11.6 8.3 %collective-permute-done.1 = bf16[624,128]{1,0:T(8,128)(2,1)S(1)} collective-permute-done((bf16[624,128]{1,0:T(8,128)(2,1)S(1)}, bf16[624,128]{1,0:T(8,128)(2,1)S(1)}, u32[]{:S(2)}, u32[]{:S(2)}) %collective-permute-start.1) | collective-permute-done | bytes 159776 | tf_op jit(solution)/shard_map/ppermute | solution.py:111
  20.0 1.6 collective-permute-start.4
  21.6 1.5 collective-permute-start.3
  23.3 2.6 collective-permute-start.12
  26.0 1.1 collective-permute-start.13
  27.1 1.4 collective-permute-start.14
  28.4 5.2 %collective-permute-done.4.refs_2_ = bf16[4,624,128]{2,1,0:T(8,128)(2,1)S(1)} collective-permute-done((bf16[4,624,128]{2,1,0:T(8,128)(2,1)S(1)}, bf16[4,624,128]{2,1,0:T(8,128)(2,1)S(1)}, u32[]{:S(2)}, u32[]{:S(2)}) %collective-permute-start.4) | collective-permute-done | bytes 639008 | tf_op jit(solution)/shard_map/ppermute | solution.py:111
  34.5 1.5 collective-permute-start.5
  36.9 1.4 collective-permute-start.6
  43.3 8.8 %collective-permute-done.13 = bf16[1312,128]{1,0:T(8,128)(2,1)S(1)} collective-permute-done((bf16[1312,128]{1,0:T(8,128)(2,1)S(1)}, bf16[1312,128]{1,0:T(8,128)(2,1)S(1)}, u32[]{:S(2)}, u32[]{:S(2)}) %collective-permute-start.13) | collective-permute-done | bytes 335904 | tf_op jit(solution)/shard_map/ppermute | solution.py:111
  53.4 1.0 pad_maximum_fusion.1.refs_1_
  55.6 1.0 pad_maximum_fusion.refs_0_
  56.6 1.6 collective-permute-start.15
  58.2 1.5 collective-permute-start.17
  60.6 1.0 collective-permute-done.10.refs_8_
  64.1 20.3 %shard_map.220 = (bf16[768,3072]{1,0:T(8,128)(2,1)}, f32[8,768]{1,0:T(8,128)}, f32[256,768]{1,0:T(8,128)}, bf16[512,768]{1,0:T(8,128)(2,1)}, bf16[512,2304]{1,0:...) custom-call(s32[1]{0:T(128)} %bitcast.me_ref, ...), custom_call_target="tpu_custom_call" | custom-call | tf_op jit(solution)/shard_map/pallas_call | solution.py:466
  84.7 1.4 collective-permute-done.15.refs_2_
  86.3 1.5 collective-permute-start.19
  89.0 13.6 %collective-permute-done.19.refs_6_ = bf16[2,1312,128]{2,1,0:T(8,128)(2,1)S(1)} collective-permute-done((bf16[2,1312,128]{2,1,0:T(8,128)(2,1)}, bf16[2,1312,128]{2,1,0:T(8,128)(2,1)S(1)}, u32[]{:S(2)}, u32[]{:S(2)}) %collective-permute-start.19) | collective-permute-done | bytes 671776 | tf_op jit(solution)/shard_map/ppermute | solution.py:111
  102.6 1.1 collective-permute-done.20.refs_7_
  106.9 10.0 %shard_map.221 = (bf16[768,6912]{1,0:T(8,128)(2,1)S(1)}, f32[8,768]{1,0:T(8,128)S(1)}, bf16[16,768]{1,0:T(8,128)(2,1)S(1)}, f32[16,5376]{1,0:T(8,128)S(1)}) custom-call(s32[1]{0:T(128)} %bitcast.me_ref, s32[9]{0:T(128)S(1)} %pad_add_fusion.1.pick_ref, bf16[2,1312,128]{2,1,0:T(8,128)(2,1)} %copy-done.14, bf16[2,1312,128]{2,1,0:T(8,128)(2,1)} %copy-done.13, ...), custom_call_target="tpu_custom_call" | custom-call | tf_op jit(solution)/shard_map/pallas_call | solution.py:752
  117.1 5.1 %collective-permute-start.29 = (bf16[16,768]{1,0:T(8,128)(2,1)S(1)}, bf16[16,768]{1,0:T(8,128)(2,1)S(1)}, u32[]{:S(2)}, u32[]{:S(2)}) collective-permute-start(bf16[16,768]{1,0:T(8,128)(2,1)S(1)} %get-tuple-element.155), channel_id=1, source_target_pairs={{0,8},{1,9},{2,10},{3,11},{4,12},{5,13},{6,14},{7,15},{8,0},{9,1},... | collective-permute-start | bytes 73736 | tf_op jit(solution)/shard_map/ppermute | solution.py:111
  122.2 1.2 collective-permute-start.30
  123.4 1.5 collective-permute-start.31
  124.9 1.1 copy-done.8
  126.0 12.4 %shard_map.222 = (bf16[512,3072]{1,0:T(8,128)(2,1)S(1)}, bf16[512,3072]{1,0:T(8,128)(2,1)S(1)}, bf16[2,256,768]{2,1,0:T(8,128)(2,1)}, f32[512,768]{1,0:T(8,128)S...) custom-call(bf16[512,768]{1,0:T(8,128)(2,1)S(1)} %copy-done.2, f32[512,768]{1,0:T(8,128)S(1)} %copy-done.1, ...), custom_call_target="tpu_custom_call" | custom-call | tf_op jit(solution)/shard_map/pallas_call | solution.py:851
  139.1 2.1 collective-permute-start.34
  141.7 1.0 collective-permute-start.36
  142.7 9.4 %shard_map.223 = (bf16[512,3072]{1,0:T(8,128)(2,1)S(1)}, f32[512,768]{1,0:T(8,128)}, f32[8,768]{1,0:T(8,128)S(1)}) custom-call(bf16[512,768]{1,0:T(8,128)(2,1)S(1)} %get-tuple-element.148.down_ref.refs_4_, bf16[512,3072]{1,0:T(8,128)(2,1)S(1)} %get-tuple-element.149.slope_ref, f32[512,768]{1,0:T(8,128)S(1)} %get-tuple-element.150.d_res_ref, ...), custom_call_target="tpu_custom_call" | custom-call | tf_op jit(solution)/shard_map/pallas_call | solution.py:898
  152.3 1.7 collective-permute-done.39.sib_ref
  154.8 9.1 %shard_map.224 = (f32[1,1]{1,0:T(1,128)}, f32[16,768]{1,0:T(8,128)}, f32[32,3840]{1,0:T(8,128)S(1)}, bf16[32,1536]{1,0:T(8,128)(2,1)S(1)}, f32[8,768]{1,0:T(8,128)S(1)}) custom-call(s32[1]{0:T(128)} %bitcast.me_ref, bf16[4,4,16,768]{3,2,1,0:T(8,128)(2,1)} %copy-done.18, bf16[4,4,16,768]{3,2,1,0:T(8,128)(2,1)} %copy-done.40, bf16[768,6912]{1,0:T(8,128)(2,1)} %copy-done, ...), custom_call_target="tpu_custom_call" | custom-call | tf_op jit(solution)/shard_map/pallas_call | solution.py:998
  164.0 14.3 %shard_map.225 = (bf16[2,1312,128]{2,1,0:T(8,128)(2,1)}, bf16[2,1312,128]{2,1,0:T(8,128)(2,1)}, bf16[2,1312,128]{2,1,0:T(8,128)(2,1)}, bf16[2,1312,128]{2,1,0:T(...) custom-call(s32[1]{0:T(128)} %bitcast.me_ref, ...), custom_call_target="tpu_custom_call" | custom-call | tf_op jit(solution)/shard_map/pallas_call | solution.py:1100
  178.3 2.0 collective-permute-start.42
  180.9 1.5 collective-permute-start.45
  182.4 6.1 %shard_map.226 = (f32[512,768]{1,0:T(8,128)S(1)}, bf16[768,768]{1,0:T(8,128)(2,1)S(1)}, bf16[512,768]{1,0:T(8,128)(2,1)S(1)}, f32[8,768]{1,0:T(8,128)S(1)}) custom-call(s32[9]{0:T(128)S(1)} %pad_add_fusion.1.pick_ref, f32[512,768]{1,0:T(8,128)} %get-tuple-element.182.d_first, f32[16,768]{1,0:T(8,128)} %get-tuple-element.183.d_cls_in, ...), custom_call_target="tpu_custom_call" | custom-call | tf_op jit(solution)/shard_map/pallas_call | solution.py:541
  188.5 8.8 %shard_map.227 = (bf16[512,2304]{1,0:T(8,128)(2,1)S(1)}, f32[8,768]{1,0:T(8,128)}) custom-call(bf16[512,768]{1,0:T(8,128)(2,1)S(1)} %get-tuple-element.188.d_mixed, bf16[512,2304]{1,0:T(8,128)(2,1)S(1)} %copy-done.5, f32[4,6,256,128]{3,2,1,0:T(8,128)S(1)} %copy-done.4), custom_call_target="tpu_custom_call" | custom-call | tf_op jit(solution)/shard_map/pallas_call | solution.py:596
  197.3 1.1 collective-permute-done.43
  198.5 1.0 add_convert_fusion.2
  199.6 1.5 add_convert_fusion.3
  201.1 12.9 %shard_map.228 = (f32[256,768]{1,0:T(8,128)}, bf16[4,624,128]{2,1,0:T(8,128)(2,1)}, bf16[4,624,128]{2,1,0:T(8,128)(2,1)}, bf16[4,624,128]{2,1,0:T(8,128)(2,1)}, ...) custom-call(s32[1]{0:T(128)} %bitcast.me_ref, ...), custom_call_target="tpu_custom_call" | custom-call | tf_op jit(solution)/shard_map/pallas_call | solution.py:679
  214.0 1.8 collective-permute-done.44
  216.8 1.5 add_convert_fusion
  220.1 2.1 collective-permute-start.61
  222.3 1.2 collective-permute-start.62
  223.9 12.1 %collective-permute-done.51 = bf16[2,1312,128]{2,1,0:T(8,128)(2,1)S(1)} collective-permute-done((bf16[2,1312,128]{2,1,0:T(8,128)(2,1)S(1)}, bf16[2,1312,128]{2,1,0:T(8,128)(2,1)S(1)}, u32[]{:S(2)}, u32[]{:S(2)}) %collective-permute-start.51) | collective-permute-done | bytes 671776 | tf_op jit(solution)/shard_map/ppermute | solution.py:111
  238.6 1.0 collective-permute-start.55
  239.7 6.4 %collective-permute-done.53 = bf16[2,624,128]{2,1,0:T(8,128)(2,1)S(1)} collective-permute-done((bf16[2,624,128]{2,1,0:T(8,128)(2,1)S(1)}, bf16[2,624,128]{2,1,0:T(8,128)(2,1)S(1)}, u32[]{:S(2)}, u32[]{:S(2)}) %collective-permute-start.53) | collective-permute-done | bytes 319520 | tf_op jit(solution)/shard_map/ppermute | solution.py:111
  247.5 2.1 collective-permute-start.56
  249.6 3.0 collective-permute-done.60
  253.0 8.5 %collective-permute-done.54 = bf16[4,624,128]{2,1,0:T(8,128)(2,1)S(1)} collective-permute-done((bf16[4,624,128]{2,1,0:T(8,128)(2,1)S(1)}, bf16[4,624,128]{2,1,0:T(8,128)(2,1)S(1)}, u32[]{:S(2)}, u32[]{:S(2)}) %collective-permute-start.54) | collective-permute-done | bytes 639008 | tf_op jit(solution)/shard_map/ppermute | solution.py:111
  262.4 1.3 collective-permute-start.57
  263.7 2.0 collective-permute-start.58
  265.7 1.1 collective-permute-start.59
  268.6 7.2 %collective-permute-done.58 = bf16[624,128]{1,0:T(8,128)(2,1)S(1)} collective-permute-done((bf16[624,128]{1,0:T(8,128)(2,1)S(1)}, bf16[624,128]{1,0:T(8,128)(2,1)S(1)}, u32[]{:S(2)}, u32[]{:S(2)}) %collective-permute-start.58) | collective-permute-done | bytes 159776 | tf_op jit(solution)/shard_map/ppermute | solution.py:111
  279.8 2.7 collective-permute-start.64
  284.0 3.6 %collective-permute-start.65 = (f32[]{:T(128)}, f32[]{:T(128)}, u32[]{:S(2)}, u32[]{:S(2)}) collective-permute-start(f32[]{:T(128)} %add.206), channel_id=1, source_target_pairs={{0,4},{1,5},{2,6},{3,7},{4,0},{5,1},{6,2},{7,3},{8,12},{9,13},{10,... | collective-permute-start | bytes 20 | tf_op jit(solution)/shard_map/ppermute | solution.py:111
  288.4 3.9 %collective-permute-start.66 = (f32[]{:T(128)}, f32[]{:T(128)}, u32[]{:S(2)}, u32[]{:S(2)}) collective-permute-start(f32[]{:T(128)} %add.207), channel_id=1, source_target_pairs={{0,8},{1,9},{2,10},{3,11},{4,12},{5,13},{6,14},{7,15},{8,0},{9,1},... | collective-permute-start | bytes 20 | tf_op jit(solution)/shard_map/ppermute | solution.py:111
  293.1 4.1 %collective-permute-start.67 = (f32[]{:T(128)}, f32[]{:T(128)}, u32[]{:S(2)}, u32[]{:S(2)}) collective-permute-start(f32[]{:T(128)} %add.208), channel_id=1, source_target_pairs={{0,16},{1,17},{2,18},{3,19},{4,20},{5,21},{6,22},{7,23},{8,24},{9,... | collective-permute-start | bytes 20 | tf_op jit(solution)/shard_map/ppermute | solution.py:111
  298.4 3.1 %multiply_add_fusion.1 = (f32[166080]{0:T(1024)}, f32[166080]{0:T(1024)}, f32[166080]{0:T(1024)}, f32[166080]{0:T(1024)}) fusion(f32[166080]{0:T(1024)S(1)} %copy-done.35, f32[166080]{0:T(1024)S(1)} %copy-done.16, f32[166080]{0:T(1024)S(1)} %get-tuple-element.253, f32[]{:T(128)S(6)} %min_shard_map.3, f32[166080]{0:T(1024)S(1)} %copy-done.36, f32[166080]{0:T(1024)} %param.23), kind=kLoop, calls=%fused_computation.21 | loop fusion | flops 2989440 | bytes 5978884 | tf_op jit(solution)/shard_map/add | solution.py:75
  301.5 1.2 multiply_add_fusion.3
  (240 shorter events, 30.5 us)
Async XLA Ops:
  2.0 9.6 %collective-permute-start = (bf16[624,128]{1,0:T(8,128)(2,1)S(1)}, bf16[624,128]{1,0:T(8,128)(2,1)S(1)}, u32[]{:S(2)}, u32[]{:S(2)}) collective-permute-start(bf16[624,128]{1,0:T(8,128)(2,1)S(1)} %fusion.5), channel_id=1, source_target_pairs={{0,8},{1,9},{2,10},{3,11},{4,12},{5,13},{6,14},{7,15},{8,0},{9,1},... | collective-permute-start | bytes 479240 | tf_op jit(solution)/shard_map/ppermute | solution.py:111
  5.1 14.8 %collective-permute-start.1 = (bf16[624,128]{1,0:T(8,128)(2,1)S(1)}, bf16[624,128]{1,0:T(8,128)(2,1)S(1)}, u32[]{:S(2)}, u32[]{:S(2)}) collective-permute-start(bf16[624,128]{1,0:T(8,128)(2,1)S(1)} %fusion.5), channel_id=1, source_target_pairs={{0,16},{1,17},{2,18},{3,19},{4,20},{5,21},{6,22},{7,23},{8,24},{9,... | collective-permute-start | bytes 479240 | tf_op jit(solution)/shard_map/ppermute | solution.py:111
  7.7 12.2 %collective-permute-start.2 = (bf16[624,128]{1,0:T(8,128)(2,1)S(1)}, bf16[624,128]{1,0:T(8,128)(2,1)S(1)}, u32[]{:S(2)}, u32[]{:S(2)}) collective-permute-start(bf16[624,128]{1,0:T(8,128)(2,1)S(1)} %fusion.5), channel_id=1, source_target_pairs={{0,24},{1,25},{2,26},{3,27},{4,28},{5,29},{6,30},{7,31},{8,16},{9,... | collective-permute-start | bytes 479240 | tf_op jit(solution)/shard_map/ppermute | solution.py:111
  20.0 13.7 %collective-permute-start.4 = (bf16[4,624,128]{2,1,0:T(8,128)(2,1)S(1)}, bf16[4,624,128]{2,1,0:T(8,128)(2,1)S(1)}, u32[]{:S(2)}, u32[]{:S(2)}) collective-permute-start(bf16[4,624,128]{2,1,0:T(8,128)(2,1)S(1)} %pad_maximum_fusion.2.refs_0_), channel_id=1, source_target_pairs={{0,4},{1,5},{2,6},{3,7},{4,0},{5,1},{6,2},{7,3},{8,12},{9,13},{10,... | collective-permute-start | bytes 1916936 | tf_op jit(solution)/shard_map/ppermute | solution.py:111
  21.6 14.5 %collective-permute-start.3 = (bf16[4,624,128]{2,1,0:T(8,128)(2,1)S(1)}, bf16[4,624,128]{2,1,0:T(8,128)(2,1)S(1)}, u32[]{:S(2)}, u32[]{:S(2)}) collective-permute-start(bf16[4,624,128]{2,1,0:T(8,128)(2,1)S(1)} %pad_maximum_fusion.2.refs_0_), channel_id=1, source_target_pairs={{0,2},{1,3},{2,0},{3,1},{4,6},{5,7},{6,4},{7,5},{8,10},{9,11},{10,... | collective-permute-start | bytes 1916936 | tf_op jit(solution)/shard_map/ppermute | solution.py:111
  23.3 19.8 %collective-permute-start.12 = (bf16[1312,128]{1,0:T(8,128)(2,1)S(1)}, bf16[1312,128]{1,0:T(8,128)(2,1)S(1)}, u32[]{:S(2)}, u32[]{:S(2)}) collective-permute-start(bf16[1312,128]{1,0:T(8,128)(2,1)S(1)} %fusion), channel_id=1, source_target_pairs={{0,8},{1,9},{2,10},{3,11},{4,12},{5,13},{6,14},{7,15},{8,0},{9,1},... | collective-permute-start | bytes 1007624 | tf_op jit(solution)/shard_map/ppermute | solution.py:111
  26.0 26.1 %collective-permute-start.13 = (bf16[1312,128]{1,0:T(8,128)(2,1)S(1)}, bf16[1312,128]{1,0:T(8,128)(2,1)S(1)}, u32[]{:S(2)}, u32[]{:S(2)}) collective-permute-start(bf16[1312,128]{1,0:T(8,128)(2,1)S(1)} %fusion), channel_id=1, source_target_pairs={{0,16},{1,17},{2,18},{3,19},{4,20},{5,21},{6,22},{7,23},{8,24},{9,... | collective-permute-start | bytes 1007624 | tf_op jit(solution)/shard_map/ppermute | solution.py:111
  27.1 25.0 %collective-permute-start.14 = (bf16[1312,128]{1,0:T(8,128)(2,1)S(1)}, bf16[1312,128]{1,0:T(8,128)(2,1)S(1)}, u32[]{:S(2)}, u32[]{:S(2)}) collective-permute-start(bf16[1312,128]{1,0:T(8,128)(2,1)S(1)} %fusion), channel_id=1, source_target_pairs={{0,24},{1,25},{2,26},{3,27},{4,28},{5,29},{6,30},{7,31},{8,16},{9,... | collective-permute-start | bytes 1007624 | tf_op jit(solution)/shard_map/ppermute | solution.py:111
  34.5 18.9 %collective-permute-start.5 = (bf16[2,624,128]{2,1,0:T(8,128)(2,1)}, bf16[2,624,128]{2,1,0:T(8,128)(2,1)}, u32[]{:S(2)}, u32[]{:S(2)}) collective-permute-start(bf16[2,624,128]{2,1,0:T(8,128)(2,1)} %slice.74), channel_id=1, source_target_pairs={{0,2},{1,3},{2,0},{3,1},{4,6},{5,7},{6,4},{7,5},{8,10},{9,11},{10,... | collective-permute-start | bytes 958472 | tf_op jit(solution)/shard_map/ppermute | solution.py:111
  36.9 16.5 %collective-permute-start.6 = (bf16[2,624,128]{2,1,0:T(8,128)(2,1)}, bf16[2,624,128]{2,1,0:T(8,128)(2,1)}, u32[]{:S(2)}, u32[]{:S(2)}) collective-permute-start(bf16[2,624,128]{2,1,0:T(8,128)(2,1)} %slice.75), channel_id=1, source_target_pairs={{0,4},{1,5},{2,6},{3,7},{4,0},{5,1},{6,2},{7,3},{8,12},{9,13},{10,... | collective-permute-start | bytes 958472 | tf_op jit(solution)/shard_map/ppermute | solution.py:111
  43.2 13.4 %collective-permute-start.7 = (bf16[4,624,128]{2,1,0:T(8,128)(2,1)S(1)}, bf16[4,624,128]{2,1,0:T(8,128)(2,1)}, u32[]{:S(2)}, u32[]{:S(2)}) collective-permute-start(bf16[4,624,128]{2,1,0:T(8,128)(2,1)S(1)} %pad_maximum_fusion.2.refs_0_), channel_id=1, source_target_pairs={{0,1},{1,0},{2,3},{3,2},{4,5},{5,4},{6,7},{7,6},{8,9},{9,8},{10,11... | collective-permute-start | bytes 1916936 | tf_op jit(solution)/shard_map/ppermute | solution.py:111
  52.1 6.1 %collective-permute-start.8 = (bf16[4,624,128]{2,1,0:T(8,128)(2,1)S(1)}, bf16[4,624,128]{2,1,0:T(8,128)(2,1)}, u32[]{:S(2)}, u32[]{:S(2)}) collective-permute-start(bf16[4,624,128]{2,1,0:T(8,128)(2,1)S(1)} %collective-permute-done.3.refs_1_), channel_id=1, source_target_pairs={{0,1},{1,0},{2,3},{3,2},{4,5},{5,4},{6,7},{7,6},{8,9},{9,8},{10,11... | collective-permute-start | bytes 1916936 | tf_op jit(solution)/shard_map/ppermute | solution.py:111
  52.1 7.6 %collective-permute-start.9 = (bf16[4,624,128]{2,1,0:T(8,128)(2,1)S(1)}, bf16[4,624,128]{2,1,0:T(8,128)(2,1)}, u32[]{:S(2)}, u32[]{:S(2)}) collective-permute-start(bf16[4,624,128]{2,1,0:T(8,128)(2,1)S(1)} %collective-permute-done.4.refs_2_), channel_id=1, source_target_pairs={{0,1},{1,0},{2,3},{3,2},{4,5},{5,4},{6,7},{7,6},{8,9},{9,8},{10,11... | collective-permute-start | bytes 1916936 | tf_op jit(solution)/shard_map/ppermute | solution.py:111
  54.5 30.0 %collective-permute-start.16 = (bf16[2,1312,128]{2,1,0:T(8,128)(2,1)S(1)}, bf16[2,1312,128]{2,1,0:T(8,128)(2,1)}, u32[]{:S(2)}, u32[]{:S(2)}) collective-permute-start(bf16[2,1312,128]{2,1,0:T(8,128)(2,1)S(1)} %pad_maximum_fusion.1.refs_1_), channel_id=1, source_target_pairs={{0,2},{1,3},{2,0},{3,1},{4,6},{5,7},{6,4},{7,5},{8,10},{9,11},{10,... | collective-permute-start | bytes 2015240 | tf_op jit(solution)/shard_map/ppermute | solution.py:111
  55.1 29.6 %collective-permute-start.18 = (bf16[2,1312,128]{2,1,0:T(8,128)(2,1)S(1)}, bf16[2,1312,128]{2,1,0:T(8,128)(2,1)}, u32[]{:S(2)}, u32[]{:S(2)}) collective-permute-start(bf16[2,1312,128]{2,1,0:T(8,128)(2,1)S(1)} %pad_maximum_fusion.1.refs_1_), channel_id=1, source_target_pairs={{0,4},{1,5},{2,6},{3,7},{4,0},{5,1},{6,2},{7,3},{8,12},{9,13},{10,... | collective-permute-start | bytes 2015240 | tf_op jit(solution)/shard_map/ppermute | solution.py:111
  56.6 29.4 %collective-permute-start.15 = (bf16[2,1312,128]{2,1,0:T(8,128)(2,1)S(1)}, bf16[2,1312,128]{2,1,0:T(8,128)(2,1)}, u32[]{:S(2)}, u32[]{:S(2)}) collective-permute-start(bf16[2,1312,128]{2,1,0:T(8,128)(2,1)S(1)} %pad_maximum_fusion.refs_0_), channel_id=1, source_target_pairs={{0,2},{1,3},{2,0},{3,1},{4,6},{5,7},{6,4},{7,5},{8,10},{9,11},{10,... | collective-permute-start | bytes 2015240 | tf_op jit(solution)/shard_map/ppermute | solution.py:111
  58.2 28.1 %collective-permute-start.17 = (bf16[2,1312,128]{2,1,0:T(8,128)(2,1)S(1)}, bf16[2,1312,128]{2,1,0:T(8,128)(2,1)}, u32[]{:S(2)}, u32[]{:S(2)}) collective-permute-start(bf16[2,1312,128]{2,1,0:T(8,128)(2,1)S(1)} %pad_maximum_fusion.refs_0_), channel_id=1, source_target_pairs={{0,4},{1,5},{2,6},{3,7},{4,0},{5,1},{6,2},{7,3},{8,12},{9,13},{10,... | collective-permute-start | bytes 2015240 | tf_op jit(solution)/shard_map/ppermute | solution.py:111
  63.4 25.0 %collective-permute-start.22 = (bf16[2,1312,128]{2,1,0:T(8,128)(2,1)S(1)}, bf16[2,1312,128]{2,1,0:T(8,128)(2,1)S(1)}, u32[]{:S(2)}, u32[]{:S(2)}) collective-permute-start(bf16[2,1312,128]{2,1,0:T(8,128)(2,1)S(1)} %pad_maximum_fusion.1.refs_1_), channel_id=1, source_target_pairs={{0,1},{1,0},{2,3},{3,2},{4,5},{5,4},{6,7},{7,6},{8,9},{9,8},{10,11... | collective-permute-start | bytes 2015240 | tf_op jit(solution)/shard_map/ppermute | solution.py:111
  84.5 4.4 %collective-permute-start.21 = (bf16[2,1312,128]{2,1,0:T(8,128)(2,1)S(1)}, bf16[2,1312,128]{2,1,0:T(8,128)(2,1)S(1)}, u32[]{:S(2)}, u32[]{:S(2)}) collective-permute-start(bf16[2,1312,128]{2,1,0:T(8,128)(2,1)S(1)} %pad_maximum_fusion.refs_0_), channel_id=1, source_target_pairs={{0,1},{1,0},{2,3},{3,2},{4,5},{5,4},{6,7},{7,6},{8,9},{9,8},{10,11... | collective-permute-start | bytes 2015240 | tf_op jit(solution)/shard_map/ppermute | solution.py:111
  86.3 16.2 %collective-permute-start.19 = (bf16[2,1312,128]{2,1,0:T(8,128)(2,1)}, bf16[2,1312,128]{2,1,0:T(8,128)(2,1)S(1)}, u32[]{:S(2)}, u32[]{:S(2)}) collective-permute-start(bf16[2,1312,128]{2,1,0:T(8,128)(2,1)} %collective-permute-done.17.refs_4_), channel_id=1, source_target_pairs={{0,2},{1,3},{2,0},{3,1},{4,6},{5,7},{6,4},{7,5},{8,10},{9,11},{10,... | collective-permute-start | bytes 2015240 | tf_op jit(solution)/shard_map/ppermute | solution.py:111
  87.8 15.8 %collective-permute-start.20 = (bf16[2,1312,128]{2,1,0:T(8,128)(2,1)}, bf16[2,1312,128]{2,1,0:T(8,128)(2,1)S(1)}, u32[]{:S(2)}, u32[]{:S(2)}) collective-permute-start(bf16[2,1312,128]{2,1,0:T(8,128)(2,1)} %collective-permute-done.16.refs_3_), channel_id=1, source_target_pairs={{0,4},{1,5},{2,6},{3,7},{4,0},{5,1},{6,2},{7,3},{8,12},{9,13},{10,... | collective-permute-start | bytes 2015240 | tf_op jit(solution)/shard_map/ppermute | solution.py:111
  88.3 15.3 %collective-permute-start.23 = (bf16[2,1312,128]{2,1,0:T(8,128)(2,1)}, bf16[2,1312,128]{2,1,0:T(8,128)(2,1)S(1)}, u32[]{:S(2)}, u32[]{:S(2)}) collective-permute-start(bf16[2,1312,128]{2,1,0:T(8,128)(2,1)} %collective-permute-done.15.refs_2_), channel_id=1, source_target_pairs={{0,1},{1,0},{2,3},{3,2},{4,5},{5,4},{6,7},{7,6},{8,9},{9,8},{10,11... | collective-permute-start | bytes 2015240 | tf_op jit(solution)/shard_map/ppermute | solution.py:111
  88.4 15.8 %collective-permute-start.24 = (bf16[2,1312,128]{2,1,0:T(8,128)(2,1)}, bf16[2,1312,128]{2,1,0:T(8,128)(2,1)S(1)}, u32[]{:S(2)}, u32[]{:S(2)}) collective-permute-start(bf16[2,1312,128]{2,1,0:T(8,128)(2,1)} %collective-permute-done.16.refs_3_), channel_id=1, source_target_pairs={{0,1},{1,0},{2,3},{3,2},{4,5},{5,4},{6,7},{7,6},{8,9},{9,8},{10,11... | collective-permute-start | bytes 2015240 | tf_op jit(solution)/shard_map/ppermute | solution.py:111
  88.9 15.3 %collective-permute-start.25 = (bf16[2,1312,128]{2,1,0:T(8,128)(2,1)}, bf16[2,1312,128]{2,1,0:T(8,128)(2,1)S(1)}, u32[]{:S(2)}, u32[]{:S(2)}) collective-permute-start(bf16[2,1312,128]{2,1,0:T(8,128)(2,1)} %collective-permute-done.17.refs_4_), channel_id=1, source_target_pairs={{0,1},{1,0},{2,3},{3,2},{4,5},{5,4},{6,7},{7,6},{8,9},{9,8},{10,11... | collective-permute-start | bytes 2015240 | tf_op jit(solution)/shard_map/ppermute | solution.py:111
  102.6 2.3 collective-permute-start.26
  103.7 2.2 collective-permute-start.27
  103.7 3.2 %collective-permute-start.28 = (bf16[2,1312,128]{2,1,0:T(8,128)(2,1)S(1)}, bf16[2,1312,128]{2,1,0:T(8,128)(2,1)}, u32[]{:S(2)}, u32[]{:S(2)}) collective-permute-start(bf16[2,1312,128]{2,1,0:T(8,128)(2,1)S(1)} %collective-permute-done.20.refs_7_), channel_id=1, source_target_pairs={{0,1},{1,0},{2,3},{3,2},{4,5},{5,4},{6,7},{7,6},{8,9},{9,8},{10,11... | collective-permute-start | bytes 2015240 | tf_op jit(solution)/shard_map/ppermute | solution.py:111
  116.9 21.6 %collective-permute-start.32 = (f32[16,5376]{1,0:T(8,128)S(1)}, f32[16,5376]{1,0:T(8,128)S(1)}, u32[]{:S(2)}, u32[]{:S(2)}) collective-permute-start(f32[16,5376]{1,0:T(8,128)S(1)} %get-tuple-element.147.cls_own), channel_id=1, source_target_pairs={{0,1},{1,0},{2,3},{3,2},{4,5},{5,4},{6,7},{7,6},{8,9},{9,8},{10,11... | collective-permute-start | bytes 1032200 | tf_op jit(solution)/shard_map/ppermute | solution.py:111
  117.1 21.3 %collective-permute-start.29 = (bf16[16,768]{1,0:T(8,128)(2,1)S(1)}, bf16[16,768]{1,0:T(8,128)(2,1)S(1)}, u32[]{:S(2)}, u32[]{:S(2)}) collective-permute-start(bf16[16,768]{1,0:T(8,128)(2,1)S(1)} %get-tuple-element.155), channel_id=1, source_target_pairs={{0,8},{1,9},{2,10},{3,11},{4,12},{5,13},{6,14},{7,15},{8,0},{9,1},... | collective-permute-start | bytes 73736 | tf_op jit(solution)/shard_map/ppermute | solution.py:111
  122.2 16.3 %collective-permute-start.30 = (bf16[16,768]{1,0:T(8,128)(2,1)S(1)}, bf16[16,768]{1,0:T(8,128)(2,1)S(1)}, u32[]{:S(2)}, u32[]{:S(2)}) collective-permute-start(bf16[16,768]{1,0:T(8,128)(2,1)S(1)} %get-tuple-element.155), channel_id=1, source_target_pairs={{0,16},{1,17},{2,18},{3,19},{4,20},{5,21},{6,22},{7,23},{8,24},{9,... | collective-permute-start | bytes 73736 | tf_op jit(solution)/shard_map/ppermute | solution.py:111
  123.4 15.1 %collective-permute-start.31 = (bf16[16,768]{1,0:T(8,128)(2,1)S(1)}, bf16[16,768]{1,0:T(8,128)(2,1)S(1)}, u32[]{:S(2)}, u32[]{:S(2)}) collective-permute-start(bf16[16,768]{1,0:T(8,128)(2,1)S(1)} %get-tuple-element.155), channel_id=1, source_target_pairs={{0,24},{1,25},{2,26},{3,27},{4,28},{5,29},{6,30},{7,31},{8,16},{9,... | collective-permute-start | bytes 73736 | tf_op jit(solution)/shard_map/ppermute | solution.py:111
  138.5 13.7 %collective-permute-start.37 = (bf16[512,3072]{1,0:T(8,128)(2,1)S(1)}, bf16[512,3072]{1,0:T(8,128)(2,1)S(1)}, u32[]{:S(2)}, u32[]{:S(2)}) collective-permute-start(bf16[512,3072]{1,0:T(8,128)(2,1)S(1)} %get-tuple-element.159.refs_6_), channel_id=1, source_target_pairs={{0,1},{1,0},{2,3},{3,2},{4,5},{5,4},{6,7},{7,6},{8,9},{9,8},{10,11... | collective-permute-start | bytes 9437192 | tf_op jit(solution)/shard_map/ppermute | solution.py:111
  138.6 13.6 %collective-permute-start.38 = (bf16[512,768]{1,0:T(8,128)(2,1)S(1)}, bf16[512,768]{1,0:T(8,128)(2,1)S(1)}, u32[]{:S(2)}, u32[]{:S(2)}) collective-permute-start(bf16[512,768]{1,0:T(8,128)(2,1)S(1)} %get-tuple-element.148.down_ref.refs_4_), channel_id=1, source_target_pairs={{0,1},{1,0},{2,3},{3,2},{4,5},{5,4},{6,7},{7,6},{8,9},{9,8},{10,11... | collective-permute-start | bytes 2359304 | tf_op jit(solution)/shard_map/ppermute | solution.py:111
  139.1 13.0 %collective-permute-start.34 = (bf16[4,16,768]{2,1,0:T(8,128)(2,1)S(1)}, bf16[4,16,768]{2,1,0:T(8,128)(2,1)S(1)}, u32[]{:S(2)}, u32[]{:S(2)}) collective-permute-start(bf16[4,16,768]{2,1,0:T(8,128)(2,1)S(1)} %pad_maximum_fusion.6), channel_id=1, source_target_pairs={{0,2},{1,3},{2,0},{3,1},{4,6},{5,7},{6,4},{7,5},{8,10},{9,11},{10,... | collective-permute-start | bytes 294920 | tf_op jit(solution)/shard_map/ppermute | solution.py:111
  141.2 11.0 %collective-permute-start.35 = (bf16[4,16,768]{2,1,0:T(8,128)(2,1)S(1)}, bf16[4,16,768]{2,1,0:T(8,128)(2,1)S(1)}, u32[]{:S(2)}, u32[]{:S(2)}) collective-permute-start(bf16[4,16,768]{2,1,0:T(8,128)(2,1)S(1)} %pad_maximum_fusion.6), channel_id=1, source_target_pairs={{0,4},{1,5},{2,6},{3,7},{4,0},{5,1},{6,2},{7,3},{8,12},{9,13},{10,... | collective-permute-start | bytes 294920 | tf_op jit(solution)/shard_map/ppermute | solution.py:111
  141.7 10.5 %collective-permute-start.36 = (bf16[4,16,768]{2,1,0:T(8,128)(2,1)S(1)}, bf16[4,16,768]{2,1,0:T(8,128)(2,1)S(1)}, u32[]{:S(2)}, u32[]{:S(2)}) collective-permute-start(bf16[4,16,768]{2,1,0:T(8,128)(2,1)S(1)} %pad_maximum_fusion.6), channel_id=1, source_target_pairs={{0,6},{1,7},{2,4},{3,5},{4,2},{5,3},{6,0},{7,1},{8,14},{9,15},{10,... | collective-permute-start | bytes 294920 | tf_op jit(solution)/shard_map/ppermute | solution.py:111
  154.0 9.9 %collective-permute-start.40 = (bf16[512,3072]{1,0:T(8,128)(2,1)S(1)}, bf16[512,3072]{1,0:T(8,128)(2,1)S(1)}, u32[]{:S(2)}, u32[]{:S(2)}) collective-permute-start(bf16[512,3072]{1,0:T(8,128)(2,1)S(1)} %get-tuple-element.165.refs_2_), channel_id=1, source_target_pairs={{0,1},{1,0},{2,3},{3,2},{4,5},{5,4},{6,7},{7,6},{8,9},{9,8},{10,11... | collective-permute-start | bytes 9437192 | tf_op jit(solution)/shard_map/ppermute | solution.py:111
  154.2 9.8 %collective-permute-start.33 = (bf16[512,768]{1,0:T(8,128)(2,1)S(1)}, bf16[512,768]{1,0:T(8,128)(2,1)S(1)}, u32[]{:S(2)}, u32[]{:S(2)}) collective-permute-start(bf16[512,768]{1,0:T(8,128)(2,1)S(1)} %copy-done.2), channel_id=1, source_target_pairs={{0,1},{1,0},{2,3},{3,2},{4,5},{5,4},{6,7},{7,6},{8,9},{9,8},{10,11... | collective-permute-start | bytes 2359304 | tf_op jit(solution)/shard_map/ppermute | solution.py:111
  154.6 9.4 %collective-permute-start.41 = (f32[8,768]{1,0:T(8,128)S(1)}, f32[8,768]{1,0:T(8,128)S(1)}, u32[]{:S(2)}, u32[]{:S(2)}) collective-permute-start(f32[8,768]{1,0:T(8,128)S(1)} %get-tuple-element.173.refs_11_), channel_id=1, source_target_pairs={{0,1},{1,0},{2,3},{3,2},{4,5},{5,4},{6,7},{7,6},{8,9},{9,8},{10,11... | collective-permute-start | bytes 73736 | tf_op jit(solution)/shard_map/ppermute | solution.py:111
  178.3 19.0 %collective-permute-start.42 = (bf16[2,1312,128]{2,1,0:T(8,128)(2,1)}, bf16[2,1312,128]{2,1,0:T(8,128)(2,1)S(1)}, u32[]{:S(2)}, u32[]{:S(2)}) collective-permute-start(bf16[2,1312,128]{2,1,0:T(8,128)(2,1)} %get-tuple-element.192), channel_id=1, source_target_pairs={{0,2},{1,3},{2,0},{3,1},{4,6},{5,7},{6,4},{7,5},{8,10},{9,11},{10,... | collective-permute-start | bytes 2015240 | tf_op jit(solution)/shard_map/ppermute | solution.py:111
  180.3 18.1 %collective-permute-start.43 = (bf16[2,1312,128]{2,1,0:T(8,128)(2,1)}, bf16[2,1312,128]{2,1,0:T(8,128)(2,1)S(1)}, u32[]{:S(2)}, u32[]{:S(2)}) collective-permute-start(bf16[2,1312,128]{2,1,0:T(8,128)(2,1)} %get-tuple-element.193), channel_id=1, source_target_pairs={{0,4},{1,5},{2,6},{3,7},{4,0},{5,1},{6,2},{7,3},{8,12},{9,13},{10,... | collective-permute-start | bytes 2015240 | tf_op jit(solution)/shard_map/ppermute | solution.py:111
  180.9 33.2 %collective-permute-start.45 = (bf16[2,1312,128]{2,1,0:T(8,128)(2,1)}, bf16[2,1312,128]{2,1,0:T(8,128)(2,1)S(1)}, u32[]{:S(2)}, u32[]{:S(2)}) collective-permute-start(bf16[2,1312,128]{2,1,0:T(8,128)(2,1)} %get-tuple-element.220), channel_id=1, source_target_pairs={{0,4},{1,5},{2,6},{3,7},{4,0},{5,1},{6,2},{7,3},{8,12},{9,13},{10,... | collective-permute-start | bytes 2015240 | tf_op jit(solution)/shard_map/ppermute | solution.py:111
  199.5 16.3 %collective-permute-start.44 = (bf16[2,1312,128]{2,1,0:T(8,128)(2,1)}, bf16[2,1312,128]{2,1,0:T(8,128)(2,1)}, u32[]{:S(2)}, u32[]{:S(2)}) collective-permute-start(bf16[2,1312,128]{2,1,0:T(8,128)(2,1)} %add_convert_fusion.2), channel_id=1, source_target_pairs={{0,2},{1,3},{2,0},{3,1},{4,6},{5,7},{6,4},{7,5},{8,10},{9,11},{10,... | collective-permute-start | bytes 2015240 | tf_op jit(solution)/shard_map/ppermute | solution.py:111
  215.8 2.6 collective-permute-start.50
  215.8 3.6 %collective-permute-start.49 = (bf16[2,624,128]{2,1,0:T(8,128)(2,1)}, bf16[2,624,128]{2,1,0:T(8,128)(2,1)S(1)}, u32[]{:S(2)}, u32[]{:S(2)}) collective-permute-start(bf16[2,624,128]{2,1,0:T(8,128)(2,1)} %get-tuple-element.228), channel_id=1, source_target_pairs={{0,1},{1,0},{2,3},{3,2},{4,5},{5,4},{6,7},{7,6},{8,9},{9,8},{10,11... | collective-permute-start | bytes 958472 | tf_op jit(solution)/shard_map/ppermute | solution.py:111
  216.3 3.7 %collective-permute-start.48 = (bf16[4,624,128]{2,1,0:T(8,128)(2,1)}, bf16[4,624,128]{2,1,0:T(8,128)(2,1)S(1)}, u32[]{:S(2)}, u32[]{:S(2)}) collective-permute-start(bf16[4,624,128]{2,1,0:T(8,128)(2,1)} %get-tuple-element.226), channel_id=1, source_target_pairs={{0,1},{1,0},{2,3},{3,2},{4,5},{5,4},{6,7},{7,6},{8,9},{9,8},{10,11... | collective-permute-start | bytes 1916936 | tf_op jit(solution)/shard_map/ppermute | solution.py:111
  216.3 6.0 %collective-permute-start.47 = (bf16[4,624,128]{2,1,0:T(8,128)(2,1)}, bf16[4,624,128]{2,1,0:T(8,128)(2,1)S(1)}, u32[]{:S(2)}, u32[]{:S(2)}) collective-permute-start(bf16[4,624,128]{2,1,0:T(8,128)(2,1)} %get-tuple-element.224), channel_id=1, source_target_pairs={{0,1},{1,0},{2,3},{3,2},{4,5},{5,4},{6,7},{7,6},{8,9},{9,8},{10,11... | collective-permute-start | bytes 1916936 | tf_op jit(solution)/shard_map/ppermute | solution.py:111
  216.8 6.9 %collective-permute-start.46 = (bf16[4,624,128]{2,1,0:T(8,128)(2,1)}, bf16[4,624,128]{2,1,0:T(8,128)(2,1)S(1)}, u32[]{:S(2)}, u32[]{:S(2)}) collective-permute-start(bf16[4,624,128]{2,1,0:T(8,128)(2,1)} %get-tuple-element.222), channel_id=1, source_target_pairs={{0,1},{1,0},{2,3},{3,2},{4,5},{5,4},{6,7},{7,6},{8,9},{9,8},{10,11... | collective-permute-start | bytes 1916936 | tf_op jit(solution)/shard_map/ppermute | solution.py:111
  218.4 17.6 %collective-permute-start.51 = (bf16[2,1312,128]{2,1,0:T(8,128)(2,1)S(1)}, bf16[2,1312,128]{2,1,0:T(8,128)(2,1)S(1)}, u32[]{:S(2)}, u32[]{:S(2)}) collective-permute-start(bf16[2,1312,128]{2,1,0:T(8,128)(2,1)S(1)} %copy-done.51), channel_id=1, source_target_pairs={{0,2},{1,3},{2,0},{3,1},{4,6},{5,7},{6,4},{7,5},{8,10},{9,11},{10,... | collective-permute-start | bytes 2015240 | tf_op jit(solution)/shard_map/ppermute | solution.py:111
  219.4 17.6 %collective-permute-start.52 = (bf16[2,1312,128]{2,1,0:T(8,128)(2,1)S(1)}, bf16[2,1312,128]{2,1,0:T(8,128)(2,1)S(1)}, u32[]{:S(2)}, u32[]{:S(2)}) collective-permute-start(bf16[2,1312,128]{2,1,0:T(8,128)(2,1)S(1)} %add_convert_fusion.3), channel_id=1, source_target_pairs={{0,4},{1,5},{2,6},{3,7},{4,0},{5,1},{6,2},{7,3},{8,12},{9,13},{10,... | collective-permute-start | bytes 2015240 | tf_op jit(solution)/shard_map/ppermute | solution.py:111
  220.1 29.5 %collective-permute-start.61 = (bf16[1312,128]{1,0:T(8,128)(2,1)S(1)}, bf16[1312,128]{1,0:T(8,128)(2,1)S(1)}, u32[]{:S(2)}, u32[]{:S(2)}) collective-permute-start(bf16[1312,128]{1,0:T(8,128)(2,1)S(1)} %get-tuple-element.260), channel_id=1, source_target_pairs={{0,16},{1,17},{2,18},{3,19},{4,20},{5,21},{6,22},{7,23},{8,24},{9,... | collective-permute-start | bytes 1007624 | tf_op jit(solution)/shard_map/ppermute | solution.py:111
  222.3 27.3 %collective-permute-start.62 = (bf16[1312,128]{1,0:T(8,128)(2,1)S(1)}, bf16[1312,128]{1,0:T(8,128)(2,1)S(1)}, u32[]{:S(2)}, u32[]{:S(2)}) collective-permute-start(bf16[1312,128]{1,0:T(8,128)(2,1)S(1)} %get-tuple-element.261), channel_id=1, source_target_pairs={{0,24},{1,25},{2,26},{3,27},{4,28},{5,29},{6,30},{7,31},{8,16},{9,... | collective-permute-start | bytes 1007624 | tf_op jit(solution)/shard_map/ppermute | solution.py:111
  236.9 9.2 %collective-permute-start.53 = (bf16[2,624,128]{2,1,0:T(8,128)(2,1)S(1)}, bf16[2,624,128]{2,1,0:T(8,128)(2,1)S(1)}, u32[]{:S(2)}, u32[]{:S(2)}) collective-permute-start(bf16[2,624,128]{2,1,0:T(8,128)(2,1)S(1)} %add_convert_fusion.10), channel_id=1, source_target_pairs={{0,4},{1,5},{2,6},{3,7},{4,0},{5,1},{6,2},{7,3},{8,12},{9,13},{10,... | collective-permute-start | bytes 958472 | tf_op jit(solution)/shard_map/ppermute | solution.py:111
  237.8 14.9 %collective-permute-start.60 = (bf16[1312,128]{1,0:T(8,128)(2,1)S(1)}, bf16[1312,128]{1,0:T(8,128)(2,1)S(1)}, u32[]{:S(2)}, u32[]{:S(2)}) collective-permute-start(bf16[1312,128]{1,0:T(8,128)(2,1)S(1)} %get-tuple-element.258), channel_id=1, source_target_pairs={{0,8},{1,9},{2,10},{3,11},{4,12},{5,13},{6,14},{7,15},{8,0},{9,1},... | collective-permute-start | bytes 1007624 | tf_op jit(solution)/shard_map/ppermute | solution.py:111
  238.6 8.7 %collective-permute-start.55 = (bf16[2,624,128]{2,1,0:T(8,128)(2,1)S(1)}, bf16[2,624,128]{2,1,0:T(8,128)(2,1)S(1)}, u32[]{:S(2)}, u32[]{:S(2)}) collective-permute-start(bf16[2,624,128]{2,1,0:T(8,128)(2,1)S(1)} %add_convert_fusion.11), channel_id=1, source_target_pairs={{0,2},{1,3},{2,0},{3,1},{4,6},{5,7},{6,4},{7,5},{8,10},{9,11},{10,... | collective-permute-start | bytes 958472 | tf_op jit(solution)/shard_map/ppermute | solution.py:111
  246.3 15.2 %collective-permute-start.54 = (bf16[4,624,128]{2,1,0:T(8,128)(2,1)S(1)}, bf16[4,624,128]{2,1,0:T(8,128)(2,1)S(1)}, u32[]{:S(2)}, u32[]{:S(2)}) collective-permute-start(bf16[4,624,128]{2,1,0:T(8,128)(2,1)S(1)} %pad_maximum_fusion.3), channel_id=1, source_target_pairs={{0,2},{1,3},{2,0},{3,1},{4,6},{5,7},{6,4},{7,5},{8,10},{9,11},{10,... | collective-permute-start | bytes 1916936 | tf_op jit(solution)/shard_map/ppermute | solution.py:111
  247.5 14.6 %collective-permute-start.56 = (bf16[4,624,128]{2,1,0:T(8,128)(2,1)S(1)}, bf16[4,624,128]{2,1,0:T(8,128)(2,1)S(1)}, u32[]{:S(2)}, u32[]{:S(2)}) collective-permute-start(bf16[4,624,128]{2,1,0:T(8,128)(2,1)S(1)} %pad_maximum_fusion.4), channel_id=1, source_target_pairs={{0,4},{1,5},{2,6},{3,7},{4,0},{5,1},{6,2},{7,3},{8,12},{9,13},{10,... | collective-permute-start | bytes 1916936 | tf_op jit(solution)/shard_map/ppermute | solution.py:111
  262.4 6.2 %collective-permute-start.57 = (bf16[624,128]{1,0:T(8,128)(2,1)S(1)}, bf16[624,128]{1,0:T(8,128)(2,1)S(1)}, u32[]{:S(2)}, u32[]{:S(2)}) collective-permute-start(bf16[624,128]{1,0:T(8,128)(2,1)S(1)} %get-tuple-element.262), channel_id=1, source_target_pairs={{0,8},{1,9},{2,10},{3,11},{4,12},{5,13},{6,14},{7,15},{8,0},{9,1},... | collective-permute-start | bytes 479240 | tf_op jit(solution)/shard_map/ppermute | solution.py:111
  263.7 12.1 %collective-permute-start.58 = (bf16[624,128]{1,0:T(8,128)(2,1)S(1)}, bf16[624,128]{1,0:T(8,128)(2,1)S(1)}, u32[]{:S(2)}, u32[]{:S(2)}) collective-permute-start(bf16[624,128]{1,0:T(8,128)(2,1)S(1)} %get-tuple-element.264), channel_id=1, source_target_pairs={{0,16},{1,17},{2,18},{3,19},{4,20},{5,21},{6,22},{7,23},{8,24},{9,... | collective-permute-start | bytes 479240 | tf_op jit(solution)/shard_map/ppermute | solution.py:111
  265.7 10.1 %collective-permute-start.59 = (bf16[624,128]{1,0:T(8,128)(2,1)S(1)}, bf16[624,128]{1,0:T(8,128)(2,1)S(1)}, u32[]{:S(2)}, u32[]{:S(2)}) collective-permute-start(bf16[624,128]{1,0:T(8,128)(2,1)S(1)} %get-tuple-element.263), channel_id=1, source_target_pairs={{0,24},{1,25},{2,26},{3,27},{4,28},{5,29},{6,30},{7,31},{8,16},{9,... | collective-permute-start | bytes 479240 | tf_op jit(solution)/shard_map/ppermute | solution.py:111
  279.8 3.6 %collective-permute-start.64 = (f32[]{:T(128)}, f32[]{:T(128)}, u32[]{:S(2)}, u32[]{:S(2)}) collective-permute-start(f32[]{:T(128)} %add.205), channel_id=1, source_target_pairs={{0,2},{1,3},{2,0},{3,1},{4,6},{5,7},{6,4},{7,5},{8,10},{9,11},{10,... | collective-permute-start | bytes 20 | tf_op jit(solution)/shard_map/ppermute | solution.py:111
  284.0 3.8 %collective-permute-start.65 = (f32[]{:T(128)}, f32[]{:T(128)}, u32[]{:S(2)}, u32[]{:S(2)}) collective-permute-start(f32[]{:T(128)} %add.206), channel_id=1, source_target_pairs={{0,4},{1,5},{2,6},{3,7},{4,0},{5,1},{6,2},{7,3},{8,12},{9,13},{10,... | collective-permute-start | bytes 20 | tf_op jit(solution)/shard_map/ppermute | solution.py:111
  288.4 4.1 %collective-permute-start.66 = (f32[]{:T(128)}, f32[]{:T(128)}, u32[]{:S(2)}, u32[]{:S(2)}) collective-permute-start(f32[]{:T(128)} %add.207), channel_id=1, source_target_pairs={{0,8},{1,9},{2,10},{3,11},{4,12},{5,13},{6,14},{7,15},{8,0},{9,1},... | collective-permute-start | bytes 20 | tf_op jit(solution)/shard_map/ppermute | solution.py:111
  293.1 4.5 %collective-permute-start.67 = (f32[]{:T(128)}, f32[]{:T(128)}, u32[]{:S(2)}, u32[]{:S(2)}) collective-permute-start(f32[]{:T(128)} %add.208), channel_id=1, source_target_pairs={{0,16},{1,17},{2,18},{3,19},{4,20},{5,21},{6,22},{7,23},{8,24},{9,... | collective-permute-start | bytes 20 | tf_op jit(solution)/shard_map/ppermute | solution.py:111
  (59 other events, 723.7 us)
